TPU v7x, 32 devices: a whole 2x2x4 slice. The times are simulated.
32 devices in a mesh: dp: 8 (over z, y), blk: 4 (over x, core).
Axes of the slice: x: 2, y: 2, z: 4, core: 2. Of those that a mesh axis runs over, the one named last changes fastest.
Arguments:
- tokens: bfloat16 [4, 8192, 512], P(None, ('dp', 'blk')), may hold values from -6 to 6
- lengths: int32 [4, 8, 2], P(None, 'dp'), may hold values from 196 to 784, as said below
- attn_gain: bfloat16 [512], P(('dp', 'blk')), may hold values from 0.5 to 1.5
- attn_shift: bfloat16 [512], P(('dp', 'blk')), may hold values from -1.75 to 1.75
- w_qkv: bfloat16 [512, 1536], P(('dp', 'blk')), may hold values from -0.25 to 0.25
- qv_bias: bfloat16 [1024], P(('dp', 'blk')), may hold values from -1.75 to 1.75
- w_proj: bfloat16 [512, 512], P(('dp', 'blk')), may hold values from -1 to 1
- proj_bias: bfloat16 [512], P(('dp', 'blk')), may hold values from -1.75 to 1.75
- mlp_gain: bfloat16 [512], P(('dp', 'blk')), may hold values from 0.5 to 1.5
- mlp_shift: bfloat16 [512], P(('dp', 'blk')), may hold values from -1.75 to 1.75
- w_expand: bfloat16 [512, 2048], P(('dp', 'blk')), may hold values from -0.25 to 0.25
- expand_bias: bfloat16 [2048], P(('dp', 'blk')), may hold values from -3 to 3
- w_reduce: bfloat16 [2048, 512], P(('dp', 'blk')), may hold values from -0.125 to 0.125
- reduce_bias: bfloat16 [512], P(('dp', 'blk')), may hold values from -1.75 to 1.75
- cotangent: bfloat16 [4, 8192, 512], P(None, ('dp', 'blk')), may hold values from -6 to 6
Outputs:
- result: bfloat16 [4, 8192, 512], P(None, ('dp', 'blk'))
- grad_tokens: bfloat16 [4, 8192, 512], P(None, ('dp', 'blk'))
- grad_attn_gain: float32 [512], P(('dp', 'blk'))
- grad_attn_shift: float32 [512], P(('dp', 'blk'))
- grad_w_qkv: float32 [512, 1536], P(('dp', 'blk'))
- grad_qv_bias: float32 [1024], P(('dp', 'blk'))
- grad_w_proj: float32 [512, 512], P(('dp', 'blk'))
- grad_proj_bias: float32 [512], P(('dp', 'blk'))
- grad_mlp_gain: float32 [512], P(('dp', 'blk'))
- grad_mlp_shift: float32 [512], P(('dp', 'blk'))
- grad_w_expand: float32 [512, 2048], P(('dp', 'blk'))
- grad_expand_bias: float32 [2048], P(('dp', 'blk'))
- grad_w_reduce: float32 [2048, 512], P(('dp', 'blk'))
- grad_reduce_bias: float32 [512], P(('dp', 'blk'))
Inputs may be any that keep to these rules, and one draw needn't show every extreme that they name: `lengths`: each group holds one image of 784 tokens and one of 196 tokens, in an order drawn from the seed.
All inputs are finite; a program needn't handle non-finite values.
Results may differ from a plain program's by a relative error of at most 0.01.
Values may be sent and summed in bfloat16 or wider, within the bound.
A program may use at most 128 MiB of HBM per device.

v0:
```python
import math

import jax
import jax.numpy as jnp
from jax import lax
from jax.sharding import PartitionSpec as P

HEAD_DIM = 32


epsilon = 1e-06
masked_score = -1e30


def segment_ids(positions, bounds):
    first_end = bounds[0]
    second_end = bounds[0] + bounds[1]
    return (positions >= first_end).astype(jnp.int32) + (positions >= second_end).astype(jnp.int32)


def normalize(values, norm_gain, norm_shift):
    centered = values - jnp.mean(values, axis=-1, keepdims=True)
    inverse = lax.rsqrt(jnp.mean(centered * centered, axis=-1, keepdims=True) + epsilon)
    normed = centered * inverse
    return (normed * norm_gain + norm_shift, normed, inverse)


def normalize_back(gradient, normed, inverse, norm_gain):
    scaled = gradient * norm_gain
    inner_term = (
        scaled
        - jnp.mean(scaled, axis=-1, keepdims=True)
        - normed * jnp.mean(scaled * normed, axis=-1, keepdims=True)
    )
    return (inverse * inner_term, jnp.sum(gradient * normed, axis=0), jnp.sum(gradient, axis=0))


def matmul(left_hand, right_hand):
    return jnp.dot(left_hand, right_hand, preferred_element_type=jnp.float32)


def row_product(left_hand, right_hand):
    return lax.dot_general(
        left_hand, right_hand, (((0,), (0,)), ((), ())), preferred_element_type=jnp.float32
    )


def times_transposed(left_hand, right_hand):
    return lax.dot_general(
        left_hand, right_hand, (((1,), (1,)), ((), ())), preferred_element_type=jnp.float32
    )


def exact_gelu(values):
    return jax.nn.gelu(values, approximate=False)


def masked_scores(query_heads, key_heads, same_segment, scaling):
    raw_scores = (
        jnp.einsum("qhd,khd->hqk", query_heads, key_heads, preferred_element_type=jnp.float32)
        * scaling
    )
    return jnp.where(same_segment[None], raw_scores, masked_score)


def exps_of(scores, row_top, same_segment):
    return jnp.where(same_segment[None], jnp.exp(scores - row_top), 0.0)


def attend_forward(query_heads, key_heads, value_heads, same_segment, scaling):
    scores = masked_scores(query_heads, key_heads, same_segment, scaling)
    row_top = jnp.max(scores, axis=-1, keepdims=True)
    exps = exps_of(scores, row_top, same_segment)
    row_total = jnp.sum(exps, axis=-1, keepdims=True)
    probs_low = (exps / row_total).astype(jnp.bfloat16)
    attended = jnp.einsum(
        "hqk,khd->qhd", probs_low, value_heads, preferred_element_type=jnp.float32
    )
    return (attended.astype(jnp.bfloat16), row_top, row_total)


def attend_backward(
    query_heads, key_heads, value_heads, same_segment, scaling, row_top, row_total, d_attended
):
    scores = masked_scores(query_heads, key_heads, same_segment, scaling)
    probs = exps_of(scores, row_top, same_segment) / row_total
    probs_low = probs.astype(jnp.bfloat16)
    d_probs = jnp.einsum(
        "qhd,khd->hqk", d_attended, value_heads, preferred_element_type=jnp.float32
    )
    grad_values = jnp.einsum(
        "hqk,qhd->khd", probs_low, d_attended, preferred_element_type=jnp.float32
    )
    row_inner = jnp.sum(probs * d_probs, axis=-1, keepdims=True)
    d_scores = (probs * (d_probs - row_inner)).astype(jnp.bfloat16)
    grad_queries = (
        jnp.einsum("hqk,khd->qhd", d_scores, key_heads, preferred_element_type=jnp.float32)
        * scaling
    )
    grad_keys = (
        jnp.einsum("hqk,qhd->khd", d_scores, query_heads, preferred_element_type=jnp.float32)
        * scaling
    )
    return (grad_queries, grad_keys, grad_values)


def micro_step(weights, token_rows, bounds, cotan_rows, block_index):
    (
        attn_gain,
        attn_shift,
        w_qkv,
        qv_bias,
        w_proj,
        proj_bias,
        mlp_gain,
        mlp_shift,
        w_expand,
        expand_bias,
        w_reduce,
        reduce_bias,
    ) = weights
    height = token_rows.shape[0]
    width = token_rows.shape[1]
    heads = width // HEAD_DIM
    scaling = 1.0 / math.sqrt(HEAD_DIM)
    inputs = token_rows.astype(jnp.float32)
    first_gain = attn_gain.astype(jnp.float32)
    second_gain = mlp_gain.astype(jnp.float32)
    normed_a, plain_a, inverse_a = normalize(inputs, first_gain, attn_shift.astype(jnp.float32))
    lowered_a = normed_a.astype(jnp.bfloat16)
    shift_qkv = jnp.concatenate(
        [qv_bias[:width], jnp.zeros((width,), qv_bias.dtype), qv_bias[width:]]
    ).astype(jnp.float32)
    projected = (matmul(lowered_a, w_qkv) + shift_qkv).astype(jnp.bfloat16)
    query_local = projected[:, :width].reshape(height, heads, HEAD_DIM)
    all_keys, all_values = (
        lax.all_gather(projected[:, width : 2 * width], "blk", axis=0, tiled=True),
        lax.all_gather(projected[:, 2 * width :], "blk", axis=0, tiled=True),
    )
    group_rows = all_keys.shape[0]
    key_heads = all_keys.reshape(group_rows, heads, HEAD_DIM)
    value_heads = all_values.reshape(group_rows, heads, HEAD_DIM)
    query_segment = segment_ids(block_index * height + jnp.arange(height, dtype=jnp.int32), bounds)
    key_segment = segment_ids(jnp.arange(group_rows, dtype=jnp.int32), bounds)
    same_segment = query_segment[:, None] == key_segment[None, :]
    local_attended, row_top, row_total = attend_forward(
        query_local, key_heads, value_heads, same_segment, scaling
    )
    attended = local_attended.reshape(height, width)
    middle = inputs + (matmul(attended, w_proj) + proj_bias.astype(jnp.float32))
    normed_b, plain_b, inverse_b = normalize(middle, second_gain, mlp_shift.astype(jnp.float32))
    lowered_b = normed_b.astype(jnp.bfloat16)
    expanded = matmul(lowered_b, w_expand) + expand_bias.astype(jnp.float32)
    activated = exact_gelu(expanded).astype(jnp.bfloat16)
    result = (middle + (matmul(activated, w_reduce) + reduce_bias.astype(jnp.float32))).astype(
        jnp.bfloat16
    )
    cotan_float = cotan_rows.astype(jnp.float32)
    grad_reduce = row_product(activated, cotan_rows)
    grad_reduce_bias = jnp.sum(cotan_float, axis=0)
    d_activated = times_transposed(cotan_rows, w_reduce)
    gelu_value, gelu_pull = jax.vjp(exact_gelu, expanded)
    d_expanded = gelu_pull(d_activated)[0].astype(jnp.bfloat16)
    grad_expand = row_product(lowered_b, d_expanded)
    grad_expand_bias = jnp.sum(d_expanded.astype(jnp.float32), axis=0)
    d_normed_b = times_transposed(d_expanded, w_expand)
    d_middle_b, grad_mlp_gain, grad_mlp_shift = normalize_back(
        d_normed_b, plain_b, inverse_b, second_gain
    )
    d_middle = cotan_float + d_middle_b
    d_branch = d_middle.astype(jnp.bfloat16)
    grad_proj = row_product(attended, d_branch)
    grad_proj_bias = jnp.sum(d_branch.astype(jnp.float32), axis=0)
    d_attended = (
        times_transposed(d_branch, w_proj).astype(jnp.bfloat16).reshape(height, heads, HEAD_DIM)
    )
    grad_queries, grad_keys, grad_values = attend_backward(
        query_local, key_heads, value_heads, same_segment, scaling, row_top, row_total, d_attended
    )
    key_sum, value_sum = (
        lax.psum_scatter(
            grad_keys.reshape(group_rows, width).astype(jnp.bfloat16),
            "blk",
            scatter_dimension=0,
            tiled=True,
        ).astype(jnp.float32),
        lax.psum_scatter(
            grad_values.reshape(group_rows, width).astype(jnp.bfloat16),
            "blk",
            scatter_dimension=0,
            tiled=True,
        ).astype(jnp.float32),
    )
    d_projected = jnp.concatenate(
        [grad_queries.reshape(height, width), key_sum, value_sum], axis=1
    ).astype(jnp.bfloat16)
    grad_qkv = row_product(lowered_a, d_projected)
    d_projected_float = d_projected.astype(jnp.float32)
    grad_qv_bias = jnp.concatenate(
        [
            jnp.sum(d_projected_float[:, :width], axis=0),
            jnp.sum(d_projected_float[:, 2 * width :], axis=0),
        ]
    )
    d_normed_a = times_transposed(d_projected, w_qkv)
    d_inputs_a, grad_attn_gain, grad_attn_shift = normalize_back(
        d_normed_a, plain_a, inverse_a, first_gain
    )
    grad_rows = (d_middle + d_inputs_a).astype(jnp.bfloat16)
    terms = (
        grad_attn_gain,
        grad_attn_shift,
        grad_qkv,
        grad_qv_bias,
        grad_proj,
        grad_proj_bias,
        grad_mlp_gain,
        grad_mlp_shift,
        grad_expand,
        grad_expand_bias,
        grad_reduce,
        grad_reduce_bias,
    )
    return (result, grad_rows, terms)


def body(
    tokens,
    lengths,
    attn_gain,
    attn_shift,
    w_qkv,
    qv_bias,
    w_proj,
    proj_bias,
    mlp_gain,
    mlp_shift,
    w_expand,
    expand_bias,
    w_reduce,
    reduce_bias,
    cotangent,
):
    shards = (
        attn_gain,
        attn_shift,
        w_qkv,
        qv_bias,
        w_proj,
        proj_bias,
        mlp_gain,
        mlp_shift,
        w_expand,
        expand_bias,
        w_reduce,
        reduce_bias,
    )
    micro_count = tokens.shape[0]
    block_index = lax.axis_index("blk")
    devices_all = lax.axis_size(("dp", "blk"))
    starting = tuple(
        (
            jnp.zeros((sharded.shape[0] * devices_all,) + sharded.shape[1:], jnp.float32)
            for sharded in shards
        )
    )

    def one_batch(number, carried):
        results, grads_rows, summed = carried
        weights = (
            lax.all_gather(attn_gain, ("dp", "blk"), axis=0, tiled=True),
            lax.all_gather(attn_shift, ("dp", "blk"), axis=0, tiled=True),
            lax.all_gather(w_qkv, ("dp", "blk"), axis=0, tiled=True),
            lax.all_gather(qv_bias, ("dp", "blk"), axis=0, tiled=True),
            lax.all_gather(w_proj, ("dp", "blk"), axis=0, tiled=True),
            lax.all_gather(proj_bias, ("dp", "blk"), axis=0, tiled=True),
            lax.all_gather(mlp_gain, ("dp", "blk"), axis=0, tiled=True),
            lax.all_gather(mlp_shift, ("dp", "blk"), axis=0, tiled=True),
            lax.all_gather(w_expand, ("dp", "blk"), axis=0, tiled=True),
            lax.all_gather(expand_bias, ("dp", "blk"), axis=0, tiled=True),
            lax.all_gather(w_reduce, ("dp", "blk"), axis=0, tiled=True),
            lax.all_gather(reduce_bias, ("dp", "blk"), axis=0, tiled=True),
        )
        token_rows = lax.dynamic_index_in_dim(tokens, number, 0, keepdims=False)
        cotan_rows = lax.dynamic_index_in_dim(cotangent, number, 0, keepdims=False)
        bounds = lax.dynamic_index_in_dim(lengths, number, 0, keepdims=False)[0]
        result, grad_rows, terms = micro_step(weights, token_rows, bounds, cotan_rows, block_index)
        summed = tuple((earlier + addend for earlier, addend in zip(summed, terms)))
        results = lax.dynamic_update_index_in_dim(results, result, number, 0)
        grads_rows = lax.dynamic_update_index_in_dim(grads_rows, grad_rows, number, 0)
        return (results, grads_rows, summed)

    results, grads_rows, summed = lax.fori_loop(
        0, micro_count, one_batch, (jnp.zeros_like(tokens), jnp.zeros_like(tokens), starting)
    )
    summed = (
        lax.psum_scatter(summed[0], ("dp", "blk"), scatter_dimension=0, tiled=True),
        lax.psum_scatter(summed[1], ("dp", "blk"), scatter_dimension=0, tiled=True),
        lax.psum_scatter(summed[2], ("dp", "blk"), scatter_dimension=0, tiled=True),
        lax.psum_scatter(summed[3], ("dp", "blk"), scatter_dimension=0, tiled=True),
        lax.psum_scatter(summed[4], ("dp", "blk"), scatter_dimension=0, tiled=True),
        lax.psum_scatter(summed[5], ("dp", "blk"), scatter_dimension=0, tiled=True),
        lax.psum_scatter(summed[6], ("dp", "blk"), scatter_dimension=0, tiled=True),
        lax.psum_scatter(summed[7], ("dp", "blk"), scatter_dimension=0, tiled=True),
        lax.psum_scatter(summed[8], ("dp", "blk"), scatter_dimension=0, tiled=True),
        lax.psum_scatter(summed[9], ("dp", "blk"), scatter_dimension=0, tiled=True),
        lax.psum_scatter(summed[10], ("dp", "blk"), scatter_dimension=0, tiled=True),
        lax.psum_scatter(summed[11], ("dp", "blk"), scatter_dimension=0, tiled=True),
    )
    return (
        results,
        grads_rows,
        summed[0],
        summed[1],
        summed[2],
        summed[3],
        summed[4],
        summed[5],
        summed[6],
        summed[7],
        summed[8],
        summed[9],
        summed[10],
        summed[11],
    )


def solution(mesh):
    in_specs = (
        P(None, ("dp", "blk"), None),
        P(None, "dp", None),
        P(("dp", "blk")),
        P(("dp", "blk")),
        P(("dp", "blk"), None),
        P(("dp", "blk")),
        P(("dp", "blk"), None),
        P(("dp", "blk")),
        P(("dp", "blk")),
        P(("dp", "blk")),
        P(("dp", "blk"), None),
        P(("dp", "blk")),
        P(("dp", "blk"), None),
        P(("dp", "blk")),
        P(None, ("dp", "blk"), None),
    )
    out_specs = (
        P(None, ("dp", "blk"), None),
        P(None, ("dp", "blk"), None),
        P(("dp", "blk")),
        P(("dp", "blk")),
        P(("dp", "blk"), None),
        P(("dp", "blk")),
        P(("dp", "blk"), None),
        P(("dp", "blk")),
        P(("dp", "blk")),
        P(("dp", "blk")),
        P(("dp", "blk"), None),
        P(("dp", "blk")),
        P(("dp", "blk"), None),
        P(("dp", "blk")),
    )
    return jax.shard_map(body, mesh=mesh, in_specs=in_specs, out_specs=out_specs, check_vma=False)
```

profile of v0, /device:TPU:0, one launch (start us, length us, event | category | flops | bytes accessed | tf_op | source)
XLA Modules:
  0.0 1743.4 jit_solution(16280011651111448855)
XLA Ops:
  8.1 1202.9 %while.42 = (s32[]{:T(128)}, bf16[4,256,512]{2,1,0:T(8,128)(2,1)}, bf16[4,256,512]{2,1,0:T(8,128)(2,1)}, f32[512]{0:T(512)S(1)}, f32[512]{0:T(512)S(1)}, /*index...) while((s32[]{:T(128)}, bf16[4,256,512]{2,1,0:T(8,128)(2,1)}, ...), condition=%wide.region_23.24_spmd.clone, body=%wide.region_0.23_spmd.clone.sunk | while | flops 6580108288 | bytes 430149920 | solution.py:293
  15.7 42.3 %all-reduce.27 = (bf16[1024]{0:T(1024)(128)(2,1)S(1)}, bf16[512]{0:T(512)(128)(2,1)S(1)}, bf16[512]{0:T(512)(128)(2,1)S(1)}, bf16[512]{0:T(512)(128)(2,1)S(1)}, ...) all-reduce(bf16[1024]{0:T(1024)(128)(2,1)S(1)} %dynamic-update-slic, ...), channel_id=1, replica_groups=mesh['dp'=8,'blk'=4] {'dp','blk'}, use_global_device_ids=true, to_apply=%add.2 | all-reduce | flops 6144 | bytes 24576 | tf_op jit(solution)/shard_map/while
  60.4 9.6 all-gather.6.cloned.1.call-done
  78.2 41.0 %all_gather.141 = bf16[512,512]{1,0:T(8,128)(2,1)S(1)} all-gather(bf16[16,512]{1,0:T(8,128)(2,1)S(1)} %copy-done.15), channel_id=1, replica_groups=mesh['dp'=8,'blk'=4] {'dp','blk'}, dimensions={0}, use_global_device_ids=true | all-gather | bytes 540672 | tf_op jit(solution)/shard_map/while/body/eval_jaxpr/all_gather | solution.py:275
  121.1 10.7 fusion.181
  133.3 8.9 fusion.182
  143.8 25.0 %all-gather.12.cloned.1.call-done = bf16[512,2048]{1,0:T(8,128)(2,1)} async-done(((bf16[16,2048]{1,0:T(8,128)(2,1)}), bf16[512,2048]{1,0:T(8,128)(2,1)}) %all-gather.12.cloned.1.call-update) | async-done | bytes 2097168 | tf_op jit(solution)/shard_map/while/body/eval_jaxpr/all_gather | solution.py:279
  177.2 50.0 %all-gather.14.cloned.1.call-done = bf16[2048,512]{1,0:T(8,128)(2,1)} async-done(((bf16[64,512]{1,0:T(8,128)(2,1)}), bf16[2048,512]{1,0:T(8,128)(2,1)}) %all-gather.14.cloned.1.call-update) | async-done | bytes 2097168 | tf_op jit(solution)/shard_map/while/body/eval_jaxpr/all_gather | solution.py:281
  242.2 10.5 multiply_reduce_fusion.11
  252.8 12.2 multiply_convert_fusion.7
  282.9 21.2 %reduce-scatter.17.cloned.1.call-done = bf16[256,512]{0,1:T(8,128)(2,1)} async-done(((bf16[1024,512]{0,1:T(8,128)(2,1)}), bf16[256,512]{0,1:T(8,128)(2,1)}) %reduce-scatter.17.cloned.1.call-update) | async-done | bytes 262160 | tf_op jit(solution)/shard_map/while/body/eval_jaxpr/reduce_scatter | solution.py:181
  318.5 39.7 %all-reduce.27 = (bf16[1024]{0:T(1024)(128)(2,1)S(1)}, bf16[512]{0:T(512)(128)(2,1)S(1)}, bf16[512]{0:T(512)(128)(2,1)S(1)}, bf16[512]{0:T(512)(128)(2,1)S(1)}, ...) all-reduce(bf16[1024]{0:T(1024)(128)(2,1)S(1)} %dynamic-update-slic, ...), channel_id=1, replica_groups=mesh['dp'=8,'blk'=4] {'dp','blk'}, use_global_device_ids=true, to_apply=%add.2 | all-reduce | flops 6144 | bytes 24576 | tf_op jit(solution)/shard_map/while
  360.5 9.5 all-gather.6.cloned.1.call-done
  378.3 41.2 %all_gather.141 = bf16[512,512]{1,0:T(8,128)(2,1)S(1)} all-gather(bf16[16,512]{1,0:T(8,128)(2,1)S(1)} %copy-done.15), channel_id=1, replica_groups=mesh['dp'=8,'blk'=4] {'dp','blk'}, dimensions={0}, use_global_device_ids=true | all-gather | bytes 540672 | tf_op jit(solution)/shard_map/while/body/eval_jaxpr/all_gather | solution.py:275
  421.3 10.7 fusion.181
  433.6 8.9 fusion.182
  444.1 24.9 %all-gather.12.cloned.1.call-done = bf16[512,2048]{1,0:T(8,128)(2,1)} async-done(((bf16[16,2048]{1,0:T(8,128)(2,1)}), bf16[512,2048]{1,0:T(8,128)(2,1)}) %all-gather.12.cloned.1.call-update) | async-done | bytes 2097168 | tf_op jit(solution)/shard_map/while/body/eval_jaxpr/all_gather | solution.py:279
  477.4 50.0 %all-gather.14.cloned.1.call-done = bf16[2048,512]{1,0:T(8,128)(2,1)} async-done(((bf16[64,512]{1,0:T(8,128)(2,1)}), bf16[2048,512]{1,0:T(8,128)(2,1)}) %all-gather.14.cloned.1.call-update) | async-done | bytes 2097168 | tf_op jit(solution)/shard_map/while/body/eval_jaxpr/all_gather | solution.py:281
  542.4 10.5 multiply_reduce_fusion.11
  553.0 12.2 multiply_convert_fusion.7
  584.5 19.7 %reduce-scatter.17.cloned.1.call-done = bf16[256,512]{0,1:T(8,128)(2,1)} async-done(((bf16[1024,512]{0,1:T(8,128)(2,1)}), bf16[256,512]{0,1:T(8,128)(2,1)}) %reduce-scatter.17.cloned.1.call-update) | async-done | bytes 262160 | tf_op jit(solution)/shard_map/while/body/eval_jaxpr/reduce_scatter | solution.py:181
  618.4 39.6 %all-reduce.27 = (bf16[1024]{0:T(1024)(128)(2,1)S(1)}, bf16[512]{0:T(512)(128)(2,1)S(1)}, bf16[512]{0:T(512)(128)(2,1)S(1)}, bf16[512]{0:T(512)(128)(2,1)S(1)}, ...) all-reduce(bf16[1024]{0:T(1024)(128)(2,1)S(1)} %dynamic-update-slic, ...), channel_id=1, replica_groups=mesh['dp'=8,'blk'=4] {'dp','blk'}, use_global_device_ids=true, to_apply=%add.2 | all-reduce | flops 6144 | bytes 24576 | tf_op jit(solution)/shard_map/while
  660.3 9.4 all-gather.6.cloned.1.call-done
  678.0 41.2 %all_gather.141 = bf16[512,512]{1,0:T(8,128)(2,1)S(1)} all-gather(bf16[16,512]{1,0:T(8,128)(2,1)S(1)} %copy-done.15), channel_id=1, replica_groups=mesh['dp'=8,'blk'=4] {'dp','blk'}, dimensions={0}, use_global_device_ids=true | all-gather | bytes 540672 | tf_op jit(solution)/shard_map/while/body/eval_jaxpr/all_gather | solution.py:275
  721.1 10.7 fusion.181
  733.4 8.9 fusion.182
  743.9 24.8 %all-gather.12.cloned.1.call-done = bf16[512,2048]{1,0:T(8,128)(2,1)} async-done(((bf16[16,2048]{1,0:T(8,128)(2,1)}), bf16[512,2048]{1,0:T(8,128)(2,1)}) %all-gather.12.cloned.1.call-update) | async-done | bytes 2097168 | tf_op jit(solution)/shard_map/while/body/eval_jaxpr/all_gather | solution.py:279
  768.6 8.3 multiply_convert_fusion.6
  777.0 50.2 %all-gather.14.cloned.1.call-done = bf16[2048,512]{1,0:T(8,128)(2,1)} async-done(((bf16[64,512]{1,0:T(8,128)(2,1)}), bf16[2048,512]{1,0:T(8,128)(2,1)}) %all-gather.14.cloned.1.call-update) | async-done | bytes 2097168 | tf_op jit(solution)/shard_map/while/body/eval_jaxpr/all_gather | solution.py:281
  842.2 10.5 multiply_reduce_fusion.11
  852.8 12.2 multiply_convert_fusion.7
  884.2 19.8 %reduce-scatter.17.cloned.1.call-done = bf16[256,512]{0,1:T(8,128)(2,1)} async-done(((bf16[1024,512]{0,1:T(8,128)(2,1)}), bf16[256,512]{0,1:T(8,128)(2,1)}) %reduce-scatter.17.cloned.1.call-update) | async-done | bytes 262160 | tf_op jit(solution)/shard_map/while/body/eval_jaxpr/reduce_scatter | solution.py:181
  918.4 39.7 %all-reduce.27 = (bf16[1024]{0:T(1024)(128)(2,1)S(1)}, bf16[512]{0:T(512)(128)(2,1)S(1)}, bf16[512]{0:T(512)(128)(2,1)S(1)}, bf16[512]{0:T(512)(128)(2,1)S(1)}, ...) all-reduce(bf16[1024]{0:T(1024)(128)(2,1)S(1)} %dynamic-update-slic, ...), channel_id=1, replica_groups=mesh['dp'=8,'blk'=4] {'dp','blk'}, use_global_device_ids=true, to_apply=%add.2 | all-reduce | flops 6144 | bytes 24576 | tf_op jit(solution)/shard_map/while
  960.4 9.5 all-gather.6.cloned.1.call-done
  978.2 41.2 %all_gather.141 = bf16[512,512]{1,0:T(8,128)(2,1)S(1)} all-gather(bf16[16,512]{1,0:T(8,128)(2,1)S(1)} %copy-done.15), channel_id=1, replica_groups=mesh['dp'=8,'blk'=4] {'dp','blk'}, dimensions={0}, use_global_device_ids=true | all-gather | bytes 540672 | tf_op jit(solution)/shard_map/while/body/eval_jaxpr/all_gather | solution.py:275
  1021.3 10.7 fusion.181
  1033.5 8.9 fusion.182
  1044.0 24.9 %all-gather.12.cloned.1.call-done = bf16[512,2048]{1,0:T(8,128)(2,1)} async-done(((bf16[16,2048]{1,0:T(8,128)(2,1)}), bf16[512,2048]{1,0:T(8,128)(2,1)}) %all-gather.12.cloned.1.call-update) | async-done | bytes 2097168 | tf_op jit(solution)/shard_map/while/body/eval_jaxpr/all_gather | solution.py:279
  1069.0 8.4 multiply_convert_fusion.6
  1077.3 50.0 %all-gather.14.cloned.1.call-done = bf16[2048,512]{1,0:T(8,128)(2,1)} async-done(((bf16[64,512]{1,0:T(8,128)(2,1)}), bf16[2048,512]{1,0:T(8,128)(2,1)}) %all-gather.14.cloned.1.call-update) | async-done | bytes 2097168 | tf_op jit(solution)/shard_map/while/body/eval_jaxpr/all_gather | solution.py:281
  1142.4 10.5 multiply_reduce_fusion.11
  1153.0 12.2 multiply_convert_fusion.7
  1184.4 19.8 %reduce-scatter.17.cloned.1.call-done = bf16[256,512]{0,1:T(8,128)(2,1)} async-done(((bf16[1024,512]{0,1:T(8,128)(2,1)}), bf16[256,512]{0,1:T(8,128)(2,1)}) %reduce-scatter.17.cloned.1.call-update) | async-done | bytes 262160 | tf_op jit(solution)/shard_map/while/body/eval_jaxpr/reduce_scatter | solution.py:181
  1213.5 39.8 %all-reduce.25 = (f32[512]{0:T(512)S(1)}, f32[512]{0:T(512)S(1)}, f32[1024]{0:T(1024)S(1)}, f32[512]{0:T(512)S(1)}, f32[512]{0:T(512)S(1)}, /*index=5*/f32[512]{0:T(512)S(1)}, f32[2048]{0:T(1024)S(1)}, f32[512]{0:T(512)S(1)}) all-reduce(f32[512]{0:T(512)S(1)} %get-tuple-element.703, ...), channel_id=4, replica_groups=mesh['dp'=8,'blk'=4] {'dp','blk'}, use_global_device_ids=true, to_apply=%region_24.25.clone | all-reduce | flops 6144 | bytes 49152
  1257.9 91.3 %reduce-scatter.9.cloned.1.call-done = f32[16,512]{1,0:T(8,128)} async-done(((f32[512,512]{1,0:T(8,128)}), f32[16,512]{1,0:T(8,128)}) %reduce-scatter.9.cloned.1.call-update) | async-done | bytes 32784 | tf_op jit(solution)/shard_map/reduce_scatter | solution.py:301
  1349.2 104.2 %reduce-scatter.7.cloned.1.call-done = f32[16,1536]{1,0:T(8,128)} async-done(((f32[512,1536]{1,0:T(8,128)}), f32[16,1536]{1,0:T(8,128)}) %reduce-scatter.7.cloned.1.call-update) | async-done | bytes 98320 | tf_op jit(solution)/shard_map/reduce_scatter | solution.py:299
  1453.4 142.8 %reduce-scatter.11.cloned.1.call-done = f32[16,2048]{1,0:T(8,128)} async-done(((f32[512,2048]{1,0:T(8,128)}), f32[16,2048]{1,0:T(8,128)}) %reduce-scatter.11.cloned.1.call-update) | async-done | bytes 131088 | tf_op jit(solution)/shard_map/reduce_scatter | solution.py:305
  1596.2 139.6 %reduce-scatter.13.cloned.1.call-done = f32[64,512]{1,0:T(8,128)} async-done(((f32[2048,512]{1,0:T(8,128)}), f32[64,512]{1,0:T(8,128)}) %reduce-scatter.13.cloned.1.call-update) | async-done | bytes 131088 | tf_op jit(solution)/shard_map/reduce_scatter | solution.py:307
  (548 shorter events, 272.3 us)
Async XLA Ops:
  8.2 61.8 %all-gather.6.cloned.1.call-start = ((), (), s32[]{:S(2)}) async-start(), calls=%async_computation.10 | async-start | bytes 1622016 | tf_op jit(solution)/shard_map/while/body/eval_jaxpr/all_gather | solution.py:273
  8.9 110.7 %all-gather.10.cloned.1.call-start = ((), (), s32[]{:S(2)}) async-start(), calls=%async_computation.12 | async-start | bytes 1310720 | tf_op jit(solution)/shard_map/while/body/eval_jaxpr/all_gather | solution.py:137
  60.3 14.6 copy-start.16
  60.3 17.9 %copy-start.15 = (bf16[16,512]{1,0:T(8,128)(2,1)S(1)}, bf16[16,512]{1,0:T(8,128)(2,1)}, u32[]{:S(2)}) copy-start(bf16[16,512]{1,0:T(8,128)(2,1)} %get-tuple-element.1311) | copy-start | bytes 49156 | tf_op jit(solution)/shard_map/while
  73.0 58.8 %all-gather.8.cloned.1.call-start = ((), (), s32[]{:S(2)}) async-start(), calls=%async_computation.11 | async-start | bytes 1310720 | tf_op jit(solution)/shard_map/while/body/eval_jaxpr/all_gather | solution.py:138
  73.7 95.1 %all-gather.12.cloned.1.call-start = ((), (), s32[]{:S(2)}) async-start(), calls=%async_computation.13 | async-start | bytes 2162688 | tf_op jit(solution)/shard_map/while/body/eval_jaxpr/all_gather | solution.py:279
  74.3 152.9 %all-gather.14.cloned.1.call-start = ((), (), s32[]{:S(2)}) async-start(), calls=%async_computation.14 | async-start | bytes 2162688 | tf_op jit(solution)/shard_map/while/body/eval_jaxpr/all_gather | solution.py:281
  74.9 208.0 %reduce-scatter.15.cloned.1.call-start = ((), (), s32[]{:S(2)}) async-start(), calls=%async_computation.15 | async-start | bytes 1310720 | tf_op jit(solution)/shard_map/while/body/eval_jaxpr/reduce_scatter | solution.py:187
  252.8 51.4 %reduce-scatter.17.cloned.1.call-start = ((), (), s32[]{:S(2)}) async-start(), calls=%async_computation.16 | async-start | bytes 1310720 | tf_op jit(solution)/shard_map/while/body/eval_jaxpr/reduce_scatter | solution.py:181
  282.9 22.7 %copy-start.5 = (bf16[4,256,512]{2,1,0:T(8,128)(2,1)S(1)}, bf16[4,256,512]{2,1,0:T(8,128)(2,1)}, u32[]{:S(2)}) copy-start(bf16[4,256,512]{2,1,0:T(8,128)(2,1)} %get-tuple-element.1304) | copy-start | bytes 3145732 | tf_op jit(solution)/shard_map/while
  282.9 22.7 %copy-start.9 = (bf16[256,512]{0,1:T(8,128)(2,1)S(1)}, bf16[256,512]{0,1:T(8,128)(2,1)}, u32[]{:S(2)}) copy-start(bf16[256,512]{0,1:T(8,128)(2,1)} %reduce-scatter.15.cloned.1.call-done) | copy-start | bytes 786436 | tf_op jit(solution)/shard_map/while
  310.9 59.1 %all-gather.6.cloned.1.call-start = ((), (), s32[]{:S(2)}) async-start(), calls=%async_computation.10 | async-start | bytes 1622016 | tf_op jit(solution)/shard_map/while/body/eval_jaxpr/all_gather | solution.py:273
  311.6 108.2 %all-gather.10.cloned.1.call-start = ((), (), s32[]{:S(2)}) async-start(), calls=%async_computation.12 | async-start | bytes 1310720 | tf_op jit(solution)/shard_map/while/body/eval_jaxpr/all_gather | solution.py:137
  360.5 14.5 copy-start.16
  360.5 17.8 %copy-start.15 = (bf16[16,512]{1,0:T(8,128)(2,1)S(1)}, bf16[16,512]{1,0:T(8,128)(2,1)}, u32[]{:S(2)}) copy-start(bf16[16,512]{1,0:T(8,128)(2,1)} %get-tuple-element.1311) | copy-start | bytes 49156 | tf_op jit(solution)/shard_map/while
  373.0 59.1 %all-gather.8.cloned.1.call-start = ((), (), s32[]{:S(2)}) async-start(), calls=%async_computation.11 | async-start | bytes 1310720 | tf_op jit(solution)/shard_map/while/body/eval_jaxpr/all_gather | solution.py:138
  373.6 95.4 %all-gather.12.cloned.1.call-start = ((), (), s32[]{:S(2)}) async-start(), calls=%async_computation.13 | async-start | bytes 2162688 | tf_op jit(solution)/shard_map/while/body/eval_jaxpr/all_gather | solution.py:279
  374.3 153.1 %all-gather.14.cloned.1.call-start = ((), (), s32[]{:S(2)}) async-start(), calls=%async_computation.14 | async-start | bytes 2162688 | tf_op jit(solution)/shard_map/while/body/eval_jaxpr/all_gather | solution.py:281
  374.9 209.6 %reduce-scatter.15.cloned.1.call-start = ((), (), s32[]{:S(2)}) async-start(), calls=%async_computation.15 | async-start | bytes 1310720 | tf_op jit(solution)/shard_map/while/body/eval_jaxpr/reduce_scatter | solution.py:187
  552.9 51.2 %reduce-scatter.17.cloned.1.call-start = ((), (), s32[]{:S(2)}) async-start(), calls=%async_computation.16 | async-start | bytes 1310720 | tf_op jit(solution)/shard_map/while/body/eval_jaxpr/reduce_scatter | solution.py:181
  584.4 21.2 %copy-start.5 = (bf16[4,256,512]{2,1,0:T(8,128)(2,1)S(1)}, bf16[4,256,512]{2,1,0:T(8,128)(2,1)}, u32[]{:S(2)}) copy-start(bf16[4,256,512]{2,1,0:T(8,128)(2,1)} %get-tuple-element.1304) | copy-start | bytes 3145732 | tf_op jit(solution)/shard_map/while
  584.5 21.2 %copy-start.9 = (bf16[256,512]{0,1:T(8,128)(2,1)S(1)}, bf16[256,512]{0,1:T(8,128)(2,1)}, u32[]{:S(2)}) copy-start(bf16[256,512]{0,1:T(8,128)(2,1)} %reduce-scatter.15.cloned.1.call-done) | copy-start | bytes 786436 | tf_op jit(solution)/shard_map/while
  610.9 58.8 %all-gather.6.cloned.1.call-start = ((), (), s32[]{:S(2)}) async-start(), calls=%async_computation.10 | async-start | bytes 1622016 | tf_op jit(solution)/shard_map/while/body/eval_jaxpr/all_gather | solution.py:273
  611.5 108.1 %all-gather.10.cloned.1.call-start = ((), (), s32[]{:S(2)}) async-start(), calls=%async_computation.12 | async-start | bytes 1310720 | tf_op jit(solution)/shard_map/while/body/eval_jaxpr/all_gather | solution.py:137
  660.3 14.4 copy-start.16
  660.3 17.7 %copy-start.15 = (bf16[16,512]{1,0:T(8,128)(2,1)S(1)}, bf16[16,512]{1,0:T(8,128)(2,1)}, u32[]{:S(2)}) copy-start(bf16[16,512]{1,0:T(8,128)(2,1)} %get-tuple-element.1311) | copy-start | bytes 49156 | tf_op jit(solution)/shard_map/while
  672.8 59.1 %all-gather.8.cloned.1.call-start = ((), (), s32[]{:S(2)}) async-start(), calls=%async_computation.11 | async-start | bytes 1310720 | tf_op jit(solution)/shard_map/while/body/eval_jaxpr/all_gather | solution.py:138
  673.3 95.3 %all-gather.12.cloned.1.call-start = ((), (), s32[]{:S(2)}) async-start(), calls=%async_computation.13 | async-start | bytes 2162688 | tf_op jit(solution)/shard_map/while/body/eval_jaxpr/all_gather | solution.py:279
  673.9 153.2 %all-gather.14.cloned.1.call-start = ((), (), s32[]{:S(2)}) async-start(), calls=%async_computation.14 | async-start | bytes 2162688 | tf_op jit(solution)/shard_map/while/body/eval_jaxpr/all_gather | solution.py:281
  674.7 209.6 %reduce-scatter.15.cloned.1.call-start = ((), (), s32[]{:S(2)}) async-start(), calls=%async_computation.15 | async-start | bytes 1310720 | tf_op jit(solution)/shard_map/while/body/eval_jaxpr/reduce_scatter | solution.py:187
  852.7 51.3 %reduce-scatter.17.cloned.1.call-start = ((), (), s32[]{:S(2)}) async-start(), calls=%async_computation.16 | async-start | bytes 1310720 | tf_op jit(solution)/shard_map/while/body/eval_jaxpr/reduce_scatter | solution.py:181
  884.2 21.4 %copy-start.5 = (bf16[4,256,512]{2,1,0:T(8,128)(2,1)S(1)}, bf16[4,256,512]{2,1,0:T(8,128)(2,1)}, u32[]{:S(2)}) copy-start(bf16[4,256,512]{2,1,0:T(8,128)(2,1)} %get-tuple-element.1304) | copy-start | bytes 3145732 | tf_op jit(solution)/shard_map/while
  884.2 21.3 %copy-start.9 = (bf16[256,512]{0,1:T(8,128)(2,1)S(1)}, bf16[256,512]{0,1:T(8,128)(2,1)}, u32[]{:S(2)}) copy-start(bf16[256,512]{0,1:T(8,128)(2,1)} %reduce-scatter.15.cloned.1.call-done) | copy-start | bytes 786436 | tf_op jit(solution)/shard_map/while
  910.8 59.1 %all-gather.6.cloned.1.call-start = ((), (), s32[]{:S(2)}) async-start(), calls=%async_computation.10 | async-start | bytes 1622016 | tf_op jit(solution)/shard_map/while/body/eval_jaxpr/all_gather | solution.py:273
  911.6 108.2 %all-gather.10.cloned.1.call-start = ((), (), s32[]{:S(2)}) async-start(), calls=%async_computation.12 | async-start | bytes 1310720 | tf_op jit(solution)/shard_map/while/body/eval_jaxpr/all_gather | solution.py:137
  960.4 14.5 copy-start.16
  960.4 17.8 %copy-start.15 = (bf16[16,512]{1,0:T(8,128)(2,1)S(1)}, bf16[16,512]{1,0:T(8,128)(2,1)}, u32[]{:S(2)}) copy-start(bf16[16,512]{1,0:T(8,128)(2,1)} %get-tuple-element.1311) | copy-start | bytes 49156 | tf_op jit(solution)/shard_map/while
  972.9 59.1 %all-gather.8.cloned.1.call-start = ((), (), s32[]{:S(2)}) async-start(), calls=%async_computation.11 | async-start | bytes 1310720 | tf_op jit(solution)/shard_map/while/body/eval_jaxpr/all_gather | solution.py:138
  973.5 95.5 %all-gather.12.cloned.1.call-start = ((), (), s32[]{:S(2)}) async-start(), calls=%async_computation.13 | async-start | bytes 2162688 | tf_op jit(solution)/shard_map/while/body/eval_jaxpr/all_gather | solution.py:279
  974.3 153.1 %all-gather.14.cloned.1.call-start = ((), (), s32[]{:S(2)}) async-start(), calls=%async_computation.14 | async-start | bytes 2162688 | tf_op jit(solution)/shard_map/while/body/eval_jaxpr/all_gather | solution.py:281
  974.9 209.6 %reduce-scatter.15.cloned.1.call-start = ((), (), s32[]{:S(2)}) async-start(), calls=%async_computation.15 | async-start | bytes 1310720 | tf_op jit(solution)/shard_map/while/body/eval_jaxpr/reduce_scatter | solution.py:187
  1152.9 51.3 %reduce-scatter.17.cloned.1.call-start = ((), (), s32[]{:S(2)}) async-start(), calls=%async_computation.16 | async-start | bytes 1310720 | tf_op jit(solution)/shard_map/while/body/eval_jaxpr/reduce_scatter | solution.py:181
  1184.4 21.4 %copy-start.5 = (bf16[4,256,512]{2,1,0:T(8,128)(2,1)S(1)}, bf16[4,256,512]{2,1,0:T(8,128)(2,1)}, u32[]{:S(2)}) copy-start(bf16[4,256,512]{2,1,0:T(8,128)(2,1)} %get-tuple-element.1304) | copy-start | bytes 3145732 | tf_op jit(solution)/shard_map/while
  1184.4 21.3 %copy-start.9 = (bf16[256,512]{0,1:T(8,128)(2,1)S(1)}, bf16[256,512]{0,1:T(8,128)(2,1)}, u32[]{:S(2)}) copy-start(bf16[256,512]{0,1:T(8,128)(2,1)} %reduce-scatter.15.cloned.1.call-done) | copy-start | bytes 786436 | tf_op jit(solution)/shard_map/while
  1211.0 138.2 %reduce-scatter.9.cloned.1.call-start = ((), (), s32[]{:S(2)}) async-start(), calls=%async_computation.7 | async-start | bytes 1081344 | tf_op jit(solution)/shard_map/reduce_scatter | solution.py:301
  1211.6 241.8 %reduce-scatter.7.cloned.1.call-start = ((), (), s32[]{:S(2)}) async-start(), calls=%async_computation.6 | async-start | bytes 3244032 | tf_op jit(solution)/shard_map/reduce_scatter | solution.py:299
  1212.2 384.0 %reduce-scatter.11.cloned.1.call-start = ((), (), s32[]{:S(2)}) async-start(), calls=%async_computation.8 | async-start | bytes 4325376 | tf_op jit(solution)/shard_map/reduce_scatter | solution.py:305
  1212.7 523.0 %reduce-scatter.13.cloned.1.call-start = ((), (), s32[]{:S(2)}) async-start(), calls=%async_computation.9 | async-start | bytes 4325376 | tf_op jit(solution)/shard_map/reduce_scatter | solution.py:307
  (68 other events, 305.7 us)
Sparse Core Ops, SparseCore 0:
  12.3 57.6 all-gather.5
  73.1 16.9 all-gather.9
  91.8 17.4 all-gather.7
  112.4 56.3 all-gather.11
  172.0 55.2 all-gather.13
  252.9 23.7 reduce-scatter.14
  279.2 24.8 reduce-scatter.16
  315.0 54.9 all-gather.5
  373.1 17.2 all-gather.9
  391.9 17.4 all-gather.7
  412.6 56.3 all-gather.11
  472.1 55.2 all-gather.13
  553.1 23.7 reduce-scatter.14
  579.2 24.8 reduce-scatter.16
  614.7 54.9 all-gather.5
  672.9 17.2 all-gather.9
  691.6 17.4 all-gather.7
  712.3 56.3 all-gather.11
  771.9 55.2 all-gather.13
  852.8 23.7 reduce-scatter.14
  879.2 24.8 reduce-scatter.16
  914.9 54.9 all-gather.5
  973.1 17.2 all-gather.9
  991.8 17.4 all-gather.7
  1012.6 56.3 all-gather.11
  1072.1 55.2 all-gather.13
  1153.0 23.7 reduce-scatter.14
  1179.3 24.8 reduce-scatter.16
Sparse Core Ops, SparseCore 1:
  1214.3 134.9 reduce-scatter.8
  1356.0 97.4 reduce-scatter.6
  1456.2 139.9 reduce-scatter.10
  1599.1 136.6 reduce-scatter.12
where the time goes:
time: 1750 us; the launch traced here: 1740 us
  waiting for transfers between devices  908 us (52%)
  blocking collectives  366 us (21%)
  matrix products  297 us (17%)
  other arithmetic  79.7 us (5%)
  local copies, waits for them, and re-layouts  68.4 us (4%)
    all_gather x4, waiting for transfers between devices, one_batch(): lax.all_gather(w_reduce, ('dp', 'blk'), axis=0, tiled=True)  200 us
    all_gather x4, blocking collectives, one_batch(): lax.all_gather(w_proj, ('dp', 'blk'), axis=0, tiled=True)  165 us
    while x4, blocking collectives  161 us
    reduce_scatter x1, waiting for transfers between devices, body(): lax.psum_scatter(summed[8], ('dp', 'blk'), scatter_dimension=0, tiled=True)  143 us
    reduce_scatter x1, waiting for transfers between devices, body(): lax.psum_scatter(summed[10], ('dp', 'blk'), scatter_dimension=0, tiled=True)  140 us
    reduce_scatter x1, waiting for transfers between devices, body(): lax.psum_scatter(summed[2], ('dp', 'blk'), scatter_dimension=0, tiled=True)  104 us
    all_gather x4, waiting for transfers between devices, one_batch(): lax.all_gather(w_expand, ('dp', 'blk'), axis=0, tiled=True)  99.7 us
    reduce_scatter x1, waiting for transfers between devices, body(): lax.psum_scatter(summed[4], ('dp', 'blk'), scatter_dimension=0, tiled=True)  91.3 us
  transfers between devices with their start and end apart: 32, of which 20 were waited for; matrix products, arithmetic and copies ran while one was open for 17% of the time, Pallas kernels for 0%

commit v1 on v0

v1 whole, which is shorter than its diff:
```python
import functools
import math

import jax
import jax.numpy as jnp
from jax import lax
from jax.experimental import pallas as pl
from jax.experimental.pallas import tpu as pltpu
from jax.sharding import PartitionSpec as P

HEAD_DIM = 32
LONG_IMG = 784
SHORT_IMG = 196
LANES = 128
HEADS_IN_BLOCK = LANES // HEAD_DIM
LONG_KEYS = 896
BF = jnp.bfloat16
F32 = jnp.float32
epsilon = 1e-06
LOG2E = math.log2(math.e)
SCALE = 1.0 / math.sqrt(HEAD_DIM)
MASKED = -1e30
ROWS = 256
A_GAIN, A_SHIFT, Q_BIAS, V_BIAS, P_BIAS, M_GAIN, M_SHIFT, R_BIAS, E_BIAS = range(9)
VEC_ROWS = 16


def nt(left, right):
    return lax.dot_general(left, right, (((1,), (1,)), ((), ())), preferred_element_type=F32)


def nn(left, right):
    return lax.dot_general(left, right, (((1,), (0,)), ((), ())), preferred_element_type=F32)


def tn(left, right):
    return lax.dot_general(left, right, (((0,), (0,)), ((), ())), preferred_element_type=F32)


def pieces(total, size):
    return [(at, min(size, total - at)) for at in range(0, total, size)]


def lanes(rows, width=LANES):
    return lax.broadcasted_iota(jnp.int32, (rows, width), 1)


def to_canonical(swapped, natural, moved):
    total = natural.shape[0]
    tail = LONG_IMG + SHORT_IMG
    moved[0:LONG_IMG] = natural[SHORT_IMG:tail]
    moved[LONG_IMG:tail] = natural[0:SHORT_IMG]
    moved[tail:total] = natural[tail:total]


def to_natural(ordered, moved):
    total = ordered.shape[0]
    tail = LONG_IMG + SHORT_IMG
    moved[SHORT_IMG:tail] = ordered[0:LONG_IMG]
    moved[0:SHORT_IMG] = ordered[LONG_IMG:tail]
    moved[tail:total] = ordered[tail:total]


def norm_parts(values):
    centered = values - jnp.mean(values, axis=-1, keepdims=True)
    inverse = lax.rsqrt(jnp.mean(centered * centered, axis=-1, keepdims=True) + epsilon)
    return centered * inverse, inverse


def norm_back(gradient, normed, inverse, gain):
    scaled = gradient * gain
    return inverse * (
        scaled
        - jnp.mean(scaled, axis=-1, keepdims=True)
        - normed * jnp.mean(scaled * normed, axis=-1, keepdims=True)
    )


def gelu_parts(values):
    size = jnp.abs(values)
    z = size * math.sqrt(0.5)
    t = 1.0 / (1.0 + 0.5 * z)
    poly = 0.17087277
    for factor in (-0.82215223, 1.48851587, -1.13520398, 0.27886807, -0.18628806, 0.09678418,
                   0.37409196, 1.00002368, -1.26551223):
        poly = poly * t + factor
    bell = jnp.exp(-z * z)
    tail = 0.5 * t * bell * jnp.exp(poly)
    phi = jnp.where(values >= 0.0, 1.0 - tail, tail)
    return values * phi, phi + values * (bell * (1.0 / math.sqrt(2.0 * math.pi)))


def fill_masks(aug_q, aug_k):
    total = aug_q.shape[0]
    row = lax.broadcasted_iota(jnp.int32, (total, LANES), 0)
    segment = (row >= LONG_IMG).astype(jnp.int32) + (row >= LONG_IMG + SHORT_IMG).astype(jnp.int32)
    place = lanes(total) % HEAD_DIM
    aug_q[...] = jnp.where(place == segment, 1.0, 0.0).astype(BF)
    aug_k[...] = jnp.where((place < 3) & (place != segment), MASKED, 0.0).astype(BF)


def attend_tiles(total, size):
    tail = total - LONG_IMG
    first = total - 2 * LANES
    return [(at, n, 0, LONG_KEYS, True, at) for at, n in pieces(LONG_IMG, size)] + [
        (LONG_IMG + at, n, first, 2 * LANES, False, at) for at, n in pieces(tail, size)
    ]


def block_columns(ref, j, offset=0):
    return ref[:, pl.ds(pl.multiple_of(offset + j * LANES, LANES), LANES)]


def forward_block(j, qkv, attended, inverse, e_long, e_tail, aug_q, aug_k, size=400):
    total, width = attended.shape
    cols = pl.ds(pl.multiple_of(j * LANES, LANES), LANES)
    qb, kb, vb = (block_columns(qkv, j, width * i) for i in range(3))
    group = lanes(total) // HEAD_DIM
    for head in range(HEADS_IN_BLOCK):
        mine = group == head
        qa = jnp.where(mine, qb, aug_q[...])
        ka = jnp.where(mine, kb, aug_k[...])
        va = jnp.where(mine, vb, jnp.ones_like(vb))
        at = j * HEADS_IN_BLOCK + head
        for row, rows, key, keys, is_long, place in attend_tiles(total, size):
            scores = nt(qa[row : row + rows], ka[key : key + keys])
            exps = jnp.exp2(scores - jnp.max(scores, axis=1, keepdims=True)).astype(BF)
            store = e_long if is_long else e_tail
            store[at, place : place + rows, :] = exps
            product = nn(exps, va[key : key + keys])
            inv = 1.0 / pltpu.roll(product, HEAD_DIM, 1)
            out = (product * inv).astype(BF)
            here = (pl.ds(row, rows), cols)
            if head == 0:
                attended[here] = out
                inverse[here] = inv
            else:
                keep = lanes(rows) // HEAD_DIM == head
                attended[here] = jnp.where(keep, out, attended[here])
                inverse[here] = jnp.where(keep, inv, inverse[here])


def backward_block(j, qkv, attended, inverse, e_long, e_tail, d_att, dq_b, dk_t, dv_t, size=400):
    total, width = attended.shape
    qb, kb, vb = (block_columns(qkv, j, width * i) for i in range(3))
    group = lanes(total) // HEAD_DIM
    scaled = block_columns(d_att, j).astype(F32) * block_columns(inverse, j)
    inner = scaled * block_columns(attended, j).astype(F32)
    from_group = lax.broadcasted_iota(jnp.int32, (LANES, LANES), 0) // HEAD_DIM
    to_group = lanes(LANES) // HEAD_DIM
    spread = jnp.where((from_group + 1) % HEADS_IN_BLOCK == to_group, 1.0, 0.0).astype(BF)
    high = inner.astype(BF)
    low = (inner - high.astype(F32)).astype(BF)
    sums = nn(high, spread) + nn(low, spread)
    sum_high = sums.astype(BF)
    sum_low = (sums - sum_high.astype(F32)).astype(BF)
    place = lanes(total) % HEAD_DIM
    zeros = jnp.zeros_like(sum_high)
    aug = jnp.where(place == 0, -sum_high, jnp.where(place == 1, -sum_low, zeros))
    scaled = scaled.astype(BF)
    q_t, s_t = qb.T, scaled.T
    for head in range(HEADS_IN_BLOCK):
        mine = group == head
        left = jnp.where(mine, scaled, jnp.where(group == (head + 1) % HEADS_IN_BLOCK, aug, zeros))
        va = jnp.where(mine, vb, jnp.ones_like(vb))
        at = j * HEADS_IN_BLOCK + head
        of_head = slice(HEAD_DIM * head, HEAD_DIM * (head + 1))
        sums_of = {}
        for row, rows, key, keys, is_long, where in attend_tiles(total, size):
            store = e_long if is_long else e_tail
            exps = store[at, where : where + rows, :]
            d_scores = (exps.astype(F32) * nt(left[row : row + rows], va[key : key + keys])).astype(BF)
            dq = (nn(d_scores, kb[key : key + keys]) * SCALE).astype(BF)
            here = pl.ds(row, rows)
            dq_b[here] = dq if head == 0 else jnp.where(lanes(rows) // HEAD_DIM == head, dq, dq_b[here])
            more_v = nn(s_t[of_head, row : row + rows], exps)
            more_k = nn(q_t[of_head, row : row + rows], d_scores)
            if is_long in sums_of:
                more_v, more_k = sums_of[is_long][0] + more_v, sums_of[is_long][1] + more_k
            sums_of[is_long] = (more_v, more_k)
        first = total - 2 * LANES
        both = LONG_KEYS - first
        for ref, which, factor in ((dv_t, 0, None), (dk_t, 1, 1.0 / LOG2E)):
            long_part, tail_part = sums_of[True][which], sums_of[False][which]
            if factor is not None:
                long_part, tail_part = long_part * factor, tail_part * factor
            ref[of_head, 0:first] = long_part[:, :first]
            ref[of_head, first:LONG_KEYS] = long_part[:, first:] + tail_part[:, :both]
            ref[of_head, LONG_KEYS:total] = tail_part[:, both:]
    for i, value in enumerate((dq_b[...], dk_t[...].T.astype(BF), dv_t[...].T.astype(BF))):
        qkv[:, pl.ds(pl.multiple_of(i * width + j * LANES, LANES), LANES)] = value


BUFFERS = (
    "x_in", "cot", "xc", "qkv", "attended", "inverse", "e_long", "e_tail", "aug_q", "aug_k", "middle",
    "acc_a", "acc_b", "hb", "act", "d_exp", "dq_b", "dk_t", "dv_t",
    "w_qkv", "w_proj", "w_expand", "w_reduce",
)


def buffers(total, width, ff):
    heads = width // HEAD_DIM
    rows = (total, width)
    return {
        "x_in": (rows, BF),
        "cot": (rows, BF),
        "xc": (rows, BF),
        "qkv": ((total, 3 * width), BF),
        "attended": (rows, BF),
        "inverse": (rows, F32),
        "e_long": ((heads, LONG_IMG, LONG_KEYS), BF),
        "e_tail": ((heads, total - LONG_IMG, 2 * LANES), BF),
        "aug_q": ((total, LANES), BF),
        "aug_k": ((total, LANES), BF),
        "middle": (rows, F32),
        "acc_a": (rows, F32),
        "acc_b": (rows, F32),
        "hb": (rows, BF),
        "act": (rows, BF),
        "d_exp": (rows, BF),
        "dq_b": ((total, LANES), BF),
        "dk_t": ((LANES, total), F32),
        "dv_t": ((LANES, total), F32),
        "w_qkv": ((width, 3 * width), BF),
        "w_proj": ((width, width), BF),
        "w_expand": ((width, ff), BF),
        "w_reduce": ((ff, width), BF),
    }


def compute(b, flag, vec, g_vec, hooks):
    total, width = b["xc"].shape
    ff = b["w_expand"].shape[1]
    row_tiles = pieces(total, ROWS)
    swapped = flag[0:1, :] > 0.5
    acc_a, acc_b = b["acc_a"], b["acc_b"]

    def vector(row):
        return vec[row : row + 1, :]

    def add_sum(row, values):
        g_vec[row : row + 1, :] = g_vec[row : row + 1, :] + jnp.sum(values, axis=0, keepdims=True)

    def load(source, target):
        for at, n in row_tiles:
            acc_a[at : at + n] = source[at : at + n].astype(F32)
        to_canonical(swapped, acc_a, acc_b)
        for at, n in row_tiles:
            target[at : at + n] = jnp.where(swapped, acc_b[at : at + n], acc_a[at : at + n]).astype(BF)

    def unload(values, moved, target):
        to_natural(values, moved)
        for at, n in row_tiles:
            target[at : at + n] = jnp.where(swapped, moved[at : at + n], values[at : at + n]).astype(BF)

    g_vec[...] = jnp.zeros_like(g_vec)
    fill_masks(b["aug_q"], b["aug_k"])
    hooks("need tokens")
    load(b["x_in"], b["xc"])
    hooks("need qkv")
    ha, qkv, w_qkv = b["x_in"], b["qkv"], b["w_qkv"]
    for at, n in row_tiles:
        rows = slice(at, at + n)
        normed, _ = norm_parts(b["xc"][rows].astype(F32))
        lowered = (normed * vector(A_GAIN) + vector(A_SHIFT)).astype(BF)
        ha[rows] = lowered
        projected = nn(lowered, w_qkv[...])
        qkv[rows, 0:width] = ((projected[:, :width] + vector(Q_BIAS)) * (SCALE * LOG2E)).astype(BF)
        qkv[rows, width : 2 * width] = projected[:, width : 2 * width].astype(BF)
        qkv[rows, 2 * width : 3 * width] = (projected[:, 2 * width :] + vector(V_BIAS)).astype(BF)

    blocks = width // LANES
    attended, inverse, e_long, e_tail = b["attended"], b["inverse"], b["e_long"], b["e_tail"]

    def one_forward(j, carried):
        forward_block(j, qkv, attended, inverse, e_long, e_tail, b["aug_q"], b["aug_k"])
        return carried

    lax.fori_loop(0, blocks, one_forward, 0)

    hooks("need cotangent")
    cot, middle, hb, act, d_exp = b["cot"], b["middle"], b["hb"], b["act"], b["d_exp"]
    w_proj, w_expand, w_reduce = b["w_proj"], b["w_expand"], b["w_reduce"]
    load(cot, cot)
    hooks("need proj")
    for at, n in row_tiles:
        rows = slice(at, at + n)
        mid = b["xc"][rows].astype(F32) + (nn(attended[rows], w_proj[...]) + vector(P_BIAS))
        middle[rows] = mid
        normed, _ = norm_parts(mid)
        hb[rows] = (normed * vector(M_GAIN) + vector(M_SHIFT)).astype(BF)
        acc_a[rows] = mid + vector(R_BIAS)
        add_sum(R_BIAS, cot[rows].astype(F32))

    hooks("need expand")
    hooks("need reduce")
    for part in range(ff // width):
        cols = slice(part * width, (part + 1) * width)
        for at, n in row_tiles:
            rows = slice(at, at + n)
            value, slope = gelu_parts(nn(hb[rows], w_expand[:, cols]) + vector(E_BIAS + part))
            low = value.astype(BF)
            act[rows] = low
            acc_a[rows] = acc_a[rows] + nn(low, w_reduce[cols, :])
            d_low = (nt(cot[rows], w_reduce[cols, :]) * slope).astype(BF)
            d_exp[rows] = d_low
            more = nt(d_low, w_expand[:, cols])
            acc_b[rows] = more if part == 0 else acc_b[rows] + more
            add_sum(E_BIAS + part, d_low.astype(F32))
        w_reduce[cols, :] = tn(act[...], cot[...]).astype(BF)
        w_expand[:, cols] = tn(hb[...], d_exp[...]).astype(BF)
    hooks("have reduce")
    hooks("have expand")

    d_att = d_exp
    for at, n in row_tiles:
        rows = slice(at, at + n)
        gradient = acc_b[rows]
        normed, inv = norm_parts(middle[rows])
        d_mid = cot[rows].astype(F32) + norm_back(gradient, normed, inv, vector(M_GAIN))
        add_sum(M_GAIN, gradient * normed)
        add_sum(M_SHIFT, gradient)
        middle[rows] = d_mid
        d_branch = d_mid.astype(BF)
        act[rows] = d_branch
        add_sum(P_BIAS, d_branch.astype(F32))
        d_att[rows] = nt(d_branch, w_proj[...]).astype(BF)
    w_proj[...] = tn(attended[...], act[...]).astype(BF)
    hooks("have proj")
    unload(acc_a, acc_b, hb)
    hooks("have result")

    def one_backward(j, carried):
        backward_block(j, qkv, attended, inverse, e_long, e_tail, d_att, b["dq_b"], b["dk_t"], b["dv_t"])
        return carried

    lax.fori_loop(0, blocks, one_backward, 0)

    for at, n in row_tiles:
        rows = slice(at, at + n)
        acc_b[rows] = nt(qkv[rows], w_qkv[...])
        add_sum(Q_BIAS, qkv[rows, 0:width].astype(F32))
        add_sum(V_BIAS, qkv[rows, 2 * width : 3 * width].astype(F32))
    w_qkv[...] = tn(ha[...], qkv[...]).astype(BF)
    hooks("have qkv")
    for at, n in row_tiles:
        rows = slice(at, at + n)
        gradient = acc_b[rows]
        normed, inv = norm_parts(b["xc"][rows].astype(F32))
        add_sum(A_GAIN, gradient * normed)
        add_sum(A_SHIFT, gradient)
        acc_a[rows] = middle[rows] + norm_back(gradient, normed, inv, vector(A_GAIN))
    hooks("have vectors")
    unload(acc_a, acc_b, act)
    hooks("have grad")


def local_kernel(flag, vec, x_in, cot_in, w_qkv, w_proj, w_expand, w_reduce,
                 result, grad_x, g_qkv, g_proj, g_expand, g_reduce, g_vec, *scratch):
    b = dict(zip(BUFFERS, scratch))
    sems = scratch[len(BUFFERS)]
    weights = {"qkv": (w_qkv, g_qkv), "proj": (w_proj, g_proj), "expand": (w_expand, g_expand), "reduce": (w_reduce, g_reduce)}
    moves = {"need tokens": (x_in, b["x_in"]), "need cotangent": (cot_in, b["cot"])}
    for name, (source, target) in weights.items():
        moves["need " + name] = (source, b["w_" + name])
        moves["have " + name] = (b["w_" + name], target)
    moves["have result"] = (b["hb"], result)
    moves["have grad"] = (b["act"], grad_x)
    copies = {name: pltpu.make_async_copy(source, target, sems.at[i]) for i, (name, (source, target)) in enumerate(moves.items())}
    for name, copy in copies.items():
        if name.startswith("need"):
            copy.start()

    def hooks(name):
        if name in copies:
            if name.startswith("need"):
                copies[name].wait()
            else:
                copies[name].start()

    compute(b, flag, vec, g_vec, hooks)
    for name, copy in copies.items():
        if name.startswith("have"):
            copy.wait()


def run_block(flag, vec, x_in, cot_in, w_qkv, w_proj, w_expand, w_reduce):
    vmem, anywhere = pl.BlockSpec(memory_space=pltpu.VMEM), pl.BlockSpec(memory_space=pl.ANY)
    total, width = x_in.shape
    scratch = buffers(total, width, w_expand.shape[1])
    like = (x_in, x_in, w_qkv, w_proj, w_expand, w_reduce)
    return pl.pallas_call(
        local_kernel,
        out_shape=[jax.ShapeDtypeStruct(one.shape, BF) for one in like]
        + [jax.ShapeDtypeStruct((VEC_ROWS, width), F32)],
        in_specs=[vmem] * 2 + [anywhere] * 6,
        out_specs=[anywhere] * 6 + [vmem],
        scratch_shapes=[pltpu.VMEM(*scratch[name]) for name in BUFFERS] + [pltpu.SemaphoreType.DMA((12,))],
        compiler_params=pltpu.CompilerParams(vmem_limit_bytes=63 * 2**20),
    )(flag, vec, x_in, cot_in, w_qkv, w_proj, w_expand, w_reduce)


def body(
    tokens, lengths, attn_gain, attn_shift, w_qkv, qv_bias, w_proj, proj_bias,
    mlp_gain, mlp_shift, w_expand, expand_bias, w_reduce, reduce_bias, cotangent,
):
    axes = ("dp", "blk")
    width = tokens.shape[2]
    me = lax.axis_index("blk")
    devices = lax.axis_size(axes)
    index = lax.axis_index("dp") * lax.axis_size("blk") + me
    first = lax.dynamic_index_in_dim(lengths, me, 0, keepdims=False)[0, 0]
    flag = jnp.broadcast_to((first == SHORT_IMG).astype(F32), (8, width))

    def exchange(rows):
        return lax.all_to_all(rows, "blk", 0, 0, tiled=True)

    def gather(shard):
        return lax.all_gather(shard, axes, axis=0, tiled=True)

    vectors = (attn_gain, attn_shift, qv_bias, proj_bias, mlp_gain, mlp_shift, reduce_bias, expand_bias)
    sizes = [one.shape[0] for one in vectors]
    packed = lax.all_gather(jnp.concatenate(vectors), axes, axis=0)
    starts = [sum(sizes[:i]) for i in range(len(sizes))]
    full = [packed[:, at : at + size].reshape(-1, width) for at, size in zip(starts, sizes)]
    vec = jnp.concatenate(full, axis=0).astype(F32)
    vec = jnp.pad(vec, ((0, VEC_ROWS - vec.shape[0]), (0, 0)))
    result, grad_x, g_qkv, g_proj, g_expand, g_reduce, g_vec = run_block(
        flag, vec, exchange(tokens).reshape(-1, width), exchange(cotangent).reshape(-1, width),
        gather(w_qkv), gather(w_proj), gather(w_expand), gather(w_reduce),
    )

    def scatter(whole):
        return lax.psum_scatter(whole.astype(F32), axes, scatter_dimension=0, tiled=True)

    g_vec = lax.psum(g_vec, axes).reshape(-1)
    offsets = {}
    at = 0
    for name, size in zip(("ag", "as", "qv", "pb", "mg", "ms", "rb", "eb"), sizes):
        offsets[name] = lax.dynamic_slice(g_vec, (at + index * size,), (size,))
        at += size * devices
    return (
        exchange(result.reshape(tokens.shape)),
        exchange(grad_x.reshape(tokens.shape)),
        offsets["ag"],
        offsets["as"],
        scatter(g_qkv),
        offsets["qv"],
        scatter(g_proj),
        offsets["pb"],
        offsets["mg"],
        offsets["ms"],
        scatter(g_expand),
        offsets["eb"],
        scatter(g_reduce),
        offsets["rb"],
    )


def solution(mesh):
    both = ("dp", "blk")
    rows = P(None, both, None)
    vector, matrix = P(both), P(both, None)
    weights = (
        vector, vector, matrix, vector, matrix, vector, vector, vector, matrix, vector, matrix, vector,
    )
    return jax.shard_map(
        body,
        mesh=mesh,
        in_specs=(rows, P(None, "dp", None)) + weights + (rows,),
        out_specs=(rows, rows) + weights,
        check_vma=False,
    )
```

time: 1750 us -> 816 us (0.47)
  waiting for transfers between devices: 908 us -> 496 us
  matrix products: 297 us -> 0 us
  blocking collectives: 366 us -> 182 us
  Pallas kernels: 0 us -> 88 us
  other arithmetic: 79.7 us -> 10.1 us
  local copies, waits for them, and re-layouts: 68.4 us -> 10.2 us
    all_gather x20 -> x3, waiting for transfers between devices: 338 us -> 55.7 us  [gather(): return lax.all_gather(shard, axes, axis=0, tiled=True)]
    dot_general x68 -> x0, matrix products: 254 us -> none  [the longest x16 61 us: matmul(): return jnp.dot(left_hand, right_hand, preferred_element_type=jnp.float32)]
    while x4 -> x0, blocking collectives: 161 us -> none
    all_gather x4 -> x1, blocking collectives: 165 us -> 44.2 us  [gather(): return lax.all_gather(shard, axes, axis=0, tiled=True)]
    reduce_scatter x12 -> x4, waiting for transfers between devices: 558 us -> 438 us  [scatter(): lax.psum_scatter(whole.astype(F32), axes, scatter_dimension=0, tiled=True)]
    pallas_call x0 -> x1, Pallas kernels: none -> 88 us  [run_block(): pl.pallas_call(local_kernel, out_shape=[jax.ShapeDtypeStruct(one.shape, B...]
    psum x0 -> x1, blocking collectives: none -> 48.3 us  [body(): g_vec = lax.psum(g_vec, axes).reshape(-1)]
    while x236 -> x0, local copies, waits for them, and re-layouts: 44.9 us -> none
  transfers between devices with their start and end apart: 32 -> 9, of which waited for: 20 -> 5; matrix products, arithmetic and copies ran while one was open for 17% -> 1% of each run, Pallas kernels for 0% -> 0%
where the time goes in v1:
time: 816 us; the launch traced here: 809 us
  waiting for transfers between devices  496 us (61%)
  blocking collectives  182 us (22%)
  Pallas kernels  88 us (11%)
  between operations  14.6 us (2%)
  local copies, waits for them, and re-layouts  10.2 us (1%)
  other arithmetic  10.1 us (1%)
    reduce_scatter x4, waiting for transfers between devices, scatter(): lax.psum_scatter(whole.astype(F32), axes, scatter_dimension=0, tiled=True)  438 us
    pallas_call x1, Pallas kernels, run_block(): pl.pallas_call(local_kernel, out_shape=[jax.ShapeDtypeStruct(one.shape, B...  88 us
    all_gather x3, waiting for transfers between devices, gather(): return lax.all_gather(shard, axes, axis=0, tiled=True)  55.7 us
    unnamed x1, blocking collectives  51.1 us
    psum x1, blocking collectives, body(): g_vec = lax.psum(g_vec, axes).reshape(-1)  48.3 us
    all_gather x1, blocking collectives, gather(): return lax.all_gather(shard, axes, axis=0, tiled=True)  44.2 us
    all_to_all x2, blocking collectives, exchange(): return lax.all_to_all(rows, 'blk', 0, 0, tiled=True)  38.2 us
  transfers between devices with their start and end apart: 9, of which 5 were waited for; matrix products, arithmetic and copies ran while one was open for 1% of the time, Pallas kernels for 0%

profile of v1, /device:TPU:0, one launch (start us, length us, event | category | flops | bytes accessed | tf_op | source)
XLA Modules:
  0.0 808.8 jit_solution(9246536590344703317)
XLA Ops:
  7.2 0.7 all-gather.5.cloned.1.call-update
  8.0 0.7 all-gather.7.cloned.1.call-update
  8.7 0.7 all-gather.9.cloned.1.call-update
  9.5 19.9 %all_to_all.20 = bf16[4,256,512]{2,1,0:T(8,128)(2,1)} all-to-all(bf16[4,256,512]{2,1,0:T(8,128)(2,1)} %param.15), channel_id=1, replica_groups=mesh['dp'=8,'blk'=4] {'blk'}, dimensions={0} | all-to-all | bytes 2097152 | tf_op jit(solution)/shard_map/all_to_all | solution.py:416
  29.4 4.2 all-to-all-start.1
  33.6 0.0 reduce-scatter.7.cloned.1.call-start
  33.8 0.1 concatenate.6
  33.9 0.2 dynamic-update-slice
  34.1 51.1 %all-reduce.1 = bf16[6144]{0:T(1024)(128)(2,1)S(1)} all-reduce(bf16[6144]{0:T(1024)(128)(2,1)S(1)} %dynamic-update-slice), channel_id=2, replica_groups=mesh['dp'=8,'blk'=4] {'dp','blk'}, use_global_device_ids=true, to_apply=%add.1 | all-reduce | flops 6144 | bytes 24576
  85.2 0.1 reshape.85
  85.3 0.1 slice.38
  85.4 0.1 fusion.1
  85.5 0.1 reshape.71
  85.6 0.1 reshape.72
  85.6 0.1 reshape.74
  85.7 0.1 reshape.75
  85.8 0.1 reshape.76
  85.9 0.1 reshape.77
  86.0 0.1 reshape.78
  86.1 0.1 reshape.73
  86.2 0.2 dynamic-slice_reduce_fusion
  86.4 0.1 concatenate.7
  86.5 0.6 pad_convert_fusion.vec
  87.1 44.2 %all_gather.21.w_proj = bf16[512,512]{1,0:T(8,128)(2,1)} all-gather(bf16[16,512]{1,0:T(8,128)(2,1)S(1)} %copy-done.6), channel_id=1, replica_groups=mesh['dp'=8,'blk'=4] {'dp','blk'}, dimensions={0}, use_global_device_ids=true | all-gather | bytes 540672 | tf_op jit(solution)/shard_map/all_gather | solution.py:419
  131.4 55.7 %all-gather.9.cloned.1.call-done.w_reduce = bf16[2048,512]{1,0:T(8,128)(2,1)} async-done(((bf16[64,512]{1,0:T(8,128)(2,1)}), bf16[2048,512]{1,0:T(8,128)(2,1)}) %all-gather.9.cloned.1.call-update) | async-done | bytes 2097168 | tf_op jit(solution)/shard_map/all_gather | solution.py:419
  187.1 0.6 broadcast_in_dim.3.flag
  187.7 88.0 %shard_map.254 = (bf16[1024,512]{1,0:T(8,128)(2,1)}, bf16[1024,512]{1,0:T(8,128)(2,1)}, bf16[512,1536]{1,0:T(8,128)(2,1)}, bf16[512,512]{1,0:T(8,128)(2,1)}, bf1...) custom-call(f32[8,512]{1,0:T(8,128)} %broadcast_in_dim.3.flag, ...), custom_call_target="tpu_custom_call" | custom-call | tf_op jit(solution)/shard_map/pallas_call | solution.py:392
  275.7 2.3 convert_element_type.24
  278.0 0.0 reduce-scatter.5.cloned.1.call-start
  278.1 2.1 convert_element_type.23
  280.2 0.0 reduce-scatter.11.cloned.1.call-start
  280.3 1.5 copy-done.2
  281.8 2.5 convert_element_type.26
  284.4 1.5 copy-done.1
  285.9 2.5 convert_element_type.25
  288.5 1.2 copy-done.4
  289.7 18.3 %all_to_all.21 = bf16[4,256,512]{2,1,0:T(8,128)(2,1)S(1)} all-to-all(bf16[4,256,512]{2,1,0:T(8,128)(2,1)S(1)} %bitcast.10), channel_id=1, replica_groups=mesh['dp'=8,'blk'=4] {'blk'}, dimensions={0} | all-to-all | bytes 2097152 | tf_op jit(solution)/shard_map/all_to_all | solution.py:416
  308.0 3.5 all-to-all-start.3
  311.6 48.3 %psum.7 = f32[8192]{0:T(1024)S(1)} all-reduce(f32[8192]{0:T(1024)S(1)} %bitcast.11), channel_id=1, replica_groups=mesh['dp'=8,'blk'=4] {'dp','blk'}, use_global_device_ids=true, to_apply=%region_0.1 | all-reduce | flops 8192 | bytes 65536 | tf_op jit(solution)/shard_map/psum | solution.py:436
  359.9 0.6 dynamic_slice.31
  360.5 0.6 dynamic_slice.35
  361.1 0.6 fusion
  361.7 50.8 %reduce-scatter.7.cloned.1.call-done = f32[16,512]{1,0:T(8,128)} async-done(((f32[512,512]{1,0:T(8,128)}), f32[16,512]{1,0:T(8,128)}) %reduce-scatter.7.cloned.1.call-update) | async-done | bytes 32784 | tf_op jit(solution)/shard_map/reduce_scatter | solution.py:434
  412.5 104.3 %reduce-scatter.5.cloned.1.call-done = f32[16,1536]{1,0:T(8,128)} async-done(((f32[512,1536]{1,0:T(8,128)}), f32[16,1536]{1,0:T(8,128)}) %reduce-scatter.5.cloned.1.call-update) | async-done | bytes 98320 | tf_op jit(solution)/shard_map/reduce_scatter | solution.py:434
  516.8 143.1 %reduce-scatter.11.cloned.1.call-done = f32[64,512]{1,0:T(8,128)} async-done(((f32[2048,512]{1,0:T(8,128)}), f32[64,512]{1,0:T(8,128)}) %reduce-scatter.11.cloned.1.call-update) | async-done | bytes 131088 | tf_op jit(solution)/shard_map/reduce_scatter | solution.py:434
  659.9 139.9 %reduce-scatter.9.cloned.1.call-done = f32[16,2048]{1,0:T(8,128)} async-done(((f32[512,2048]{1,0:T(8,128)}), f32[16,2048]{1,0:T(8,128)}) %reduce-scatter.9.cloned.1.call-update) | async-done | bytes 131088 | tf_op jit(solution)/shard_map/reduce_scatter | solution.py:434
  799.8 1.0 copy.33
  800.8 1.0 copy.34
  (42 shorter events, 0.3 us)
Async XLA Ops:
  7.2 79.0 %copy-start = (s32[4,1,2]{0,2,1:T(2,128)S(1)}, s32[4,1,2]{0,2,1:T(2,128)}, u32[]{:S(2)}) copy-start(s32[4,1,2]{0,2,1:T(2,128)} %param.16) | copy-start | bytes 100
  7.2 124.2 %all-gather.5.cloned.1.call-start = ((), (), s32[]{:S(2)}) async-start(), calls=%async_computation.8 | async-start | bytes 1622016 | tf_op jit(solution)/shard_map/all_gather | solution.py:419
  7.9 123.4 %all-gather.7.cloned.1.call-start = ((), (), s32[]{:S(2)}) async-start(), calls=%async_computation.9 | async-start | bytes 2162688 | tf_op jit(solution)/shard_map/all_gather | solution.py:419
  8.7 178.4 %all-gather.9.cloned.1.call-start = ((), (), s32[]{:S(2)}) async-start(), calls=%async_computation.10 | async-start | bytes 2162688 | tf_op jit(solution)/shard_map/all_gather | solution.py:419
  9.4 24.3 %copy-start.7 = (bf16[16]{0:T(256)(128)(2,1)S(1)}, bf16[16]{0:T(256)(128)(2,1)}, u32[]{:S(2)}) copy-start(bf16[16]{0:T(256)(128)(2,1)} %param.17) | copy-start | bytes 100
  9.4 24.3 %copy-start.8 = (bf16[16]{0:T(256)(128)(2,1)S(1)}, bf16[16]{0:T(256)(128)(2,1)}, u32[]{:S(2)}) copy-start(bf16[16]{0:T(256)(128)(2,1)} %param.18) | copy-start | bytes 100
  9.4 24.3 %copy-start.9 = (bf16[32]{0:T(256)(128)(2,1)S(1)}, bf16[32]{0:T(256)(128)(2,1)}, u32[]{:S(2)}) copy-start(bf16[32]{0:T(256)(128)(2,1)} %param.20) | copy-start | bytes 196
  9.4 24.3 %copy-start.10 = (bf16[16]{0:T(256)(128)(2,1)S(1)}, bf16[16]{0:T(256)(128)(2,1)}, u32[]{:S(2)}) copy-start(bf16[16]{0:T(256)(128)(2,1)} %param.22) | copy-start | bytes 100
  9.5 24.3 %copy-start.11 = (bf16[16]{0:T(256)(128)(2,1)S(1)}, bf16[16]{0:T(256)(128)(2,1)}, u32[]{:S(2)}) copy-start(bf16[16]{0:T(256)(128)(2,1)} %param.23) | copy-start | bytes 100
  9.5 24.3 %copy-start.12 = (bf16[16]{0:T(256)(128)(2,1)S(1)}, bf16[16]{0:T(256)(128)(2,1)}, u32[]{:S(2)}) copy-start(bf16[16]{0:T(256)(128)(2,1)} %param.24) | copy-start | bytes 100
  9.5 24.3 %copy-start.13 = (bf16[16]{0:T(256)(128)(2,1)S(1)}, bf16[16]{0:T(256)(128)(2,1)}, u32[]{:S(2)}) copy-start(bf16[16]{0:T(256)(128)(2,1)} %param.28) | copy-start | bytes 100
  9.5 24.3 %copy-start.14 = (bf16[64]{0:T(256)(128)(2,1)S(1)}, bf16[64]{0:T(256)(128)(2,1)}, u32[]{:S(2)}) copy-start(bf16[64]{0:T(256)(128)(2,1)} %param.26) | copy-start | bytes 388
  9.5 77.6 %copy-start.6 = (bf16[16,512]{1,0:T(8,128)(2,1)S(1)}, bf16[16,512]{1,0:T(8,128)(2,1)}, u32[]{:S(2)}) copy-start(bf16[16,512]{1,0:T(8,128)(2,1)} %param.21) | copy-start | bytes 49156
  29.4 102.0 %all-to-all-start.1 = ((bf16[4,256,512]{2,1,0:T(8,128)(2,1)}), bf16[4,256,512]{2,1,0:T(8,128)(2,1)}, u32[]{:S(2)}, u32[]{:S(2)}) async-start(bf16[4,256,512]{2,1,0:T(8,128)(2,1)} %param.29), calls=%async_computation.1 | async-start | bytes 2097152 | tf_op jit(solution)/shard_map/all_to_all | solution.py:416
  33.6 378.8 %reduce-scatter.7.cloned.1.call-start = ((), (), s32[]{:S(2)}) async-start(), calls=%async_computation.12 | async-start | bytes 1081344 | tf_op jit(solution)/shard_map/reduce_scatter | solution.py:434
  275.7 2.4 copy-start.3
  278.0 238.8 %reduce-scatter.5.cloned.1.call-start = ((), (), s32[]{:S(2)}) async-start(), calls=%async_computation.11 | async-start | bytes 3244032 | tf_op jit(solution)/shard_map/reduce_scatter | solution.py:434
  280.2 1.6 copy-start.2
  280.2 379.7 %reduce-scatter.11.cloned.1.call-start = ((), (), s32[]{:S(2)}) async-start(), calls=%async_computation.14 | async-start | bytes 4325376 | tf_op jit(solution)/shard_map/reduce_scatter | solution.py:434
  284.3 1.6 copy-start.1
  284.3 515.5 %reduce-scatter.9.cloned.1.call-start = ((), (), s32[]{:S(2)}) async-start(), calls=%async_computation.13 | async-start | bytes 4325376 | tf_op jit(solution)/shard_map/reduce_scatter | solution.py:434
  288.4 1.2 copy-start.4
  289.7 21.9 %copy-start.5 = (f32[16,512]{1,0:T(8,128)S(1)}, f32[16,512]{1,0:T(8,128)}, u32[]{:S(2)}) copy-start(f32[16,512]{1,0:T(8,128)} %get-tuple-element.23) | copy-start | bytes 98308
  308.0 53.7 %all-to-all-start.3 = ((bf16[4,256,512]{2,1,0:T(8,128)(2,1)}), bf16[4,256,512]{2,1,0:T(8,128)(2,1)S(1)}, u32[]{:S(2)}, u32[]{:S(2)}) async-start(bf16[4,256,512]{2,1,0:T(8,128)(2,1)} %bitcast.4), calls=%async_computation.3 | async-start | bytes 2097152 | tf_op jit(solution)/shard_map/all_to_all | solution.py:416
Sparse Core Ops, SparseCore 0:
  10.9 58.8 all-gather.4
  72.7 55.9 all-gather.6
  131.5 55.5 all-gather.8
  278.1 134.2 reduce-scatter.6
  419.2 97.5 reduce-scatter.4
  519.6 140.2 reduce-scatter.10
  662.9 136.9 reduce-scatter.8

commit v2 on v1

v2 whole, which is shorter than its diff:
```python
import math
import typing

import jax
import jax.numpy as jnp
from jax import lax
from jax.experimental import pallas as pl
from jax.experimental.pallas import tpu as pltpu
from jax.sharding import PartitionSpec as P

HEAD_DIM = 32
LONG_IMG = 784
SHORT_IMG = 196
LANES = 128
HEADS_IN_BLOCK = LANES // HEAD_DIM
LONG_KEYS = 896
BF = jnp.bfloat16
F32 = jnp.float32
epsilon = 1e-06
LOG2E = math.log2(math.e)
SCALE = 1.0 / math.sqrt(HEAD_DIM)
MASKED = -1e30
ROWS = 256
A_GAIN, A_SHIFT, Q_BIAS, V_BIAS, P_BIAS, M_GAIN, M_SHIFT, R_BIAS, E_BIAS = range(9)
VEC_ROWS = 16
PACKED = 16
TRIO = 3 * LANES
CHUNKS = 4
Z, Y, X, C = range(4)
SPREAD = (4, 2, 2, 2)
QKV, PROJ, EXPAND, REDUCE = range(4)
GATHER_ORDER = ((X, Z, Y), (X, Z, Y), (X, Z, Y), (Z, Y, X))
SCATTER_ORDER = tuple((C,) + order[::-1] for order in GATHER_ORDER)


def nt(left, right):
    return lax.dot_general(left, right, (((1,), (1,)), ((), ())), preferred_element_type=F32)


def nn(left, right):
    return lax.dot_general(left, right, (((1,), (0,)), ((), ())), preferred_element_type=F32)


def tn(left, right):
    return lax.dot_general(left, right, (((0,), (0,)), ((), ())), preferred_element_type=F32)


def pieces(total, size):
    return [(at, min(size, total - at)) for at in range(0, total, size)]


def lanes(rows, width=LANES):
    return lax.broadcasted_iota(jnp.int32, (rows, width), 1)


def to_canonical(swapped, natural, moved):
    total = natural.shape[0]
    tail = LONG_IMG + SHORT_IMG
    moved[0:LONG_IMG] = natural[SHORT_IMG:tail]
    moved[LONG_IMG:tail] = natural[0:SHORT_IMG]
    moved[tail:total] = natural[tail:total]


def to_natural(ordered, moved):
    total = ordered.shape[0]
    tail = LONG_IMG + SHORT_IMG
    moved[SHORT_IMG:tail] = ordered[0:LONG_IMG]
    moved[0:SHORT_IMG] = ordered[LONG_IMG:tail]
    moved[tail:total] = ordered[tail:total]


def norm_parts(values):
    centered = values - jnp.mean(values, axis=-1, keepdims=True)
    inverse = lax.rsqrt(jnp.mean(centered * centered, axis=-1, keepdims=True) + epsilon)
    return centered * inverse, inverse


def norm_back(gradient, normed, inverse, gain):
    scaled = gradient * gain
    return inverse * (
        scaled
        - jnp.mean(scaled, axis=-1, keepdims=True)
        - normed * jnp.mean(scaled * normed, axis=-1, keepdims=True)
    )


def gelu_parts(values):
    size = jnp.abs(values)
    z = size * math.sqrt(0.5)
    t = 1.0 / (1.0 + 0.5 * z)
    poly = 0.17087277
    for factor in (-0.82215223, 1.48851587, -1.13520398, 0.27886807, -0.18628806, 0.09678418,
                   0.37409196, 1.00002368, -1.26551223):
        poly = poly * t + factor
    bell = jnp.exp(-z * z)
    tail = 0.5 * t * bell * jnp.exp(poly)
    phi = jnp.where(values >= 0.0, 1.0 - tail, tail)
    return values * phi, phi + values * (bell * (1.0 / math.sqrt(2.0 * math.pi)))


def fill_masks(aug_q, aug_k):
    total = aug_q.shape[0]
    row = lax.broadcasted_iota(jnp.int32, (total, LANES), 0)
    segment = (row >= LONG_IMG).astype(jnp.int32) + (row >= LONG_IMG + SHORT_IMG).astype(jnp.int32)
    place = lanes(total) % HEAD_DIM
    aug_q[...] = jnp.where(place == segment, 1.0, 0.0).astype(BF)
    aug_k[...] = jnp.where((place < 3) & (place != segment), MASKED, 0.0).astype(BF)


def attend_tiles(total, size):
    tail = total - LONG_IMG
    first = total - 2 * LANES
    return [(at, n, 0, LONG_KEYS, True, at) for at, n in pieces(LONG_IMG, size)] + [
        (LONG_IMG + at, n, first, 2 * LANES, False, at) for at, n in pieces(tail, size)
    ]


def get(ref, at, n):
    cols = pl.ds(at if isinstance(at, int) else pl.multiple_of(at, LANES), n)
    value = ref[:, cols] if len(ref.shape) == 2 else ref[:, :, :, :, :, cols]
    return value.reshape(-1, n)


def put(ref, value, at, n):
    cols = pl.ds(at if isinstance(at, int) else pl.multiple_of(at, LANES), n)
    if len(ref.shape) == 2:
        ref[:, cols] = value
    else:
        ref[:, :, :, :, :, cols] = value.reshape(ref.shape[:-1] + (n,))


def get_rows(ref, part, parts):
    if len(ref.shape) == 2:
        rows = ref.shape[0] // parts
        return ref[pl.ds(pl.multiple_of(part * rows, rows), rows)]
    each = ref.shape[0] // parts
    value = ref[pl.ds(part * each, each)]
    return value.reshape(-1, value.shape[-1])


def put_rows(ref, value, part, parts):
    if len(ref.shape) == 2:
        rows = ref.shape[0] // parts
        ref[pl.ds(pl.multiple_of(part * rows, rows), rows)] = value
    else:
        each = ref.shape[0] // parts
        ref[pl.ds(part * each, each)] = value.reshape((each,) + ref.shape[1:])


def of_block(ref, j, offset=0):
    return ref.at[:, pl.ds(pl.multiple_of(offset + j * LANES, LANES), LANES)]


def of_trio(ref, j, which):
    return ref.at[:, pl.ds(pl.multiple_of(j * TRIO + which * LANES, LANES), LANES)]


def forward_head(j, head, qkv, attended, inverse, e_long, e_tail, aug_q, aug_k, size=400):
    total, width = attended.shape
    q, k, v = (of_trio(qkv, j, i) for i in range(3))
    attended, inverse = of_block(attended, j), of_block(inverse, j)
    mine = lanes(1) // HEAD_DIM == head
    ka = jnp.where(mine, k[...], aug_k[...])
    va = jnp.where(mine, v[...], jnp.ones_like(aug_k[...]))
    at = j * HEADS_IN_BLOCK + head
    for row, rows, key, keys, is_long, place in attend_tiles(total, size):
        here = pl.ds(row, rows)
        scores = nt(jnp.where(mine, q[here], aug_q[here]), ka[key : key + keys])
        exps = jnp.exp2(scores - jnp.max(scores, axis=1, keepdims=True)).astype(BF)
        store = e_long if is_long else e_tail
        store[at, place : place + rows, :] = exps
        product = nn(exps, va[key : key + keys])
        inv = 1.0 / pltpu.roll(product, HEAD_DIM, 1)
        attended[here] = jnp.where(mine, (product * inv).astype(BF), attended[here])
        inverse[here] = jnp.where(mine, inv, inverse[here])


def backward_prepare(j, qkv, attended, inverse, d_att, scaled_b, aug_b, q_t, s_t, k_b):
    total, width = attended.shape
    for at, n in pieces(total, ROWS):
        here = pl.ds(at, n)
        scaled = of_block(d_att, j)[here].astype(F32) * of_block(inverse, j)[here]
        inner = scaled * of_block(attended, j)[here].astype(F32)
        from_group = lax.broadcasted_iota(jnp.int32, (LANES, LANES), 0) // HEAD_DIM
        to_group = lanes(LANES) // HEAD_DIM
        spread = jnp.where((from_group + 1) % HEADS_IN_BLOCK == to_group, 1.0, 0.0).astype(BF)
        high = inner.astype(BF)
        low = (inner - high.astype(F32)).astype(BF)
        sums = nn(high, spread) + nn(low, spread)
        sum_high = sums.astype(BF)
        sum_low = (sums - sum_high.astype(F32)).astype(BF)
        place = lanes(n) % HEAD_DIM
        zeros = jnp.zeros_like(sum_high)
        aug_b[here] = jnp.where(place == 0, -sum_high, jnp.where(place == 1, -sum_low, zeros))
        scaled = scaled.astype(BF)
        scaled_b[here] = scaled
        s_t[:, at : at + n] = scaled.T
        q_t[:, at : at + n] = of_trio(qkv, j, 0)[here].T
        k_b[here] = of_trio(qkv, j, 1)[here]


def backward_head(j, head, qkv, e_long, e_tail, scaled_b, aug_b, q_t, s_t, k_b, dk_t, dv_t, size=400):
    total = scaled_b.shape[0]
    dq, v = of_trio(qkv, j, 0), of_trio(qkv, j, 2)
    mine = lanes(1) // HEAD_DIM == head
    following = lanes(1) // HEAD_DIM == (head + 1) % HEADS_IN_BLOCK
    va = jnp.where(mine, v[...], jnp.ones_like(k_b[...]))
    at = j * HEADS_IN_BLOCK + head
    of_head = pl.ds(pl.multiple_of(head * HEAD_DIM, HEAD_DIM), HEAD_DIM)
    sums_of = {}
    for row, rows, key, keys, is_long, where in attend_tiles(total, size):
        here = pl.ds(row, rows)
        store = e_long if is_long else e_tail
        exps = store[at, where : where + rows, :]
        side = jnp.where(following, aug_b[here], jnp.zeros_like(aug_b[here]))
        left = jnp.where(mine, scaled_b[here], side)
        d_scores = (exps.astype(F32) * nt(left, va[key : key + keys])).astype(BF)
        dq_here = (nn(d_scores, k_b[key : key + keys]) * SCALE).astype(BF)
        dq[here] = jnp.where(mine, dq_here, dq[here])
        more_v = nn(s_t[of_head, row : row + rows], exps)
        more_k = nn(q_t[of_head, row : row + rows], d_scores)
        if is_long in sums_of:
            more_v, more_k = sums_of[is_long][0] + more_v, sums_of[is_long][1] + more_k
        sums_of[is_long] = (more_v, more_k)
    first = total - 2 * LANES
    both = LONG_KEYS - first
    for ref, which, factor in ((dv_t, 0, 1.0), (dk_t, 1, 1.0 / LOG2E)):
        long_part, tail_part = (sums_of[is_long][which] * factor for is_long in (True, False))
        ref[of_head, 0:first] = long_part[:, :first].astype(BF)
        ref[of_head, first:LONG_KEYS] = (long_part[:, first:] + tail_part[:, :both]).astype(BF)
        ref[of_head, LONG_KEYS:total] = tail_part[:, both:].astype(BF)


def all_forward(b, transfers):
    unrolled = 2

    def step(i, carried):
        for one in range(unrolled):
            at = i * unrolled + one
            forward_head(
                at // HEADS_IN_BLOCK, at % HEADS_IN_BLOCK, b.qkv, b.attended, b.inverse,
                b.e_long, b.e_tail, b.aug_q, b.aug_k,
            )
        transfers.after_forward(i)
        return carried

    lax.fori_loop(0, b.attended.shape[1] // HEAD_DIM // unrolled, step, 0)


def all_backward(b, transfers):
    total, width = b.attended.shape
    unrolled = 2
    keep = (b.scaled_b, b.aug_b, b.q_t, b.s_t, b.k_b)

    def block(j, carried):
        backward_prepare(j, b.qkv, b.attended, b.inverse, b.d_exp, *keep)

        def step(i, inside):
            for one in range(unrolled):
                backward_head(
                    j, i * unrolled + one, b.qkv, b.e_long, b.e_tail, *keep, b.dk_t, b.dv_t
                )
            return inside

        lax.fori_loop(0, HEADS_IN_BLOCK // unrolled, step, 0)
        of_trio(b.qkv, j, 1)[...] = b.dk_t[...].T
        of_trio(b.qkv, j, 2)[...] = b.dv_t[...].T
        here = pl.ds(pl.multiple_of(j * LANES, LANES), LANES)
        trio = pl.ds(pl.multiple_of(j * TRIO, LANES), TRIO)
        for row, which in ((Q_BIAS, 0), (V_BIAS, 2)):
            values = of_trio(b.qkv, j, which)[...].astype(F32)
            b.g_vec[row : row + 1, here] = jnp.sum(values, axis=0, keepdims=True)

        def rows_of(i, inside):
            rows = pl.ds(pl.multiple_of(i * ROWS, ROWS), ROWS)
            b.acc_b[rows] = b.acc_b[rows] + nt(b.qkv[rows, trio], get(b.w_qkv, j * TRIO, TRIO))
            return inside

        lax.fori_loop(0, total // ROWS, rows_of, 0)
        put(b.w_qkv, tn(b.x_in[...], b.qkv[:, trio]).astype(BF), j * TRIO, TRIO)
        transfers.after_backward(j)
        return carried

    lax.fori_loop(0, width // LANES, block, 0)


class Buffers(typing.NamedTuple):
    x_in: typing.Any
    cot: typing.Any
    xc: typing.Any
    qkv: typing.Any
    attended: typing.Any
    inverse: typing.Any
    e_long: typing.Any
    e_tail: typing.Any
    aug_q: typing.Any
    aug_k: typing.Any
    middle: typing.Any
    acc_a: typing.Any
    acc_b: typing.Any
    hb: typing.Any
    act: typing.Any
    d_exp: typing.Any
    scaled_b: typing.Any
    aug_b: typing.Any
    q_t: typing.Any
    s_t: typing.Any
    k_b: typing.Any
    dk_t: typing.Any
    dv_t: typing.Any
    vec: typing.Any
    g_vec: typing.Any
    w_qkv: typing.Any
    w_proj: typing.Any
    w_expand: typing.Any
    w_reduce: typing.Any


def buffers(total, width, weights):
    heads = width // HEAD_DIM
    rows, lane, turned = (total, width), (total, LANES), (LANES, total)
    shapes = Buffers(
        x_in=(rows, BF),
        cot=(rows, BF),
        xc=(rows, BF),
        qkv=((total, 3 * width), BF),
        attended=(rows, BF),
        inverse=(rows, F32),
        e_long=((heads, LONG_IMG, LONG_KEYS), BF),
        e_tail=((heads, total - LONG_IMG, 2 * LANES), BF),
        aug_q=(lane, BF),
        aug_k=(lane, BF),
        middle=(rows, F32),
        acc_a=(rows, F32),
        acc_b=(rows, F32),
        hb=(rows, BF),
        act=(rows, BF),
        d_exp=(rows, BF),
        scaled_b=(lane, BF),
        aug_b=(lane, BF),
        q_t=(turned, BF),
        s_t=(turned, BF),
        k_b=(lane, BF),
        dk_t=(turned, BF),
        dv_t=(turned, BF),
        vec=((VEC_ROWS, width), F32),
        g_vec=((VEC_ROWS, width), F32),
        w_qkv=(weights[QKV], BF),
        w_proj=(weights[PROJ], BF),
        w_expand=(weights[EXPAND], BF),
        w_reduce=(weights[REDUCE], BF),
    )
    return [pltpu.VMEM(*one) for one in shapes]


def compute(b, first_length, transfers):
    total, width = b.xc.shape
    ff = b.w_expand.shape[-1]
    swapped = jnp.full((1, width), first_length, jnp.int32) == SHORT_IMG
    acc_a, acc_b, vec, g_vec = b.acc_a, b.acc_b, b.vec, b.g_vec

    def by_rows(function):
        def step(i, carried):
            function(pl.ds(pl.multiple_of(i * ROWS, ROWS), ROWS))
            return carried

        lax.fori_loop(0, total // ROWS, step, 0)

    def vector(row):
        return vec[pl.ds(row, 1), :]

    def add_sum(row, values):
        g_vec[pl.ds(row, 1), :] = g_vec[pl.ds(row, 1), :] + jnp.sum(values, axis=0, keepdims=True)

    def load(source):
        @by_rows
        def _(rows):
            acc_a[rows] = source[rows].astype(F32)

        to_canonical(swapped, acc_a, acc_b)

    def loaded(rows):
        return jnp.where(swapped, acc_b[rows], acc_a[rows])

    def unload(values, moved, target):
        to_natural(values, moved)

        @by_rows
        def _(rows):
            target[rows] = jnp.where(swapped, moved[rows], values[rows]).astype(BF)

    transfers.begin()
    g_vec[...] = jnp.zeros_like(g_vec)
    fill_masks(b.aug_q, b.aug_k)
    transfers.need_tokens()
    load(b.x_in)

    @by_rows
    def _(rows):
        values = loaded(rows)
        b.xc[rows] = values.astype(BF)
        acc_a[rows], _ = norm_parts(values)

    transfers.need_qkv()
    ha, qkv, w_qkv = b.x_in, b.qkv, b.w_qkv

    @by_rows
    def _(rows):
        lowered = (acc_a[rows] * vector(A_GAIN) + vector(A_SHIFT)).astype(BF)
        ha[rows] = lowered
        projected = nn(lowered, get(w_qkv, 0, 3 * width))
        for j in range(width // LANES):
            here = slice(j * LANES, (j + 1) * LANES)
            q, k, v = (projected[:, j * TRIO + i * LANES : j * TRIO + (i + 1) * LANES] for i in range(3))
            q = (q + vec[Q_BIAS : Q_BIAS + 1, here]) * (SCALE * LOG2E)
            v = v + vec[V_BIAS : V_BIAS + 1, here]
            for i, value in enumerate((q, k, v)):
                qkv[rows, j * TRIO + i * LANES : j * TRIO + (i + 1) * LANES] = value.astype(BF)

    transfers.forward()
    all_forward(b, transfers)

    transfers.need_cotangent()
    cot, middle, hb, act, d_exp, attended = b.cot, b.middle, b.hb, b.act, b.d_exp, b.attended
    w_proj, w_expand, w_reduce = b.w_proj, b.w_expand, b.w_reduce
    load(cot)

    @by_rows
    def _(rows):
        cot[rows] = loaded(rows).astype(BF)

    transfers.need_proj()

    @by_rows
    def _(rows):
        mid = b.xc[rows].astype(F32) + (nn(attended[rows], get(w_proj, 0, width)) + vector(P_BIAS))
        middle[rows] = mid
        normed, _ = norm_parts(mid)
        hb[rows] = (normed * vector(M_GAIN) + vector(M_SHIFT)).astype(BF)
        acc_a[rows] = mid + vector(R_BIAS)
        acc_b[rows] = jnp.zeros_like(mid)
        add_sum(R_BIAS, cot[rows].astype(F32))

    transfers.need_mlp()
    parts = ff // width

    def one_part(part, carried):
        for at, n in pieces(total, ROWS):
            rows = slice(at, at + n)
            w_in, w_out = get(w_expand, part * width, width), get_rows(w_reduce, part, parts)
            value, slope = gelu_parts(nn(hb[rows], w_in) + vector(E_BIAS + part))
            low = value.astype(BF)
            act[rows] = low
            acc_a[rows] = acc_a[rows] + nn(low, w_out)
            d_low = (nt(cot[rows], w_out) * slope).astype(BF)
            d_exp[rows] = d_low
            acc_b[rows] = acc_b[rows] + nt(d_low, w_in)
            add_sum(E_BIAS + part, d_low.astype(F32))
        put_rows(w_reduce, tn(act[...], cot[...]).astype(BF), part, parts)
        put(w_expand, tn(hb[...], d_exp[...]).astype(BF), part * width, width)
        transfers.after_part(part)
        return carried

    lax.fori_loop(0, parts, one_part, 0)

    d_att = d_exp

    @by_rows
    def _(rows):
        gradient = acc_b[rows]
        normed, inv = norm_parts(middle[rows])
        d_mid = cot[rows].astype(F32) + norm_back(gradient, normed, inv, vector(M_GAIN))
        add_sum(M_GAIN, gradient * normed)
        add_sum(M_SHIFT, gradient)
        middle[rows] = d_mid
        d_branch = d_mid.astype(BF)
        act[rows] = d_branch
        add_sum(P_BIAS, d_branch.astype(F32))
        d_att[rows] = nt(d_branch, get(w_proj, 0, width)).astype(BF)

    put(w_proj, tn(attended[...], act[...]).astype(BF), 0, width)
    transfers.have_proj()
    unload(acc_a, acc_b, hb)
    transfers.have_result()
    acc_b[...] = jnp.zeros_like(acc_b)
    all_backward(b, transfers)

    @by_rows
    def _(rows):
        gradient = acc_b[rows]
        normed, inv = norm_parts(b.xc[rows].astype(F32))
        add_sum(A_GAIN, gradient * normed)
        add_sum(A_SHIFT, gradient)
        acc_a[rows] = middle[rows] + norm_back(gradient, normed, inv, vector(A_GAIN))

    transfers.have_vectors()
    unload(acc_a, acc_b, act)
    transfers.have_grad()


class Local:
    def __init__(self, b, ins, outs, sems):
        self.b, self.outs = b, outs
        targets = (b.x_in, b.cot) + tuple(b[-4:])
        self.loads = [pltpu.make_async_copy(one, target, sems.at[i]) for i, (one, target) in enumerate(zip(ins, targets))]
        sources = (b.hb, b.act) + tuple(b[-4:])
        self.stores = [pltpu.make_async_copy(one, out, sems.at[6 + i]) for i, (one, out) in enumerate(zip(sources, outs))]

    def begin(self):
        for copy in self.loads:
            copy.start()

    def need_tokens(self):
        self.loads[0].wait()

    def need_qkv(self):
        self.loads[2 + QKV].wait()

    def forward(self):
        pass

    def after_forward(self, i):
        pass

    def need_cotangent(self):
        self.loads[1].wait()

    def need_proj(self):
        self.loads[2 + PROJ].wait()

    def need_mlp(self):
        self.loads[2 + EXPAND].wait()
        self.loads[2 + REDUCE].wait()

    def after_part(self, part):
        pass

    def have_proj(self):
        for which in (PROJ, EXPAND, REDUCE):
            self.stores[2 + which].start()

    def have_result(self):
        self.stores[0].start()

    def after_backward(self, j):
        pass

    def have_vectors(self):
        self.stores[2 + QKV].start()

    def have_grad(self):
        self.stores[1].start()
        for copy in self.stores:
            copy.wait()


def local_kernel(lengths, vec, x_in, cot_in, w_qkv, w_proj, w_expand, w_reduce,
                 result, grad_x, g_qkv, g_proj, g_expand, g_reduce, g_vec, *scratch):
    b = Buffers(*scratch[:-1])
    b.vec[...] = vec[...]
    ins = (x_in, cot_in, w_qkv, w_proj, w_expand, w_reduce)
    outs = (result, grad_x, g_qkv, g_proj, g_expand, g_reduce)
    compute(b, lengths[lax.axis_index("blk"), 0, 0], Local(b, ins, outs, scratch[-1]))
    g_vec[...] = b.g_vec[...]


def run_local(lengths, vec, x_in, cot_in, weights):
    vmem, anywhere = pl.BlockSpec(memory_space=pltpu.VMEM), pl.BlockSpec(memory_space=pl.ANY)
    total, width = x_in.shape
    like = (x_in, x_in) + tuple(weights)
    return pl.pallas_call(
        local_kernel,
        out_shape=[jax.ShapeDtypeStruct(one.shape, BF) for one in like]
        + [jax.ShapeDtypeStruct((VEC_ROWS, width), F32)],
        in_specs=[pl.BlockSpec(memory_space=pltpu.SMEM), vmem] + [anywhere] * 6,
        out_specs=[anywhere] * 6 + [vmem],
        scratch_shapes=buffers(total, width, [one.shape for one in weights]) + [pltpu.SemaphoreType.DMA((12,))],
        compiler_params=pltpu.CompilerParams(vmem_limit_bytes=62 * 2**20),
    )(lengths, vec, x_in, cot_in, *weights)


UNITS = (
    (QKV, 0, 2 * TRIO), (QKV, 2 * TRIO, 2 * TRIO + LANES), (PROJ, 0, 6 * LANES),
    (EXPAND, 0, 8 * LANES), (EXPAND, 8 * LANES, 8 * LANES), (REDUCE, 0, 2 * LANES), (REDUCE, 2 * LANES, 2 * LANES),
)
EARLY_UNITS, PROJ_UNITS, EXPAND_UNITS, REDUCE_UNITS = (0, 1), (2,), (3, 4), (5, 6)
VECTOR_TILES = ((QKV, 4 * TRIO), (PROJ, 4 * LANES), (PROJ, 5 * LANES))


class Group:
    def __init__(self, b, ins, outs, scratch):
        self.b = b
        self.tokens, self.cotangent, self.vectors, self.shards = ins
        self.result, self.grad_x, self.outs, self.g_total = outs
        (self.own_qkv, self.own_vec, self.packed, self.turn, self.arrived, self.v_two, self.v_z,
         self.local_sem, self.token_sem, self.ag_sem, self.rs_sem, self.v_sem) = scratch
        self.weights = tuple(b[-4:])
        dp, blk = lax.axis_index("dp"), lax.axis_index("blk")
        z, y, x, c = dp // SPREAD[Y], dp % SPREAD[Y], blk // SPREAD[C], blk % SPREAD[C]
        self.mine = (z, y, x, c)
        self.index = dp * (SPREAD[X] * SPREAD[C]) + blk
        self.blk = blk
        n_blk = SPREAD[X] * SPREAD[C]
        self.others = [(dp, (blk + k) % n_blk) for k in range(1, n_blk)]
        z_places = [(z + k) % SPREAD[Z] for k in range(1, SPREAD[Z])]
        self.along = (
            [((place * SPREAD[Y] + y, blk), place) for place in z_places],
            [((dp + 1 - 2 * y, blk), 1 - y)],
            [((dp, blk + SPREAD[C] * (1 - 2 * x)), 1 - x)],
            [((dp, blk + 1 - 2 * c), 1 - c)],
        )
        height = self.tokens.shape[1]

        def rows(ref):
            return lambda i: ref.at[pl.ds(pl.multiple_of(i * height, height), height)]

        def part(ref):
            return lambda i: ref.at[i]

        moves = (
            (part(self.tokens), rows(b.x_in)),
            (part(self.cotangent), rows(b.cot)),
            (rows(b.hb), part(self.result)),
            (rows(b.act), part(self.grad_x)),
        )
        self.swaps = [
            [
                self.remote(source(device[1]), target(blk), self.token_sem.at[i, k], self.token_sem.at[4 + i, k], device)
                for k, device in enumerate(self.others)
            ]
            for i, (source, target) in enumerate(moves)
        ]
        self.kept = [
            pltpu.make_async_copy(source(blk), target(blk), self.local_sem.at[i])
            for i, (source, target) in enumerate(moves)
        ]

    @staticmethod
    def remote(source, target, send, recv, device):
        return pltpu.make_async_remote_copy(
            src_ref=source, dst_ref=target, send_sem=send, recv_sem=recv,
            device_id=device, device_id_type=pl.DeviceIdType.MESH,
        )

    @staticmethod
    def start(copies):
        for copy in copies:
            copy.start()

    @staticmethod
    def arrive(copies):
        for copy in copies:
            copy.wait_recv()

    @staticmethod
    def sent(copies):
        for copy in copies:
            copy.wait_send()

    def place(self, free, at=None):
        index = [slice(None) if axis in free else self.mine[axis] for axis in range(4)]
        for axis, value in (at or {}).items():
            index[axis] = value
        return tuple(index)


    def gather(self, unit, stage):
        which, first, columns = UNITS[unit]
        w, order = self.weights[which], GATHER_ORDER[which]
        cols = (slice(None), pl.ds(first, columns))

        def one(i, view, device):
            return self.remote(view, view, self.ag_sem.at[0, unit, i], self.ag_sem.at[1, unit, i], device)

        if stage < 3:
            view = w.at[self.place(order[:stage]) + cols]
            return [one(3 * stage + k, view, device) for k, (device, _) in enumerate(self.along[order[stage]])]
        device, _ = self.along[C][0]
        last = order[2]
        if stage == 3:
            return [one(9, w.at[self.place(order[:2]) + cols], device)]
        (_, other), = self.along[last]
        return [one(10, w.at[self.place(order[:2], {last: other}) + cols], device)]

    def gather_on(self, units, stage):
        for unit in units:
            copies = self.gather(unit, stage)
            self.arrive(copies)
            self.sent(copies)
            if stage < 2:
                self.start(self.gather(unit, stage + 1))
            if stage in (1, 2):
                self.start(self.gather(unit, stage + 2))

    def gathered(self, units):
        for unit in units:
            for stage in (3, 4):
                copies = self.gather(unit, stage)
                self.arrive(copies)
                self.sent(copies)

    def unpack(self, tile):
        which, first = VECTOR_TILES[tile]
        w = self.weights[which]
        all_of = w[:, :, :, :, 0:PACKED, first : first + LANES].astype(F32)
        total = jnp.sum(all_of.reshape(-1, PACKED, LANES), axis=0)
        for i in range(PACKED):
            row, at = divmod(tile * PACKED + i, 4)
            self.b.vec[row : row + 1, at * LANES : (at + 1) * LANES] = total[i : i + 1, :]


    def chunk_view(self, which, chunk):
        if which == REDUCE:
            return chunk, slice(None)
        columns = (TRIO, 4 * LANES, 4 * LANES)[which]
        return None, pl.ds(pl.multiple_of(chunk * columns, LANES), columns)

    def scatter(self, which, stage, chunk):
        w, order = self.weights[which], SCATTER_ORDER[which]
        axis, rest = order[stage], order[stage + 1 :]
        buffer = self.arrived[which][stage]
        at_z, cols = self.chunk_view(which, chunk)
        copies = []
        for k, (device, other) in enumerate(self.along[axis]):
            at = {axis: other}
            if at_z is not None and Z in rest:
                at[Z] = at_z
            source = w.at[self.place(rest, at) + (slice(None), cols)]
            sems = (self.rs_sem.at[i, which, chunk, 3 * stage + k] for i in range(2))
            copies.append(self.remote(source, buffer.at[self.landing(axis, rest, at_z, cols, k)], *sems, device))
        return copies

    @staticmethod
    def landing(axis, rest, at_z, cols, k):
        lead = (k,) if axis == Z else ()
        free = tuple(at_z if one == Z and at_z is not None else slice(None) for one in sorted(rest))
        return lead + free + (slice(None), cols)

    def scatter_on(self, which, stage, chunk):
        w, order = self.weights[which], SCATTER_ORDER[which]
        copies = self.scatter(which, stage, chunk)
        self.arrive(copies)
        axis, rest = order[stage], order[stage + 1 :]
        buffer = self.arrived[which][stage]
        at_z, cols = self.chunk_view(which, chunk)
        at = {Z: at_z} if at_z is not None and Z in rest else None
        here = self.place(rest, at) + (slice(None), cols)
        terms = [buffer[self.landing(axis, rest, at_z, cols, k)] for k in range(len(copies))]
        if not rest:
            total = w[here].astype(F32)
            for term in terms:
                total = total + term.astype(F32)
            self.keep(which, chunk, total)
        elif len(terms) == 1:
            w[here] = w[here] + terms[0]
        else:
            total = w[here].astype(F32)
            for term in terms:
                total = total + term.astype(F32)
            w[here] = total.astype(BF)
        if rest and not (which == REDUCE and rest == (Z,)):
            self.start(self.scatter(which, stage + 1, chunk))
        self.sent(copies)

    def keep(self, which, chunk, total):
        out = self.outs[which]
        if which == QKV:
            width = out.shape[1] // 3
            for i in range(3):
                cols = pl.ds(pl.multiple_of(i * width + chunk * LANES, LANES), LANES)
                out[:, cols] = total[:, i * LANES : (i + 1) * LANES]
        else:
            _, cols = self.chunk_view(which, chunk)
            out[:, cols] = total

    def tick(self, which, t, stages):
        if isinstance(t, int):
            if t < CHUNKS:
                self.start(self.scatter(which, 0, t))
            for stage in range(stages):
                if 0 <= t - stage - 1 < CHUNKS:
                    self.scatter_on(which, stage, t - stage - 1)
            return
        self.start(self.scatter(which, 0, t))
        for stage in range(min(stages, CHUNKS - 1)):
            pl.when(t >= stage + 1)(lambda stage=stage: self.scatter_on(which, stage, t - stage - 1))


    def vector_copies(self, stage):
        axis = (C, Y, X, Z)[stage]
        return [
            self.remote(
                self.b.g_vec, self.v_z.at[k] if axis == Z else self.v_two.at[stage],
                self.v_sem.at[0, 3 * stage + k], self.v_sem.at[1, 3 * stage + k], device,
            )
            for k, (device, _) in enumerate(self.along[axis])
        ]

    def vectors_on(self, stage):
        copies = self.vector_copies(stage)
        self.arrive(copies)
        self.sent(copies)
        g_vec = self.b.g_vec
        if stage < 3:
            g_vec[...] = g_vec[...] + self.v_two[stage]
            self.start(self.vector_copies(stage + 1))
        else:
            self.g_total[...] = g_vec[...] + jnp.sum(self.v_z[...], axis=0)


    def begin(self):
        barrier = pltpu.get_barrier_semaphore()
        peers = self.others + [device for axis in (Y, Z) for device, _ in self.along[axis]]
        for device in peers:
            pl.semaphore_signal(barrier, inc=1, device_id=device, device_id_type=pl.DeviceIdType.MESH)
        count = len(self.vectors)
        loads = [
            pltpu.make_async_copy(one, target, self.local_sem.at[4 + i])
            for i, (one, target) in enumerate(zip(self.vectors, self.own_vec))
        ]
        loads.append(pltpu.make_async_copy(self.shards[QKV], self.own_qkv, self.local_sem.at[4 + count]))
        width = self.shards[PROJ].shape[1]
        slots = [self.weights[which].at[self.mine] for which in range(4)]
        self.own = [
            pltpu.make_async_copy(
                self.shards[which], slots[which].at[:, pl.ds(0, self.shards[which].shape[1])],
                self.local_sem.at[4 + count + which],
            )
            for which in (PROJ, EXPAND, REDUCE)
        ]
        self.start(loads + self.own + self.kept[:2])
        self.packed[...] = jnp.zeros_like(self.packed)
        row = 0
        for load, own in zip(loads, self.own_vec):
            load.wait()
            size = own.shape[0]
            self.turn[...] = jnp.zeros_like(self.turn)
            self.turn[0:1, 0:size] = own[...].astype(F32).reshape(1, size)
            at = self.index * size
            self.packed[pl.ds(row + at // LANES, 1), :] = pltpu.roll(self.turn[...], at % LANES, 1)[0:1, :]
            row += math.prod(SPREAD) * size // LANES
        loads[-1].wait()
        w = self.weights[QKV]
        for j in range(width // LANES):
            for i in range(3):
                to = j * TRIO + i * LANES
                w[self.mine + (slice(None), pl.ds(to, LANES))] = self.own_qkv[:, i * width + j * LANES : i * width + (j + 1) * LANES]
        for tile, (which, first) in enumerate(VECTOR_TILES):
            values = self.packed[tile * PACKED : (tile + 1) * PACKED, :].astype(BF)
            self.weights[which][self.mine + (slice(None), pl.ds(first, LANES))] = values
        pl.semaphore_wait(barrier, len(peers))
        for unit in EARLY_UNITS:
            self.start(self.gather(unit, 0))
        self.start(self.swaps[0])
        for copy in self.own:
            copy.wait()

    def need_tokens(self):
        self.gather_on(EARLY_UNITS, 0)
        for unit in PROJ_UNITS + EXPAND_UNITS:
            self.start(self.gather(unit, 0))
        self.gather_on(EARLY_UNITS, 1)
        for unit in REDUCE_UNITS:
            self.start(self.gather(unit, 0))
        self.gather_on(PROJ_UNITS + EXPAND_UNITS, 0)
        self.kept[0].wait()
        self.arrive(self.swaps[0])
        self.sent(self.swaps[0])
        self.start(self.swaps[1])

    def need_qkv(self):
        self.gather_on(EARLY_UNITS, 2)
        self.gathered(EARLY_UNITS)
        self.unpack(0)

    def forward(self):
        pass

    def after_forward(self, i):
        steps = {
            0: lambda: self.gather_on(REDUCE_UNITS, 0),
            1: lambda: self.gather_on(PROJ_UNITS, 1),
            2: lambda: self.gather_on(REDUCE_UNITS, 1),
            3: lambda: (self.gather_on(EXPAND_UNITS[:1], 1), self.gather_on(PROJ_UNITS, 2)),
            4: lambda: self.gather_on(EXPAND_UNITS[1:], 1),
            5: lambda: self.gather_on(REDUCE_UNITS, 2),
            6: lambda: self.gather_on(EXPAND_UNITS[:1], 2),
            7: lambda: self.gather_on(EXPAND_UNITS[1:], 2),
        }
        for at, step in steps.items():
            pl.when(i == at)(lambda step=step: [step(), None][1])

    def need_cotangent(self):
        self.kept[1].wait()
        self.arrive(self.swaps[1])
        self.sent(self.swaps[1])

    def need_proj(self):
        self.gathered(PROJ_UNITS)
        self.unpack(1)
        self.unpack(2)

    def need_mlp(self):
        self.gathered(EXPAND_UNITS + REDUCE_UNITS)

    def after_part(self, part):
        self.tick(REDUCE, part, 3)
        self.tick(EXPAND, part, 4)

    def have_proj(self):
        self.start(self.scatter(PROJ, 0, 0))
        self.tick(REDUCE, CHUNKS, 3)
        self.tick(EXPAND, CHUNKS, 4)

    def have_result(self):
        self.start(self.swaps[2] + self.kept[2:3])

    def after_backward(self, j):
        self.tick(QKV, j, 4)

        def step(at):
            self.scatter_on(PROJ, at, 0)
            t = CHUNKS + 1 + at
            if t < CHUNKS + 3:
                self.tick(REDUCE, t, 3)
            elif t == CHUNKS + 3:
                self.start(self.scatter(REDUCE, 3, 0))
            else:
                self.scatter_on(REDUCE, 3, 0)
            if t < CHUNKS + 4:
                self.tick(EXPAND, t, 4)

        for at in range(CHUNKS):
            pl.when(j == at)(lambda at=at: step(at))

    def have_vectors(self):
        self.start(self.vector_copies(0))
        self.tick(QKV, CHUNKS, 4)

    def have_grad(self):
        self.start(self.swaps[3] + self.kept[3:4])
        for stage in range(3):
            self.vectors_on(stage)
            self.tick(QKV, CHUNKS + 1 + stage, 4)
        self.vectors_on(3)
        for i in (2, 3):
            self.kept[i].wait()
            self.arrive(self.swaps[i])
            self.sent(self.swaps[i])


N_VECTORS = 8


def group_kernel(*refs):
    refs = list(refs)

    def take(n):
        taken = refs[:n]
        del refs[:n]
        return taken

    (lengths,), vectors, (tokens, cotangent), shards = take(1), take(N_VECTORS), take(2), take(4)
    (result, grad_x), outs, (g_total,) = take(2), take(4), take(1)
    b = Buffers(*take(len(Buffers._fields)))
    (own_qkv,), own_vec, (packed, turn) = take(1), take(N_VECTORS), take(2)
    arrived = [take(4) for _ in range(4)]
    scratch = [own_qkv, own_vec, packed, turn, arrived] + refs
    group = Group(b, (tokens, cotangent, vectors, shards), (result, grad_x, outs, g_total), scratch)
    compute(b, lengths[lax.axis_index("blk"), 0, 0], group)


def run_group(lengths, vectors, tokens, cotangent, weights):
    vmem, anywhere = pl.BlockSpec(memory_space=pltpu.VMEM), pl.BlockSpec(memory_space=pl.ANY)
    blk, height, width = tokens.shape
    extra = [0] * 4
    for which, _ in VECTOR_TILES:
        extra[which] += LANES
    shapes = [SPREAD + (one.shape[0], one.shape[1] + more) for one, more in zip(weights, extra)]
    landing = []
    for which, shape in enumerate(shapes):
        for stage, axis in enumerate(SCATTER_ORDER[which]):
            rest = sorted(SCATTER_ORDER[which][stage + 1 :])
            lead = (SPREAD[Z] - 1,) if axis == Z else ()
            landing.append(pltpu.VMEM(lead + tuple(SPREAD[one] for one in rest) + weights[which].shape, BF))
    sums = (VEC_ROWS, width)
    packed_rows = math.prod(SPREAD) * sum(one.shape[0] for one in vectors) // LANES
    dma = pltpu.SemaphoreType.DMA
    return pl.pallas_call(
        group_kernel,
        out_shape=[jax.ShapeDtypeStruct(tokens.shape, BF)] * 2
        + [jax.ShapeDtypeStruct(one.shape, F32) for one in weights]
        + [jax.ShapeDtypeStruct(sums, F32)],
        in_specs=[pl.BlockSpec(memory_space=pltpu.SMEM)] + [anywhere] * (N_VECTORS + 6),
        out_specs=[anywhere] * 2 + [vmem] * 5,
        scratch_shapes=buffers(blk * height, width, shapes)
        + [pltpu.VMEM(weights[QKV].shape, BF)]
        + [pltpu.VMEM(one.shape, BF) for one in vectors]
        + [pltpu.VMEM((packed_rows, LANES), F32), pltpu.VMEM((8, LANES), F32)]
        + landing
        + [pltpu.VMEM((3,) + sums, F32), pltpu.VMEM((SPREAD[Z] - 1,) + sums, F32)]
        + [dma((16,)), dma((8, 3)), dma((2, len(UNITS), 11)), dma((2, 4, CHUNKS, 12)), dma((2, 12))],
        compiler_params=pltpu.CompilerParams(
            vmem_limit_bytes=62 * 2**20, collective_id=0, has_side_effects=True
        ),
    )(lengths, *vectors, tokens, cotangent, *weights)


def finish_kernel(result, grad_x, g_qkv, g_proj, g_expand, g_reduce, g_vec, *refs):
    sources = (result, grad_x, g_qkv, g_proj, g_expand, g_reduce)
    outs, refs = refs[: 6 + N_VECTORS], refs[6 + N_VECTORS :]
    held, short = refs[:6], refs[6 : 6 + N_VECTORS]
    turn, lines, sems = refs[6 + N_VECTORS :]
    loads = [pltpu.make_async_copy(one, to, sems.at[i]) for i, (one, to) in enumerate(zip(sources, held))]
    stores = [pltpu.make_async_copy(one, to, sems.at[6 + i]) for i, (one, to) in enumerate(zip(held, outs))]
    for load in loads:
        load.start()
    index = lax.axis_index("dp") * lax.axis_size("blk") + lax.axis_index("blk")
    devices = lax.axis_size("dp") * lax.axis_size("blk")
    width = g_vec.shape[1]
    parts = width // LANES
    for i in range(g_vec.shape[0]):
        for part in range(parts):
            lines[i * parts + part : i * parts + part + 1, :] = g_vec[i : i + 1, part * LANES : (part + 1) * LANES]
    row = 0
    for i, one in enumerate(short):
        size = one.shape[0]
        at = index * size
        turn[0:1, :] = lines[pl.ds(row + at // LANES, 1), :]
        turned = pltpu.roll(turn[...], (LANES - at % LANES) % LANES, 1)
        one[...] = turned[0:1, 0:size].reshape(size)
        stores.append(pltpu.make_async_copy(one, outs[6 + i], sems.at[12 + i]))
        stores[-1].start()
        row += devices * size // LANES
    for load, store in zip(loads, stores):
        load.wait()
        store.start()
    for store in stores:
        store.wait()


def finish(values, sizes):
    vmem, anywhere = pl.BlockSpec(memory_space=pltpu.VMEM), pl.BlockSpec(memory_space=pl.ANY)
    long = [(one.shape, one.dtype) for one in values[:6]]
    short = [((size,), F32) for size in sizes]
    return pl.pallas_call(
        finish_kernel,
        out_shape=[jax.ShapeDtypeStruct(*one) for one in long + short],
        in_specs=[anywhere] * 6 + [vmem],
        out_specs=[anywhere] * (6 + len(sizes)),
        scratch_shapes=[pltpu.VMEM(*one) for one in long + short]
        + [pltpu.VMEM((8, LANES), F32), pltpu.VMEM((values[6].size // LANES, LANES), F32)]
        + [pltpu.SemaphoreType.DMA((12 + len(sizes),))],
    )(*values)


def by_collectives(lengths, vectors, sizes, tokens, cotangent, weights):
    axes = ("dp", "blk")
    width = tokens.shape[2]
    blocks = width // LANES

    def exchange(rows):
        return lax.all_to_all(rows.reshape(tokens.shape), "blk", 0, 0, tiled=True)

    packed = lax.all_gather(jnp.concatenate(vectors), axes, axis=0)
    starts = [sum(sizes[:i]) for i in range(len(sizes))]
    full = [packed[:, at : at + size].reshape(-1, width) for at, size in zip(starts, sizes)]
    vec = jnp.concatenate(full, axis=0).astype(F32)
    vec = jnp.pad(vec, ((0, VEC_ROWS - vec.shape[0]), (0, 0)))
    whole = [lax.all_gather(one, axes, axis=0, tiled=True) for one in weights]
    whole[QKV] = whole[QKV].reshape(width, 3, blocks, LANES).swapaxes(1, 2).reshape(width, 3 * width)
    result, grad_x, *grads, g_vec = run_local(
        lengths, vec, exchange(tokens).reshape(-1, width), exchange(cotangent).reshape(-1, width), whole
    )
    grads[QKV] = grads[QKV].reshape(width, blocks, 3, LANES).swapaxes(1, 2).reshape(width, 3 * width)
    grads = [lax.psum_scatter(one.astype(F32), axes, scatter_dimension=0, tiled=True) for one in grads]
    g_vec = lax.psum(g_vec, axes).reshape(-1)
    index = lax.axis_index(axes)
    devices = lax.axis_size(axes)
    own = [
        lax.dynamic_slice(g_vec, (devices * at + index * size,), (size,)) for at, size in zip(starts, sizes)
    ]
    return (exchange(result), exchange(grad_x), *grads, *own)


def body(
    tokens, lengths, attn_gain, attn_shift, w_qkv, qv_bias, w_proj, proj_bias,
    mlp_gain, mlp_shift, w_expand, expand_bias, w_reduce, reduce_bias, cotangent,
):
    vectors = (attn_gain, attn_shift, qv_bias, proj_bias, mlp_gain, mlp_shift, reduce_bias, expand_bias)
    sizes = [one.shape[0] for one in vectors]
    weights = (w_qkv, w_proj, w_expand, w_reduce)
    sized = (lax.axis_size("dp"), lax.axis_size("blk")) == (SPREAD[Z] * SPREAD[Y], SPREAD[X] * SPREAD[C])
    if sized and all(one.shape[0] % 16 == 0 for one in weights):
        outs = finish(run_group(lengths, vectors, tokens, cotangent, weights), sizes)
    else:
        outs = by_collectives(lengths, vectors, sizes, tokens, cotangent, weights)
    result, grad_x, g_qkv, g_proj, g_expand, g_reduce, ag, as_, qv, pb, mg, ms, rb, eb = outs
    return (result, grad_x, ag, as_, g_qkv, qv, g_proj, pb, mg, ms, g_expand, eb, g_reduce, rb)


def solution(mesh):
    both = ("dp", "blk")
    rows = P(None, both, None)
    vector, matrix = P(both), P(both, None)
    weights = (
        vector, vector, matrix, vector, matrix, vector, vector, vector, matrix, vector, matrix, vector,
    )
    return jax.shard_map(
        body,
        mesh=mesh,
        in_specs=(rows, P(None, "dp", None)) + weights + (rows,),
        out_specs=(rows, rows) + weights,
        check_vma=False,
    )
```

time: 816 us -> 161 us (0.20)
  waiting for transfers between devices: 496 us -> 0 us
  blocking collectives: 182 us -> 0 us
  Pallas kernels: 88 us -> 159 us
  between operations: 14.6 us -> 0.81 us
  other arithmetic: 10.1 us -> 0 us
  local copies, waits for them, and re-layouts: 10.2 us -> 1.34 us
    reduce_scatter x4 -> x0, waiting for transfers between devices: 438 us -> none  [scatter(): lax.psum_scatter(whole.astype(F32), axes, scatter_dimension=0, tiled=True)]
    pallas_call x1 -> x2, Pallas kernels: 88 us -> 159 us  [the longest x1 155 us: run_group(): pl.pallas_call(group_kernel, out_shape=[jax.ShapeDtypeStruct(tokens.shape...]
    all_gather x3 -> x0, waiting for transfers between devices: 55.7 us -> none  [gather(): return lax.all_gather(shard, axes, axis=0, tiled=True)]
    unnamed x1 -> x0, blocking collectives: 51.1 us -> none
    psum x1 -> x0, blocking collectives: 48.3 us -> none  [body(): g_vec = lax.psum(g_vec, axes).reshape(-1)]
    all_gather x1 -> x0, blocking collectives: 44.2 us -> none  [gather(): return lax.all_gather(shard, axes, axis=0, tiled=True)]
    all_to_all x2 -> x0, blocking collectives: 38.2 us -> none  [exchange(): return lax.all_to_all(rows, 'blk', 0, 0, tiled=True)]
    convert_element_type x4 -> x0, other arithmetic: 9.47 us -> none  [scatter(): whole.astype(F32)]
  transfers between devices with their start and end apart: 9 -> 0, of which waited for: 5 -> 0; matrix products, arithmetic and copies ran while one was open for 1% -> 0% of each run, Pallas kernels for 0% -> 0%
where the time goes in v2:
time: 161 us
  Pallas kernels  159 us (99%)
    pallas_call x1, Pallas kernels, run_group(): pl.pallas_call(group_kernel, out_shape=[jax.ShapeDtypeStruct(tokens.shape...  155 us
    pallas_call x1, Pallas kernels, finish(): pl.pallas_call(finish_kernel, out_shape=[jax.ShapeDtypeStruct(*one) for o...  3.69 us

profile of v2, /device:TPU:0, one launch (start us, length us, event | category | flops | bytes accessed | tf_op | source)
XLA Modules:
  0.0 161.0 jit_solution(3833292875609174733)
XLA Ops:
  0.6 1.3 copy.29.refs_0_
  2.0 155.2 %shard_map.254 = (bf16[4,256,512]{2,1,0:T(8,128)(2,1)}, bf16[4,256,512]{2,1,0:T(8,128)(2,1)}, f32[16,1536]{1,0:T(8,128)}, f32[16,512]{1,0:T(8,128)}, f32[16,2048...) custom-call(s32[4,1,2]{2,1,0:T(1,128)} %copy.29.refs_0_, bf16[16]{0:T(256)(128)(2,1)} %refs_1_.1, ...), custom_call_target="tpu_custom_call" | custom-call | tf_op jit(solution)/shard_map/pallas_call | solution.py:989
  157.2 3.7 %shard_map.255 = (bf16[4,256,512]{2,1,0:T(8,128)(2,1)}, bf16[4,256,512]{2,1,0:T(8,128)(2,1)}, f32[16,1536]{1,0:T(8,128)}, f32[16,512]{1,0:T(8,128)}, f32[16,2048...) custom-call(bf16[4,256,512]{2,1,0:T(8,128)(2,1)} %get-tuple-element., ...), custom_call_target="tpu_custom_call" | custom-call | tf_op jit(solution)/shard_map/pallas_call | solution.py:1046

commit v3 on v2

--- a/solution.py
+++ b/solution.py
@@ -20,7 +20,7 @@
 LOG2E = math.log2(math.e)
 SCALE = 1.0 / math.sqrt(HEAD_DIM)
 MASKED = -1e30
-ROWS = 256
+ROWS = 512
 A_GAIN, A_SHIFT, Q_BIAS, V_BIAS, P_BIAS, M_GAIN, M_SHIFT, R_BIAS, E_BIAS = range(9)
 VEC_ROWS = 16
 PACKED = 16
@@ -33,6 +33,10 @@
 SCATTER_ORDER = tuple((C,) + order[::-1] for order in GATHER_ORDER)
 
 
+def copies_before(order, stage):
+    return sum(SPREAD[axis] - 1 for axis in order[:stage])
+
+
 def nt(left, right):
     return lax.dot_general(left, right, (((1,), (1,)), ((), ())), preferred_element_type=F32)
 
@@ -85,17 +89,9 @@
 
 
 def gelu_parts(values):
-    size = jnp.abs(values)
-    z = size * math.sqrt(0.5)
-    t = 1.0 / (1.0 + 0.5 * z)
-    poly = 0.17087277
-    for factor in (-0.82215223, 1.48851587, -1.13520398, 0.27886807, -0.18628806, 0.09678418,
-                   0.37409196, 1.00002368, -1.26551223):
-        poly = poly * t + factor
-    bell = jnp.exp(-z * z)
-    tail = 0.5 * t * bell * jnp.exp(poly)
-    phi = jnp.where(values >= 0.0, 1.0 - tail, tail)
-    return values * phi, phi + values * (bell * (1.0 / math.sqrt(2.0 * math.pi)))
+    phi = 0.5 + 0.5 * lax.erf(values * math.sqrt(0.5))
+    bell = jnp.exp2(values * values * (-0.5 * LOG2E) + math.log2(1.0 / math.sqrt(2.0 * math.pi)))
+    return values * phi, phi + values * bell
 
 
 def fill_masks(aug_q, aug_k):
@@ -271,13 +267,10 @@
             values = of_trio(b.qkv, j, which)[...].astype(F32)
             b.g_vec[row : row + 1, here] = jnp.sum(values, axis=0, keepdims=True)
 
-        def rows_of(i, inside):
-            rows = pl.ds(pl.multiple_of(i * ROWS, ROWS), ROWS)
-            b.acc_b[rows] = b.acc_b[rows] + nt(b.qkv[rows, trio], get(b.w_qkv, j * TRIO, TRIO))
-            return inside
-
-        lax.fori_loop(0, total // ROWS, rows_of, 0)
-        put(b.w_qkv, tn(b.x_in[...], b.qkv[:, trio]).astype(BF), j * TRIO, TRIO)
+        w_trio = get(b.w_qkv, j * TRIO, TRIO)
+        for at, n in pieces(total, ROWS):
+            b.acc_b[at : at + n] = b.acc_b[at : at + n] + nt(b.qkv[at : at + n, trio], w_trio)
+        put(b.w_qkv, nn(b.ha_t[...], b.qkv[:, trio]).astype(BF), j * TRIO, TRIO)
         transfers.after_backward(j)
         return carried
 
@@ -286,6 +279,7 @@
 
 class Buffers(typing.NamedTuple):
     x_in: typing.Any
+    ha_t: typing.Any
     cot: typing.Any
     xc: typing.Any
     qkv: typing.Any
@@ -321,6 +315,7 @@
     rows, lane, turned = (total, width), (total, LANES), (LANES, total)
     shapes = Buffers(
         x_in=(rows, BF),
+        ha_t=((width, total), BF),
         cot=(rows, BF),
         xc=(rows, BF),
         qkv=((total, 3 * width), BF),
@@ -353,10 +348,9 @@
     return [pltpu.VMEM(*one) for one in shapes]
 
 
-def compute(b, first_length, transfers):
+def compute(b, transfers):
     total, width = b.xc.shape
     ff = b.w_expand.shape[-1]
-    swapped = jnp.full((1, width), first_length, jnp.int32) == SHORT_IMG
     acc_a, acc_b, vec, g_vec = b.acc_a, b.acc_b, b.vec, b.g_vec
 
     def by_rows(function):
@@ -392,7 +386,9 @@
     transfers.begin()
     g_vec[...] = jnp.zeros_like(g_vec)
     fill_masks(b.aug_q, b.aug_k)
+    transfers.enter()
     transfers.need_tokens()
+    swapped = jnp.broadcast_to(transfers.first_length(), (1, width)) == SHORT_IMG
     load(b.x_in)
 
     @by_rows
@@ -402,16 +398,16 @@
         acc_a[rows], _ = norm_parts(values)
 
     transfers.need_qkv()
-    ha, qkv, w_qkv = b.x_in, b.qkv, b.w_qkv
-
-    @by_rows
-    def _(rows):
+    qkv, w_qkv = b.qkv, b.w_qkv
+
+    for at, n in pieces(total, ROWS):
+        rows = slice(at, at + n)
         lowered = (acc_a[rows] * vector(A_GAIN) + vector(A_SHIFT)).astype(BF)
-        ha[rows] = lowered
-        projected = nn(lowered, get(w_qkv, 0, 3 * width))
+        b.ha_t[:, rows] = lowered.T
         for j in range(width // LANES):
             here = slice(j * LANES, (j + 1) * LANES)
-            q, k, v = (projected[:, j * TRIO + i * LANES : j * TRIO + (i + 1) * LANES] for i in range(3))
+            projected = nn(lowered, get(w_qkv, j * TRIO, TRIO))
+            q, k, v = (projected[:, i * LANES : (i + 1) * LANES] for i in range(3))
             q = (q + vec[Q_BIAS : Q_BIAS + 1, here]) * (SCALE * LOG2E)
             v = v + vec[V_BIAS : V_BIAS + 1, here]
             for i, value in enumerate((q, k, v)):
@@ -445,17 +441,24 @@
     parts = ff // width
 
     def one_part(part, carried):
-        for at, n in pieces(total, ROWS):
-            rows = slice(at, at + n)
-            w_in, w_out = get(w_expand, part * width, width), get_rows(w_reduce, part, parts)
-            value, slope = gelu_parts(nn(hb[rows], w_in) + vector(E_BIAS + part))
-            low = value.astype(BF)
-            act[rows] = low
-            acc_a[rows] = acc_a[rows] + nn(low, w_out)
-            d_low = (nt(cot[rows], w_out) * slope).astype(BF)
-            d_exp[rows] = d_low
-            acc_b[rows] = acc_b[rows] + nt(d_low, w_in)
-            add_sum(E_BIAS + part, d_low.astype(F32))
+        w_in, w_out = get(w_expand, part * width, width), get_rows(w_reduce, part, parts)
+        tiles = pieces(total, ROWS // 2)
+        todo = []
+        for step in range(len(tiles) + 1):
+            if step < len(tiles):
+                at, n = tiles[step]
+                rows = slice(at, at + n)
+                todo.append((rows, nn(hb[rows], w_in) + vector(E_BIAS + part), nt(cot[rows], w_out)))
+            if step:
+                rows, expanded, d_act = todo.pop(0)
+                value, slope = gelu_parts(expanded)
+                low = value.astype(BF)
+                act[rows] = low
+                d_low = (d_act * slope).astype(BF)
+                d_exp[rows] = d_low
+                acc_a[rows] = acc_a[rows] + nn(low, w_out)
+                acc_b[rows] = acc_b[rows] + nt(d_low, w_in)
+                add_sum(E_BIAS + part, d_low.astype(F32))
         put_rows(w_reduce, tn(act[...], cot[...]).astype(BF), part, parts)
         put(w_expand, tn(hb[...], d_exp[...]).astype(BF), part * width, width)
         transfers.after_part(part)
@@ -493,14 +496,13 @@
         add_sum(A_SHIFT, gradient)
         acc_a[rows] = middle[rows] + norm_back(gradient, normed, inv, vector(A_GAIN))
 
-    transfers.have_vectors()
     unload(acc_a, acc_b, act)
     transfers.have_grad()
 
 
 class Local:
-    def __init__(self, b, ins, outs, sems):
-        self.b, self.outs = b, outs
+    def __init__(self, b, lengths, ins, outs, sems):
+        self.b, self.lengths, self.outs = b, lengths, outs
         targets = (b.x_in, b.cot) + tuple(b[-4:])
         self.loads = [pltpu.make_async_copy(one, target, sems.at[i]) for i, (one, target) in enumerate(zip(ins, targets))]
         sources = (b.hb, b.act) + tuple(b[-4:])
@@ -510,6 +512,12 @@
         for copy in self.loads:
             copy.start()
 
+    def enter(self):
+        pass
+
+    def first_length(self):
+        return jnp.full((1, 1), self.lengths[lax.axis_index("blk"), 0, 0], jnp.int32).astype(F32)
+
     def need_tokens(self):
         self.loads[0].wait()
 
@@ -545,10 +553,8 @@
     def after_backward(self, j):
         pass
 
-    def have_vectors(self):
+    def have_grad(self):
         self.stores[2 + QKV].start()
-
-    def have_grad(self):
         self.stores[1].start()
         for copy in self.stores:
             copy.wait()
@@ -560,7 +566,7 @@
     b.vec[...] = vec[...]
     ins = (x_in, cot_in, w_qkv, w_proj, w_expand, w_reduce)
     outs = (result, grad_x, g_qkv, g_proj, g_expand, g_reduce)
-    compute(b, lengths[lax.axis_index("blk"), 0, 0], Local(b, ins, outs, scratch[-1]))
+    compute(b, Local(b, lengths, ins, outs, scratch[-1]))
     g_vec[...] = b.g_vec[...]
 
 
@@ -580,10 +586,10 @@
 
 
 UNITS = (
-    (QKV, 0, 2 * TRIO), (QKV, 2 * TRIO, 2 * TRIO + LANES), (PROJ, 0, 6 * LANES),
+    (QKV, 0, TRIO), (QKV, TRIO, TRIO), (QKV, 2 * TRIO, TRIO), (QKV, 3 * TRIO, TRIO + LANES), (PROJ, 0, 6 * LANES),
     (EXPAND, 0, 8 * LANES), (EXPAND, 8 * LANES, 8 * LANES), (REDUCE, 0, 2 * LANES), (REDUCE, 2 * LANES, 2 * LANES),
 )
-EARLY_UNITS, PROJ_UNITS, EXPAND_UNITS, REDUCE_UNITS = (0, 1), (2,), (3, 4), (5, 6)
+EARLY_UNITS, PROJ_UNITS, EXPAND_UNITS, REDUCE_UNITS = (0, 1, 2, 3), (4,), (5, 6), (7, 8)
 VECTOR_TILES = ((QKV, 4 * TRIO), (PROJ, 4 * LANES), (PROJ, 5 * LANES))
 
 
@@ -592,7 +598,7 @@
         self.b = b
         self.tokens, self.cotangent, self.vectors, self.shards = ins
         self.result, self.grad_x, self.outs, self.g_total = outs
-        (self.own_qkv, self.own_vec, self.packed, self.turn, self.arrived, self.v_two, self.v_z,
+        (self.lengths, self.own_lengths, self.own_qkv, self.own_vec, self.packed, self.turn, self.arrived, self.v_two, self.v_z,
          self.local_sem, self.token_sem, self.ag_sem, self.rs_sem, self.v_sem) = scratch
         self.weights = tuple(b[-4:])
         dp, blk = lax.axis_index("dp"), lax.axis_index("blk")
@@ -674,13 +680,13 @@
 
         if stage < 3:
             view = w.at[self.place(order[:stage]) + cols]
-            return [one(3 * stage + k, view, device) for k, (device, _) in enumerate(self.along[order[stage]])]
+            return [one(copies_before(order, stage) + k, view, device) for k, (device, _) in enumerate(self.along[order[stage]])]
         device, _ = self.along[C][0]
         last = order[2]
         if stage == 3:
-            return [one(9, w.at[self.place(order[:2]) + cols], device)]
+            return [one(5, w.at[self.place(order[:2]) + cols], device)]
         (_, other), = self.along[last]
-        return [one(10, w.at[self.place(order[:2], {last: other}) + cols], device)]
+        return [one(6, w.at[self.place(order[:2], {last: other}) + cols], device)]
 
     def gather_on(self, units, stage):
         for unit in units:
@@ -726,7 +732,7 @@
             if at_z is not None and Z in rest:
                 at[Z] = at_z
             source = w.at[self.place(rest, at) + (slice(None), cols)]
-            sems = (self.rs_sem.at[i, which, chunk, 3 * stage + k] for i in range(2))
+            sems = (self.rs_sem.at[i, which, chunk % 2, copies_before(order, stage) + k] for i in range(2))
             copies.append(self.remote(source, buffer.at[self.landing(axis, rest, at_z, cols, k)], *sems, device))
         return copies
 
@@ -775,15 +781,15 @@
 
     def tick(self, which, t, stages):
         if isinstance(t, int):
+            for stage in reversed(range(stages)):
+                if 0 <= t - stage - 1 < CHUNKS:
+                    self.scatter_on(which, stage, t - stage - 1)
             if t < CHUNKS:
                 self.start(self.scatter(which, 0, t))
-            for stage in range(stages):
-                if 0 <= t - stage - 1 < CHUNKS:
-                    self.scatter_on(which, stage, t - stage - 1)
             return
+        for stage in reversed(range(min(stages, CHUNKS - 1))):
+            pl.when(t >= stage + 1)(lambda stage=stage: self.scatter_on(which, stage, t - stage - 1))
         self.start(self.scatter(which, 0, t))
-        for stage in range(min(stages, CHUNKS - 1)):
-            pl.when(t >= stage + 1)(lambda stage=stage: self.scatter_on(which, stage, t - stage - 1))
 
 
     def vector_copies(self, stage):
@@ -791,7 +797,7 @@
         return [
             self.remote(
                 self.b.g_vec, self.v_z.at[k] if axis == Z else self.v_two.at[stage],
-                self.v_sem.at[0, 3 * stage + k], self.v_sem.at[1, 3 * stage + k], device,
+                self.v_sem.at[0, stage + k], self.v_sem.at[1, stage + k], device,
             )
             for k, (device, _) in enumerate(self.along[axis])
         ]
@@ -809,16 +815,17 @@
 
 
     def begin(self):
-        barrier = pltpu.get_barrier_semaphore()
-        peers = self.others + [device for axis in (Y, Z) for device, _ in self.along[axis]]
-        for device in peers:
-            pl.semaphore_signal(barrier, inc=1, device_id=device, device_id_type=pl.DeviceIdType.MESH)
+        self.peers = self.others + [device for axis in (Y, Z) for device, _ in self.along[axis]]
+        for device in self.peers:
+            pl.semaphore_signal(
+                pltpu.get_barrier_semaphore(), inc=1, device_id=device, device_id_type=pl.DeviceIdType.MESH
+            )
         count = len(self.vectors)
         loads = [
             pltpu.make_async_copy(one, target, self.local_sem.at[4 + i])
             for i, (one, target) in enumerate(zip(self.vectors, self.own_vec))
         ]
-        loads.append(pltpu.make_async_copy(self.shards[QKV], self.own_qkv, self.local_sem.at[4 + count]))
+        loads.append(pltpu.make_async_copy(self.shards[QKV], self.own_qkv, self.local_sem.at[8 + count]))
         width = self.shards[PROJ].shape[1]
         slots = [self.weights[which].at[self.mine] for which in range(4)]
         self.own = [
@@ -828,6 +835,8 @@
             )
             for which in (PROJ, EXPAND, REDUCE)
         ]
+        loads.append(pltpu.make_async_copy(self.lengths, self.own_lengths, self.local_sem.at[4 + count + QKV]))
+        loads[-2], loads[-1] = loads[-1], loads[-2]
         self.start(loads + self.own + self.kept[:2])
         self.packed[...] = jnp.zeros_like(self.packed)
         row = 0
@@ -839,7 +848,8 @@
             at = self.index * size
             self.packed[pl.ds(row + at // LANES, 1), :] = pltpu.roll(self.turn[...], at % LANES, 1)[0:1, :]
             row += math.prod(SPREAD) * size // LANES
-        loads[-1].wait()
+        for load in loads[count:]:
+            load.wait()
         w = self.weights[QKV]
         for j in range(width // LANES):
             for i in range(3):
@@ -848,12 +858,19 @@
         for tile, (which, first) in enumerate(VECTOR_TILES):
             values = self.packed[tile * PACKED : (tile + 1) * PACKED, :].astype(BF)
             self.weights[which][self.mine + (slice(None), pl.ds(first, LANES))] = values
-        pl.semaphore_wait(barrier, len(peers))
+
+    def enter(self):
+        pl.semaphore_wait(pltpu.get_barrier_semaphore(), len(self.peers))
         for unit in EARLY_UNITS:
             self.start(self.gather(unit, 0))
         self.start(self.swaps[0])
         for copy in self.own:
             copy.wait()
+
+    def first_length(self):
+        first = self.own_lengths[0][0:1, :].astype(F32)
+        lane = lax.broadcasted_iota(jnp.int32, first.shape, 1)
+        return jnp.sum(jnp.where(lane == self.blk, first, 0.0), axis=1, keepdims=True)
 
     def need_tokens(self):
         self.gather_on(EARLY_UNITS, 0)
@@ -933,12 +950,9 @@
         for at in range(CHUNKS):
             pl.when(j == at)(lambda at=at: step(at))
 
-    def have_vectors(self):
-        self.start(self.vector_copies(0))
+    def have_grad(self):
+        self.start(self.vector_copies(0) + self.swaps[3] + self.kept[3:4])
         self.tick(QKV, CHUNKS, 4)
-
-    def have_grad(self):
-        self.start(self.swaps[3] + self.kept[3:4])
         for stage in range(3):
             self.vectors_on(stage)
             self.tick(QKV, CHUNKS + 1 + stage, 4)
@@ -963,11 +977,11 @@
     (lengths,), vectors, (tokens, cotangent), shards = take(1), take(N_VECTORS), take(2), take(4)
     (result, grad_x), outs, (g_total,) = take(2), take(4), take(1)
     b = Buffers(*take(len(Buffers._fields)))
-    (own_qkv,), own_vec, (packed, turn) = take(1), take(N_VECTORS), take(2)
+    (own_lengths, own_qkv), own_vec, (packed, turn) = take(2), take(N_VECTORS), take(2)
     arrived = [take(4) for _ in range(4)]
-    scratch = [own_qkv, own_vec, packed, turn, arrived] + refs
+    scratch = [lengths, own_lengths, own_qkv, own_vec, packed, turn, arrived] + refs
     group = Group(b, (tokens, cotangent, vectors, shards), (result, grad_x, outs, g_total), scratch)
-    compute(b, lengths[lax.axis_index("blk"), 0, 0], group)
+    compute(b, group)
 
 
 def run_group(lengths, vectors, tokens, cotangent, weights):
@@ -991,15 +1005,15 @@
         out_shape=[jax.ShapeDtypeStruct(tokens.shape, BF)] * 2
         + [jax.ShapeDtypeStruct(one.shape, F32) for one in weights]
         + [jax.ShapeDtypeStruct(sums, F32)],
-        in_specs=[pl.BlockSpec(memory_space=pltpu.SMEM)] + [anywhere] * (N_VECTORS + 6),
+        in_specs=[anywhere] * (N_VECTORS + 7),
         out_specs=[anywhere] * 2 + [vmem] * 5,
         scratch_shapes=buffers(blk * height, width, shapes)
-        + [pltpu.VMEM(weights[QKV].shape, BF)]
+        + [pltpu.VMEM(lengths.shape, lengths.dtype), pltpu.VMEM(weights[QKV].shape, BF)]
         + [pltpu.VMEM(one.shape, BF) for one in vectors]
         + [pltpu.VMEM((packed_rows, LANES), F32), pltpu.VMEM((8, LANES), F32)]
         + landing
         + [pltpu.VMEM((3,) + sums, F32), pltpu.VMEM((SPREAD[Z] - 1,) + sums, F32)]
-        + [dma((16,)), dma((8, 3)), dma((2, len(UNITS), 11)), dma((2, 4, CHUNKS, 12)), dma((2, 12))],
+        + [dma((17,)), dma((8, 3)), dma((2, len(UNITS), 7)), dma((2, 4, 2, 6)), dma((2, 6))],
         compiler_params=pltpu.CompilerParams(
             vmem_limit_bytes=62 * 2**20, collective_id=0, has_side_effects=True
         ),
@@ -1011,10 +1025,16 @@
     outs, refs = refs[: 6 + N_VECTORS], refs[6 + N_VECTORS :]
     held, short = refs[:6], refs[6 : 6 + N_VECTORS]
     turn, lines, sems = refs[6 + N_VECTORS :]
-    loads = [pltpu.make_async_copy(one, to, sems.at[i]) for i, (one, to) in enumerate(zip(sources, held))]
-    stores = [pltpu.make_async_copy(one, to, sems.at[6 + i]) for i, (one, to) in enumerate(zip(held, outs))]
+    loads, stores = [], []
+    for source, to, out in zip(sources, held, outs):
+        places = range(source.shape[0]) if len(source.shape) == 3 else (slice(None),)
+        for place in places:
+            sem = len(loads)
+            loads.append(pltpu.make_async_copy(source.at[place], to.at[place], sems.at[0, sem]))
+            stores.append(pltpu.make_async_copy(to.at[place], out.at[place], sems.at[1, sem]))
     for load in loads:
         load.start()
+    handed = []
     index = lax.axis_index("dp") * lax.axis_size("blk") + lax.axis_index("blk")
     devices = lax.axis_size("dp") * lax.axis_size("blk")
     width = g_vec.shape[1]
@@ -1029,13 +1049,13 @@
         turn[0:1, :] = lines[pl.ds(row + at // LANES, 1), :]
         turned = pltpu.roll(turn[...], (LANES - at % LANES) % LANES, 1)
         one[...] = turned[0:1, 0:size].reshape(size)
-        stores.append(pltpu.make_async_copy(one, outs[6 + i], sems.at[12 + i]))
-        stores[-1].start()
+        handed.append(pltpu.make_async_copy(one, outs[6 + i], sems.at[0, len(loads) + i]))
+        handed[-1].start()
         row += devices * size // LANES
     for load, store in zip(loads, stores):
         load.wait()
         store.start()
-    for store in stores:
+    for store in stores + handed:
         store.wait()
 
 
@@ -1050,7 +1070,7 @@
         out_specs=[anywhere] * (6 + len(sizes)),
         scratch_shapes=[pltpu.VMEM(*one) for one in long + short]
         + [pltpu.VMEM((8, LANES), F32), pltpu.VMEM((values[6].size // LANES, LANES), F32)]
-        + [pltpu.SemaphoreType.DMA((12 + len(sizes),))],
+        + [pltpu.SemaphoreType.DMA((2, 4 + 2 * values[0].shape[0] + len(sizes)))],
     )(*values)
 
 
@@ -1092,7 +1112,7 @@
     weights = (w_qkv, w_proj, w_expand, w_reduce)
     sized = (lax.axis_size("dp"), lax.axis_size("blk")) == (SPREAD[Z] * SPREAD[Y], SPREAD[X] * SPREAD[C])
     if sized and all(one.shape[0] % 16 == 0 for one in weights):
-        outs = finish(run_group(lengths, vectors, tokens, cotangent, weights), sizes)
+        outs = finish(run_group(jnp.transpose(lengths, (1, 2, 0)), vectors, tokens, cotangent, weights), sizes)
     else:
         outs = by_collectives(lengths, vectors, sizes, tokens, cotangent, weights)
     result, grad_x, g_qkv, g_proj, g_expand, g_reduce, ag, as_, qv, pb, mg, ms, rb, eb = outs

time: 161 us -> 143 us (0.89)
  Pallas kernels: 159 us -> 142 us
    pallas_call x1, Pallas kernels: 155 us -> 138 us  [run_group(): pl.pallas_call(group_kernel, out_shape=[jax.ShapeDtypeStruct(tokens.shape...]
where the time goes in v3:
time: 143 us
  Pallas kernels  142 us (99%)
    pallas_call x1, Pallas kernels, run_group(): pl.pallas_call(group_kernel, out_shape=[jax.ShapeDtypeStruct(tokens.shape...  138 us
    pallas_call x1, Pallas kernels, finish(): pl.pallas_call(finish_kernel, out_shape=[jax.ShapeDtypeStruct(*one) for o...  3.53 us

profile of v3, /device:TPU:0, one launch (start us, length us, event | category | flops | bytes accessed | tf_op | source)
XLA Modules:
  0.0 142.7 jit_solution(3685807838984663109)
XLA Ops:
  0.7 138.4 %shard_map.254 = (bf16[4,256,512]{2,1,0:T(8,128)(2,1)}, bf16[4,256,512]{2,1,0:T(8,128)(2,1)}, f32[16,1536]{1,0:T(8,128)}, f32[16,512]{1,0:T(8,128)}, f32[16,2048...) custom-call(s32[1,2,4]{2,1,0:T(2,128)} %bitcast.1, bf16[16]{0:T(256)(128)(2,1)} %refs_1_.1, bf16[16]{0:T(256)(128)(2,1)} %refs_2_.1, ...), custom_call_target="tpu_custom_call" | custom-call | tf_op jit(solution)/shard_map/pallas_call | solution.py:1003
  139.0 3.5 %shard_map.255 = (bf16[4,256,512]{2,1,0:T(8,128)(2,1)}, bf16[4,256,512]{2,1,0:T(8,128)(2,1)}, f32[16,1536]{1,0:T(8,128)}, f32[16,512]{1,0:T(8,128)}, f32[16,2048...) custom-call(bf16[4,256,512]{2,1,0:T(8,128)(2,1)} %get-tuple-element., ...), custom_call_target="tpu_custom_call" | custom-call | tf_op jit(solution)/shard_map/pallas_call | solution.py:1066

commit v4 on v3

--- a/solution.py
+++ b/solution.py
@@ -30,7 +30,7 @@
 SPREAD = (4, 2, 2, 2)
 QKV, PROJ, EXPAND, REDUCE = range(4)
 GATHER_ORDER = ((X, Z, Y), (X, Z, Y), (X, Z, Y), (Z, Y, X))
-SCATTER_ORDER = tuple((C,) + order[::-1] for order in GATHER_ORDER)
+SCATTER_ORDER = ((C, X, Y, Z), (C, Y, Z, X), (C, Y, Z, X), (C, X, Y, Z))
 
 
 def copies_before(order, stage):
@@ -227,20 +227,46 @@
         ref[of_head, LONG_KEYS:total] = tail_part[:, both:].astype(BF)
 
 
+def trio_columns(ref, j, width):
+    return ref.shape[-1] - 3 * width + j * TRIO
+
+
 def all_forward(b, transfers):
+    total, width = b.attended.shape
     unrolled = 2
 
-    def step(i, carried):
-        for one in range(unrolled):
-            at = i * unrolled + one
-            forward_head(
-                at // HEADS_IN_BLOCK, at % HEADS_IN_BLOCK, b.qkv, b.attended, b.inverse,
-                b.e_long, b.e_tail, b.aug_q, b.aug_k,
-            )
-        transfers.after_forward(i)
+    def block(j, carried):
+        transfers.before_block(j)
+        here = pl.ds(pl.multiple_of(j * LANES, LANES), LANES)
+        w_trio = get(b.w_qkv, trio_columns(b.w_qkv, j, width), TRIO)
+        for at, n in pieces(total, ROWS):
+            projected = nn(b.x_in[at : at + n], w_trio)
+            q, k, v = (projected[:, i * LANES : (i + 1) * LANES] for i in range(3))
+            q = (q + b.vec[Q_BIAS : Q_BIAS + 1, here]) * (SCALE * LOG2E)
+            v = v + b.vec[V_BIAS : V_BIAS + 1, here]
+            for i, value in enumerate((q, k, v)):
+                of_trio(b.qkv, j, i)[at : at + n] = value.astype(BF)
+
+        def step(i, inside):
+            for one in range(unrolled):
+                forward_head(
+                    j, i * unrolled + one, b.qkv, b.attended, b.inverse,
+                    b.e_long, b.e_tail, b.aug_q, b.aug_k,
+                )
+            transfers.after_forward(j * (HEADS_IN_BLOCK // unrolled) + i)
+            return inside
+
+        lax.fori_loop(0, HEADS_IN_BLOCK // unrolled, step, 0)
         return carried
 
-    lax.fori_loop(0, b.attended.shape[1] // HEAD_DIM // unrolled, step, 0)
+    lax.fori_loop(0, width // LANES, block, 0)
+
+
+def weight_of_block(b, j, transfers):
+    trio = pl.ds(pl.multiple_of(j * TRIO, LANES), TRIO)
+    at = trio_columns(b.w_qkv, j, b.attended.shape[1])
+    put(b.w_qkv, nn(b.ha_t[...], b.qkv[:, trio]).astype(BF), at, TRIO)
+    transfers.have_qkv(j)
 
 
 def all_backward(b, transfers):
@@ -248,7 +274,11 @@
     unrolled = 2
     keep = (b.scaled_b, b.aug_b, b.q_t, b.s_t, b.k_b)
 
-    def block(j, carried):
+    blocks = width // LANES
+
+    def block(number, carried):
+        j = blocks - 1 - number
+        pl.when(number > 0)(lambda: weight_of_block(b, j + 1, transfers))
         backward_prepare(j, b.qkv, b.attended, b.inverse, b.d_exp, *keep)
 
         def step(i, inside):
@@ -256,6 +286,7 @@
                 backward_head(
                     j, i * unrolled + one, b.qkv, b.e_long, b.e_tail, *keep, b.dk_t, b.dv_t
                 )
+            transfers.after_backward(number * (HEADS_IN_BLOCK // unrolled) + i)
             return inside
 
         lax.fori_loop(0, HEADS_IN_BLOCK // unrolled, step, 0)
@@ -266,15 +297,12 @@
         for row, which in ((Q_BIAS, 0), (V_BIAS, 2)):
             values = of_trio(b.qkv, j, which)[...].astype(F32)
             b.g_vec[row : row + 1, here] = jnp.sum(values, axis=0, keepdims=True)
-
-        w_trio = get(b.w_qkv, j * TRIO, TRIO)
+        w_trio = get(b.w_qkv, trio_columns(b.w_qkv, j, width), TRIO)
         for at, n in pieces(total, ROWS):
             b.acc_b[at : at + n] = b.acc_b[at : at + n] + nt(b.qkv[at : at + n, trio], w_trio)
-        put(b.w_qkv, nn(b.ha_t[...], b.qkv[:, trio]).astype(BF), j * TRIO, TRIO)
-        transfers.after_backward(j)
         return carried
 
-    lax.fori_loop(0, width // LANES, block, 0)
+    lax.fori_loop(0, blocks, block, 0)
 
 
 class Buffers(typing.NamedTuple):
@@ -395,25 +423,13 @@
     def _(rows):
         values = loaded(rows)
         b.xc[rows] = values.astype(BF)
-        acc_a[rows], _ = norm_parts(values)
-
-    transfers.need_qkv()
-    qkv, w_qkv = b.qkv, b.w_qkv
-
+        normed, _ = norm_parts(values)
+        b.x_in[rows] = (normed * vector(A_GAIN) + vector(A_SHIFT)).astype(BF)
+
+    transfers.need_first()
     for at, n in pieces(total, ROWS):
-        rows = slice(at, at + n)
-        lowered = (acc_a[rows] * vector(A_GAIN) + vector(A_SHIFT)).astype(BF)
-        b.ha_t[:, rows] = lowered.T
-        for j in range(width // LANES):
-            here = slice(j * LANES, (j + 1) * LANES)
-            projected = nn(lowered, get(w_qkv, j * TRIO, TRIO))
-            q, k, v = (projected[:, i * LANES : (i + 1) * LANES] for i in range(3))
-            q = (q + vec[Q_BIAS : Q_BIAS + 1, here]) * (SCALE * LOG2E)
-            v = v + vec[V_BIAS : V_BIAS + 1, here]
-            for i, value in enumerate((q, k, v)):
-                qkv[rows, j * TRIO + i * LANES : j * TRIO + (i + 1) * LANES] = value.astype(BF)
-
-    transfers.forward()
+        b.ha_t[:, at : at + n] = b.x_in[at : at + n].T
+
     all_forward(b, transfers)
 
     transfers.need_cotangent()
@@ -487,6 +503,7 @@
     transfers.have_result()
     acc_b[...] = jnp.zeros_like(acc_b)
     all_backward(b, transfers)
+    weight_of_block(b, 0, transfers)
 
     @by_rows
     def _(rows):
@@ -496,6 +513,7 @@
         add_sum(A_SHIFT, gradient)
         acc_a[rows] = middle[rows] + norm_back(gradient, normed, inv, vector(A_GAIN))
 
+    transfers.have_vectors()
     unload(acc_a, acc_b, act)
     transfers.have_grad()
 
@@ -521,10 +539,10 @@
     def need_tokens(self):
         self.loads[0].wait()
 
-    def need_qkv(self):
+    def need_first(self):
         self.loads[2 + QKV].wait()
 
-    def forward(self):
+    def before_block(self, j):
         pass
 
     def after_forward(self, i):
@@ -550,11 +568,16 @@
     def have_result(self):
         self.stores[0].start()
 
-    def after_backward(self, j):
+    def after_backward(self, i):
         pass
 
+    def have_qkv(self, j):
+        pass
+
+    def have_vectors(self):
+        self.stores[2 + QKV].start()
+
     def have_grad(self):
-        self.stores[2 + QKV].start()
         self.stores[1].start()
         for copy in self.stores:
             copy.wait()
@@ -586,11 +609,38 @@
 
 
 UNITS = (
-    (QKV, 0, TRIO), (QKV, TRIO, TRIO), (QKV, 2 * TRIO, TRIO), (QKV, 3 * TRIO, TRIO + LANES), (PROJ, 0, 6 * LANES),
-    (EXPAND, 0, 8 * LANES), (EXPAND, 8 * LANES, 8 * LANES), (REDUCE, 0, 2 * LANES), (REDUCE, 2 * LANES, 2 * LANES),
+    (QKV, 0, LANES + TRIO), (QKV, LANES + TRIO, TRIO), (QKV, LANES + 2 * TRIO, TRIO), (QKV, LANES + 3 * TRIO, TRIO),
+    (PROJ, 0, 6 * LANES),
+    (EXPAND, 0, 8 * LANES), (EXPAND, 8 * LANES, 8 * LANES), (REDUCE, 0, 4 * LANES), (REDUCE, 0, 4 * LANES),
 )
+HALVES = {7: pl.ds(0, SPREAD[Z] // 2), 8: pl.ds(SPREAD[Z] // 2, SPREAD[Z] // 2)}
 EARLY_UNITS, PROJ_UNITS, EXPAND_UNITS, REDUCE_UNITS = (0, 1, 2, 3), (4,), (5, 6), (7, 8)
-VECTOR_TILES = ((QKV, 4 * TRIO), (PROJ, 4 * LANES), (PROJ, 5 * LANES))
+VECTOR_TILES = ((QKV, 0), (PROJ, 4 * LANES), (PROJ, 5 * LANES))
+CHUNK_COPIES = 6
+
+
+def schedule():
+    entries = {}
+
+    def enter(t, which, stage, chunk):
+        entries.setdefault(t, []).append((which, stage, chunk))
+
+    for chunk in range(CHUNKS):
+        for stage, later in enumerate((1, 3, 5, 7)):
+            enter(chunk + later, EXPAND, stage, chunk)
+        for stage, later in enumerate((1, 3, 4)):
+            enter(chunk + later, REDUCE, stage, chunk)
+    enter(CHUNKS + 3, REDUCE, None, 0)
+    enter(CHUNKS + 6, REDUCE, 3, 0)
+    for stage, t in enumerate((5, 7, 9, 11)):
+        enter(t, PROJ, stage, 0)
+    for number, times in enumerate(((8, 9, 10, 11), (10, 11, 12, 13), (12, 13, 14, 15), (13, 14, 15, 16))):
+        for stage, t in enumerate(times):
+            enter(t, QKV, stage, CHUNKS - 1 - number)
+    return entries
+
+
+SCHEDULE = schedule()
 
 
 class Group:
@@ -598,8 +648,8 @@
         self.b = b
         self.tokens, self.cotangent, self.vectors, self.shards = ins
         self.result, self.grad_x, self.outs, self.g_total = outs
-        (self.lengths, self.own_lengths, self.own_qkv, self.own_vec, self.packed, self.turn, self.arrived, self.v_two, self.v_z,
-         self.local_sem, self.token_sem, self.ag_sem, self.rs_sem, self.v_sem) = scratch
+        (self.lengths, self.own_lengths, self.own_qkv, self.own_vec, self.packed, self.turn, self.tile, self.arrived,
+         self.local_sem, self.token_sem, self.ag_sem, self.rs_sem) = scratch
         self.weights = tuple(b[-4:])
         dp, blk = lax.axis_index("dp"), lax.axis_index("blk")
         z, y, x, c = dp // SPREAD[Y], dp % SPREAD[Y], blk // SPREAD[C], blk % SPREAD[C]
@@ -678,15 +728,20 @@
         def one(i, view, device):
             return self.remote(view, view, self.ag_sem.at[0, unit, i], self.ag_sem.at[1, unit, i], device)
 
+        half = {Z: HALVES[unit]} if unit in HALVES else {}
+        if stage == 0 and unit in HALVES:
+            if unit != min(HALVES):
+                return []
+            half = {}
         if stage < 3:
-            view = w.at[self.place(order[:stage]) + cols]
+            view = w.at[self.place(order[:stage], half) + cols]
             return [one(copies_before(order, stage) + k, view, device) for k, (device, _) in enumerate(self.along[order[stage]])]
         device, _ = self.along[C][0]
         last = order[2]
         if stage == 3:
-            return [one(5, w.at[self.place(order[:2]) + cols], device)]
+            return [one(5, w.at[self.place(order[:2], half) + cols], device)]
         (_, other), = self.along[last]
-        return [one(6, w.at[self.place(order[:2], {last: other}) + cols], device)]
+        return [one(6, w.at[self.place(order[:2], {last: other, **half}) + cols], device)]
 
     def gather_on(self, units, stage):
         for unit in units:
@@ -718,100 +773,111 @@
     def chunk_view(self, which, chunk):
         if which == REDUCE:
             return chunk, slice(None)
-        columns = (TRIO, 4 * LANES, 4 * LANES)[which]
-        return None, pl.ds(pl.multiple_of(chunk * columns, LANES), columns)
+        if which == QKV:
+            return None, pl.ds(LANES + chunk * TRIO, TRIO) if chunk else pl.ds(0, LANES + TRIO)
+        return None, pl.ds(chunk * 4 * LANES, 4 * LANES)
 
     def scatter(self, which, stage, chunk):
         w, order = self.weights[which], SCATTER_ORDER[which]
         axis, rest = order[stage], order[stage + 1 :]
         buffer = self.arrived[which][stage]
         at_z, cols = self.chunk_view(which, chunk)
-        copies = []
+        first = (which * CHUNKS + chunk) * CHUNK_COPIES + copies_before(order, stage)
+        copies, terms = [], []
         for k, (device, other) in enumerate(self.along[axis]):
             at = {axis: other}
             if at_z is not None and Z in rest:
                 at[Z] = at_z
             source = w.at[self.place(rest, at) + (slice(None), cols)]
-            sems = (self.rs_sem.at[i, which, chunk % 2, copies_before(order, stage) + k] for i in range(2))
-            copies.append(self.remote(source, buffer.at[self.landing(axis, rest, at_z, cols, k)], *sems, device))
-        return copies
-
-    @staticmethod
-    def landing(axis, rest, at_z, cols, k):
-        lead = (k,) if axis == Z else ()
-        free = tuple(at_z if one == Z and at_z is not None else slice(None) for one in sorted(rest))
-        return lead + free + (slice(None), cols)
+            lead = (k,) if axis == Z else ()
+            free = tuple(at_z if one == Z and at_z is not None else slice(None) for one in sorted(rest))
+            target = buffer.at[lead + free + (slice(None), cols)]
+            copies.append(self.remote(source, target, self.rs_sem.at[0, first + k], self.rs_sem.at[1, first + k], device))
+            terms.append(target)
+        return copies, terms
+
+    def scatter_start(self, which, stage, chunk):
+        self.start(self.scatter(which, stage, chunk)[0])
 
     def scatter_on(self, which, stage, chunk):
         w, order = self.weights[which], SCATTER_ORDER[which]
-        copies = self.scatter(which, stage, chunk)
+        copies, terms = self.scatter(which, stage, chunk)
         self.arrive(copies)
-        axis, rest = order[stage], order[stage + 1 :]
-        buffer = self.arrived[which][stage]
+        rest = order[stage + 1 :]
         at_z, cols = self.chunk_view(which, chunk)
         at = {Z: at_z} if at_z is not None and Z in rest else None
         here = self.place(rest, at) + (slice(None), cols)
-        terms = [buffer[self.landing(axis, rest, at_z, cols, k)] for k in range(len(copies))]
-        if not rest:
-            total = w[here].astype(F32)
-            for term in terms:
-                total = total + term.astype(F32)
-            self.keep(which, chunk, total)
-        elif len(terms) == 1:
-            w[here] = w[here] + terms[0]
+        sums = None
+        if which == QKV and not chunk:
+            sums = self.vector_sums(self.place(rest), terms)
+        if len(terms) == 1 and rest:
+            w[here] = w[here] + terms[0][...]
         else:
             total = w[here].astype(F32)
             for term in terms:
-                total = total + term.astype(F32)
-            w[here] = total.astype(BF)
+                total = total + term[...].astype(F32)
+            if rest:
+                w[here] = total.astype(BF)
+            else:
+                self.keep(which, chunk, total)
+        if sums is not None:
+            half = PACKED // 2
+            exact = sums[..., :half, :] + sums[..., half:, :]
+            if rest:
+                high = exact.astype(BF).astype(F32)
+                w[self.place(rest) + (slice(None), pl.ds(0, LANES))] = jnp.concatenate([high, exact - high], axis=-2).astype(BF)
+            else:
+                self.g_total[...] = exact
         if rest and not (which == REDUCE and rest == (Z,)):
-            self.start(self.scatter(which, stage + 1, chunk))
+            self.scatter_start(which, stage + 1, chunk)
         self.sent(copies)
+
+    def vector_sums(self, here, terms):
+        total = self.weights[QKV][here + (slice(None), pl.ds(0, LANES))].astype(F32)
+        for term in terms:
+            total = total + term[...][..., 0:LANES].astype(F32)
+        return total
 
     def keep(self, which, chunk, total):
         out = self.outs[which]
         if which == QKV:
             width = out.shape[1] // 3
+            if not chunk:
+                total = total[:, LANES:]
             for i in range(3):
-                cols = pl.ds(pl.multiple_of(i * width + chunk * LANES, LANES), LANES)
-                out[:, cols] = total[:, i * LANES : (i + 1) * LANES]
+                out[:, i * width + chunk * LANES : i * width + (chunk + 1) * LANES] = total[:, i * LANES : (i + 1) * LANES]
         else:
-            _, cols = self.chunk_view(which, chunk)
-            out[:, cols] = total
-
-    def tick(self, which, t, stages):
-        if isinstance(t, int):
-            for stage in reversed(range(stages)):
-                if 0 <= t - stage - 1 < CHUNKS:
-                    self.scatter_on(which, stage, t - stage - 1)
-            if t < CHUNKS:
-                self.start(self.scatter(which, 0, t))
-            return
-        for stage in reversed(range(min(stages, CHUNKS - 1))):
-            pl.when(t >= stage + 1)(lambda stage=stage: self.scatter_on(which, stage, t - stage - 1))
-        self.start(self.scatter(which, 0, t))
-
-
-    def vector_copies(self, stage):
-        axis = (C, Y, X, Z)[stage]
-        return [
-            self.remote(
-                self.b.g_vec, self.v_z.at[k] if axis == Z else self.v_two.at[stage],
-                self.v_sem.at[0, stage + k], self.v_sem.at[1, stage + k], device,
-            )
-            for k, (device, _) in enumerate(self.along[axis])
-        ]
-
-    def vectors_on(self, stage):
-        copies = self.vector_copies(stage)
-        self.arrive(copies)
-        self.sent(copies)
-        g_vec = self.b.g_vec
-        if stage < 3:
-            g_vec[...] = g_vec[...] + self.v_two[stage]
-            self.start(self.vector_copies(stage + 1))
-        else:
-            self.g_total[...] = g_vec[...] + jnp.sum(self.v_z[...], axis=0)
+            out[:, self.chunk_view(which, chunk)[1]] = total
+
+    def tick(self, t):
+        for which, stage, chunk in SCHEDULE.get(t, ()):
+            if stage is None:
+                self.scatter_start(which, 3, chunk)
+            else:
+                self.scatter_on(which, stage, chunk)
+
+
+    def spread_vectors(self):
+        g_vec, lines, tile = self.b.g_vec, self.packed, self.tile
+        parts = g_vec.shape[1] // LANES
+        for i in range(lines.shape[0]):
+            lines[i : i + 1, :] = g_vec[i // parts : i // parts + 1, i % parts * LANES : (i % parts + 1) * LANES]
+        tile[...] = jnp.zeros_like(tile)
+        devices = math.prod(SPREAD)
+        for device in range(0, devices, SPREAD[C]):
+            row = 0
+            for i, one in enumerate(self.own_vec):
+                size = one.shape[0]
+                if device * size % LANES == 0:
+                    at = row + device * size // LANES
+                    tile[i : i + 1, :] = lines[at : at + 1, :]
+                row += devices * size // LANES
+            high = tile[...].astype(BF).astype(F32)
+            value = jnp.concatenate([high, tile[...] - high], axis=0).astype(BF)
+            pair = device // SPREAD[C]
+            place = (pair // (SPREAD[X] * SPREAD[Y]), pair // SPREAD[X] % SPREAD[Y], pair % SPREAD[X])
+            for core in range(SPREAD[C]):
+                self.weights[QKV][place + (core, slice(None), pl.ds(0, LANES))] = value
 
 
     def begin(self):
@@ -853,7 +919,7 @@
         w = self.weights[QKV]
         for j in range(width // LANES):
             for i in range(3):
-                to = j * TRIO + i * LANES
+                to = LANES + j * TRIO + i * LANES
                 w[self.mine + (slice(None), pl.ds(to, LANES))] = self.own_qkv[:, i * width + j * LANES : i * width + (j + 1) * LANES]
         for tile, (which, first) in enumerate(VECTOR_TILES):
             values = self.packed[tile * PACKED : (tile + 1) * PACKED, :].astype(BF)
@@ -866,6 +932,8 @@
         self.start(self.swaps[0])
         for copy in self.own:
             copy.wait()
+        for unit in PROJ_UNITS + EXPAND_UNITS:
+            self.start(self.gather(unit, 0))
 
     def first_length(self):
         first = self.own_lengths[0][0:1, :].astype(F32)
@@ -874,37 +942,39 @@
 
     def need_tokens(self):
         self.gather_on(EARLY_UNITS, 0)
-        for unit in PROJ_UNITS + EXPAND_UNITS:
-            self.start(self.gather(unit, 0))
-        self.gather_on(EARLY_UNITS, 1)
-        for unit in REDUCE_UNITS:
-            self.start(self.gather(unit, 0))
-        self.gather_on(PROJ_UNITS + EXPAND_UNITS, 0)
+        self.gather_on(EARLY_UNITS[:2], 1)
+        self.gather_on(EARLY_UNITS[:1], 2)
+        self.gather_on(EARLY_UNITS[2:3], 1)
+        self.gather_on(EARLY_UNITS[1:2], 2)
+        self.gather_on(EARLY_UNITS[3:], 1)
+        self.start(self.gather(REDUCE_UNITS[0], 0))
+        self.gathered(EARLY_UNITS[:1])
+        self.unpack(0)
         self.kept[0].wait()
         self.arrive(self.swaps[0])
         self.sent(self.swaps[0])
         self.start(self.swaps[1])
 
-    def need_qkv(self):
-        self.gather_on(EARLY_UNITS, 2)
-        self.gathered(EARLY_UNITS)
-        self.unpack(0)
-
-    def forward(self):
-        pass
+    def need_first(self):
+        self.gather_on(PROJ_UNITS + EXPAND_UNITS, 0)
+        self.gather_on(EARLY_UNITS[2:3], 2)
+
+    def before_block(self, j):
+        for unit in EARLY_UNITS[1:]:
+            pl.when(j == unit)(lambda unit=unit: self.gathered((unit,)))
 
     def after_forward(self, i):
-        steps = {
-            0: lambda: self.gather_on(REDUCE_UNITS, 0),
-            1: lambda: self.gather_on(PROJ_UNITS, 1),
-            2: lambda: self.gather_on(REDUCE_UNITS, 1),
-            3: lambda: (self.gather_on(EXPAND_UNITS[:1], 1), self.gather_on(PROJ_UNITS, 2)),
-            4: lambda: self.gather_on(EXPAND_UNITS[1:], 1),
-            5: lambda: self.gather_on(REDUCE_UNITS, 2),
-            6: lambda: self.gather_on(EXPAND_UNITS[:1], 2),
-            7: lambda: self.gather_on(EXPAND_UNITS[1:], 2),
-        }
-        for at, step in steps.items():
+        steps = (
+            lambda: (self.gather_on(EARLY_UNITS[3:], 2), self.gather_on(REDUCE_UNITS, 0)),
+            lambda: None,
+            lambda: self.gather_on(PROJ_UNITS, 1),
+            lambda: (self.gather_on(REDUCE_UNITS, 1), self.gather_on(EXPAND_UNITS[:1], 1)),
+            lambda: self.gather_on(PROJ_UNITS, 2),
+            lambda: self.gather_on(EXPAND_UNITS[1:], 1),
+            lambda: self.gather_on(EXPAND_UNITS[:1], 2),
+            lambda: self.gather_on(REDUCE_UNITS[:1], 2),
+        )
+        for at, step in enumerate(steps):
             pl.when(i == at)(lambda step=step: [step(), None][1])
 
     def need_cotangent(self):
@@ -918,45 +988,45 @@
         self.unpack(2)
 
     def need_mlp(self):
-        self.gathered(EXPAND_UNITS + REDUCE_UNITS)
+        self.gathered(EXPAND_UNITS[:1] + REDUCE_UNITS[:1])
 
     def after_part(self, part):
-        self.tick(REDUCE, part, 3)
-        self.tick(EXPAND, part, 4)
+        for at in range(CHUNKS):
+            @pl.when(part == at)
+            def _(at=at):
+                self.scatter_start(REDUCE, 0, at)
+                self.scatter_start(EXPAND, 0, at)
+                if at == 0:
+                    self.gather_on(EXPAND_UNITS[1:] + REDUCE_UNITS[1:], 2)
+                if at == 1:
+                    self.gathered(EXPAND_UNITS[1:] + REDUCE_UNITS[1:])
+                self.tick(at)
 
     def have_proj(self):
-        self.start(self.scatter(PROJ, 0, 0))
-        self.tick(REDUCE, CHUNKS, 3)
-        self.tick(EXPAND, CHUNKS, 4)
+        self.scatter_start(PROJ, 0, 0)
+        self.tick(CHUNKS)
 
     def have_result(self):
         self.start(self.swaps[2] + self.kept[2:3])
 
-    def after_backward(self, j):
-        self.tick(QKV, j, 4)
-
-        def step(at):
-            self.scatter_on(PROJ, at, 0)
-            t = CHUNKS + 1 + at
-            if t < CHUNKS + 3:
-                self.tick(REDUCE, t, 3)
-            elif t == CHUNKS + 3:
-                self.start(self.scatter(REDUCE, 3, 0))
-            else:
-                self.scatter_on(REDUCE, 3, 0)
-            if t < CHUNKS + 4:
-                self.tick(EXPAND, t, 4)
-
-        for at in range(CHUNKS):
-            pl.when(j == at)(lambda at=at: step(at))
+    def after_backward(self, i):
+        for at in range(2 * CHUNKS):
+            pl.when(i == at)(lambda at=at: self.tick(CHUNKS + 1 + at))
+
+    def have_qkv(self, j):
+        for at in range(1, CHUNKS):
+            pl.when(j == at)(lambda at=at: self.scatter_start(QKV, 0, at))
+
+    def have_vectors(self):
+        self.spread_vectors()
+        self.scatter_start(QKV, 0, 0)
 
     def have_grad(self):
-        self.start(self.vector_copies(0) + self.swaps[3] + self.kept[3:4])
-        self.tick(QKV, CHUNKS, 4)
-        for stage in range(3):
-            self.vectors_on(stage)
-            self.tick(QKV, CHUNKS + 1 + stage, 4)
-        self.vectors_on(3)
+        end = 3 * CHUNKS + 1
+        self.tick(end)
+        self.start(self.swaps[3] + self.kept[3:4])
+        for t in range(end + 1, max(SCHEDULE) + 1):
+            self.tick(t)
         for i in (2, 3):
             self.kept[i].wait()
             self.arrive(self.swaps[i])
@@ -977,9 +1047,9 @@
     (lengths,), vectors, (tokens, cotangent), shards = take(1), take(N_VECTORS), take(2), take(4)
     (result, grad_x), outs, (g_total,) = take(2), take(4), take(1)
     b = Buffers(*take(len(Buffers._fields)))
-    (own_lengths, own_qkv), own_vec, (packed, turn) = take(2), take(N_VECTORS), take(2)
+    (own_lengths, own_qkv), own_vec, (packed, turn, tile) = take(2), take(N_VECTORS), take(3)
     arrived = [take(4) for _ in range(4)]
-    scratch = [lengths, own_lengths, own_qkv, own_vec, packed, turn, arrived] + refs
+    scratch = [lengths, own_lengths, own_qkv, own_vec, packed, turn, tile, arrived] + refs
     group = Group(b, (tokens, cotangent, vectors, shards), (result, grad_x, outs, g_total), scratch)
     compute(b, group)
 
@@ -996,24 +1066,22 @@
         for stage, axis in enumerate(SCATTER_ORDER[which]):
             rest = sorted(SCATTER_ORDER[which][stage + 1 :])
             lead = (SPREAD[Z] - 1,) if axis == Z else ()
-            landing.append(pltpu.VMEM(lead + tuple(SPREAD[one] for one in rest) + weights[which].shape, BF))
-    sums = (VEC_ROWS, width)
+            landing.append(pltpu.VMEM(lead + tuple(SPREAD[one] for one in rest) + shape[4:], BF))
     packed_rows = math.prod(SPREAD) * sum(one.shape[0] for one in vectors) // LANES
     dma = pltpu.SemaphoreType.DMA
     return pl.pallas_call(
         group_kernel,
         out_shape=[jax.ShapeDtypeStruct(tokens.shape, BF)] * 2
         + [jax.ShapeDtypeStruct(one.shape, F32) for one in weights]
-        + [jax.ShapeDtypeStruct(sums, F32)],
+        + [jax.ShapeDtypeStruct((N_VECTORS, LANES), F32)],
         in_specs=[anywhere] * (N_VECTORS + 7),
         out_specs=[anywhere] * 2 + [vmem] * 5,
         scratch_shapes=buffers(blk * height, width, shapes)
         + [pltpu.VMEM(lengths.shape, lengths.dtype), pltpu.VMEM(weights[QKV].shape, BF)]
         + [pltpu.VMEM(one.shape, BF) for one in vectors]
-        + [pltpu.VMEM((packed_rows, LANES), F32), pltpu.VMEM((8, LANES), F32)]
+        + [pltpu.VMEM((packed_rows, LANES), F32), pltpu.VMEM((8, LANES), F32), pltpu.VMEM((N_VECTORS, LANES), F32)]
         + landing
-        + [pltpu.VMEM((3,) + sums, F32), pltpu.VMEM((SPREAD[Z] - 1,) + sums, F32)]
-        + [dma((17,)), dma((8, 3)), dma((2, len(UNITS), 7)), dma((2, 4, 2, 6)), dma((2, 6))],
+        + [dma((17,)), dma((8, 3)), dma((2, len(UNITS), 7)), dma((2, 4 * CHUNKS * CHUNK_COPIES))],
         compiler_params=pltpu.CompilerParams(
             vmem_limit_bytes=62 * 2**20, collective_id=0, has_side_effects=True
         ),
@@ -1024,7 +1092,7 @@
     sources = (result, grad_x, g_qkv, g_proj, g_expand, g_reduce)
     outs, refs = refs[: 6 + N_VECTORS], refs[6 + N_VECTORS :]
     held, short = refs[:6], refs[6 : 6 + N_VECTORS]
-    turn, lines, sems = refs[6 + N_VECTORS :]
+    turn, sems = refs[6 + N_VECTORS :]
     loads, stores = [], []
     for source, to, out in zip(sources, held, outs):
         places = range(source.shape[0]) if len(source.shape) == 3 else (slice(None),)
@@ -1036,22 +1104,14 @@
         load.start()
     handed = []
     index = lax.axis_index("dp") * lax.axis_size("blk") + lax.axis_index("blk")
-    devices = lax.axis_size("dp") * lax.axis_size("blk")
-    width = g_vec.shape[1]
-    parts = width // LANES
-    for i in range(g_vec.shape[0]):
-        for part in range(parts):
-            lines[i * parts + part : i * parts + part + 1, :] = g_vec[i : i + 1, part * LANES : (part + 1) * LANES]
-    row = 0
     for i, one in enumerate(short):
         size = one.shape[0]
         at = index * size
-        turn[0:1, :] = lines[pl.ds(row + at // LANES, 1), :]
+        turn[0:1, :] = g_vec[i : i + 1, :]
         turned = pltpu.roll(turn[...], (LANES - at % LANES) % LANES, 1)
         one[...] = turned[0:1, 0:size].reshape(size)
         handed.append(pltpu.make_async_copy(one, outs[6 + i], sems.at[0, len(loads) + i]))
         handed[-1].start()
-        row += devices * size // LANES
     for load, store in zip(loads, stores):
         load.wait()
         store.start()
@@ -1069,7 +1129,7 @@
         in_specs=[anywhere] * 6 + [vmem],
         out_specs=[anywhere] * (6 + len(sizes)),
         scratch_shapes=[pltpu.VMEM(*one) for one in long + short]
-        + [pltpu.VMEM((8, LANES), F32), pltpu.VMEM((values[6].size // LANES, LANES), F32)]
+        + [pltpu.VMEM((8, LANES), F32)]
         + [pltpu.SemaphoreType.DMA((2, 4 + 2 * values[0].shape[0] + len(sizes)))],
     )(*values)
 

time: 143 us -> 138 us (0.965)
  Pallas kernels: 142 us -> 136 us
    pallas_call x1, Pallas kernels: 138 us -> 133 us  [run_group(): pl.pallas_call(group_kernel, out_shape=[jax.ShapeDtypeStruct(tokens.shape...]
where the time goes in v4:
time: 138 us; the launch traced here: 137 us
  Pallas kernels  136 us (99%)
    pallas_call x1, Pallas kernels, run_group(): pl.pallas_call(group_kernel, out_shape=[jax.ShapeDtypeStruct(tokens.shape...  133 us
    pallas_call x1, Pallas kernels, finish(): pl.pallas_call(finish_kernel, out_shape=[jax.ShapeDtypeStruct(*one) for o...  3.43 us

profile of v4, /device:TPU:0, one launch (start us, length us, event | category | flops | bytes accessed | tf_op | source)
XLA Modules:
  0.0 137.0 jit_solution(6071787857089684519)
XLA Ops:
  0.7 132.7 %shard_map.254 = (bf16[4,256,512]{2,1,0:T(8,128)(2,1)}, bf16[4,256,512]{2,1,0:T(8,128)(2,1)}, f32[16,1536]{1,0:T(8,128)}, f32[16,512]{1,0:T(8,128)}, f32[16,2048...) custom-call(s32[1,2,4]{2,1,0:T(2,128)} %bitcast.1, bf16[16]{0:T(256)(128)(2,1)} %refs_1_.1, bf16[16]{0:T(256)(128)(2,1)} %refs_2_.1, ...), custom_call_target="tpu_custom_call" | custom-call | tf_op jit(solution)/shard_map/pallas_call | solution.py:1072
  133.4 3.4 %shard_map.255 = (bf16[4,256,512]{2,1,0:T(8,128)(2,1)}, bf16[4,256,512]{2,1,0:T(8,128)(2,1)}, f32[16,1536]{1,0:T(8,128)}, f32[16,512]{1,0:T(8,128)}, f32[16,2048...) custom-call(bf16[4,256,512]{2,1,0:T(8,128)(2,1)} %get-tuple-element., ...), custom_call_target="tpu_custom_call" | custom-call | tf_op jit(solution)/shard_map/pallas_call | solution.py:1126

commit v5 on v4

--- a/solution.py
+++ b/solution.py
@@ -616,7 +616,9 @@
 HALVES = {7: pl.ds(0, SPREAD[Z] // 2), 8: pl.ds(SPREAD[Z] // 2, SPREAD[Z] // 2)}
 EARLY_UNITS, PROJ_UNITS, EXPAND_UNITS, REDUCE_UNITS = (0, 1, 2, 3), (4,), (5, 6), (7, 8)
 VECTOR_TILES = ((QKV, 0), (PROJ, 4 * LANES), (PROJ, 5 * LANES))
+VECTORS = CHUNKS
 CHUNK_COPIES = 6
+CHUNKS_BEFORE = (0, CHUNKS + 1, CHUNKS + 2, 2 * CHUNKS + 2)
 
 
 def schedule():
@@ -626,17 +628,19 @@
         entries.setdefault(t, []).append((which, stage, chunk))
 
     for chunk in range(CHUNKS):
-        for stage, later in enumerate((1, 3, 5, 7)):
+        for stage, later in enumerate((2, 4, 6, 8)):
             enter(chunk + later, EXPAND, stage, chunk)
-        for stage, later in enumerate((1, 3, 4)):
+        for stage, later in enumerate((1, 3, 5)):
             enter(chunk + later, REDUCE, stage, chunk)
-    enter(CHUNKS + 3, REDUCE, None, 0)
-    enter(CHUNKS + 6, REDUCE, 3, 0)
-    for stage, t in enumerate((5, 7, 9, 11)):
+    enter(8, REDUCE, None, 0)
+    enter(11, REDUCE, 3, 0)
+    for stage, t in enumerate((6, 8, 10, 12)):
         enter(t, PROJ, stage, 0)
     for number, times in enumerate(((8, 9, 10, 11), (10, 11, 12, 13), (12, 13, 14, 15), (13, 14, 15, 16))):
         for stage, t in enumerate(times):
             enter(t, QKV, stage, CHUNKS - 1 - number)
+    for stage, t in enumerate((15, 16, 17)):
+        enter(t, QKV, stage + 1, VECTORS)
     return entries
 
 
@@ -774,7 +778,7 @@
         if which == REDUCE:
             return chunk, slice(None)
         if which == QKV:
-            return None, pl.ds(LANES + chunk * TRIO, TRIO) if chunk else pl.ds(0, LANES + TRIO)
+            return None, pl.ds(0, LANES) if chunk == VECTORS else pl.ds(LANES + chunk * TRIO, TRIO)
         return None, pl.ds(chunk * 4 * LANES, 4 * LANES)
 
     def scatter(self, which, stage, chunk):
@@ -782,7 +786,7 @@
         axis, rest = order[stage], order[stage + 1 :]
         buffer = self.arrived[which][stage]
         at_z, cols = self.chunk_view(which, chunk)
-        first = (which * CHUNKS + chunk) * CHUNK_COPIES + copies_before(order, stage)
+        first = (CHUNKS_BEFORE[which] + chunk) * CHUNK_COPIES + copies_before(order, stage)
         copies, terms = [], []
         for k, (device, other) in enumerate(self.along[axis]):
             at = {axis: other}
@@ -807,10 +811,9 @@
         at_z, cols = self.chunk_view(which, chunk)
         at = {Z: at_z} if at_z is not None and Z in rest else None
         here = self.place(rest, at) + (slice(None), cols)
-        sums = None
-        if which == QKV and not chunk:
-            sums = self.vector_sums(self.place(rest), terms)
-        if len(terms) == 1 and rest:
+        if which == QKV and chunk == VECTORS:
+            self.add_vectors(here, terms, rest)
+        elif len(terms) == 1 and rest:
             w[here] = w[here] + terms[0][...]
         else:
             total = w[here].astype(F32)
@@ -820,30 +823,27 @@
                 w[here] = total.astype(BF)
             else:
                 self.keep(which, chunk, total)
-        if sums is not None:
-            half = PACKED // 2
-            exact = sums[..., :half, :] + sums[..., half:, :]
-            if rest:
-                high = exact.astype(BF).astype(F32)
-                w[self.place(rest) + (slice(None), pl.ds(0, LANES))] = jnp.concatenate([high, exact - high], axis=-2).astype(BF)
-            else:
-                self.g_total[...] = exact
         if rest and not (which == REDUCE and rest == (Z,)):
             self.scatter_start(which, stage + 1, chunk)
         self.sent(copies)
 
-    def vector_sums(self, here, terms):
-        total = self.weights[QKV][here + (slice(None), pl.ds(0, LANES))].astype(F32)
+    def add_vectors(self, here, terms, rest):
+        w = self.weights[QKV]
+        total = w[here].astype(F32)
         for term in terms:
-            total = total + term[...][..., 0:LANES].astype(F32)
-        return total
+            total = total + term[...].astype(F32)
+        half = PACKED // 2
+        exact = total[..., :half, :] + total[..., half:, :]
+        if rest:
+            high = exact.astype(BF).astype(F32)
+            w[here] = jnp.concatenate([high, exact - high], axis=-2).astype(BF)
+        else:
+            self.g_total[...] = exact
 
     def keep(self, which, chunk, total):
         out = self.outs[which]
         if which == QKV:
             width = out.shape[1] // 3
-            if not chunk:
-                total = total[:, LANES:]
             for i in range(3):
                 out[:, i * width + chunk * LANES : i * width + (chunk + 1) * LANES] = total[:, i * LANES : (i + 1) * LANES]
         else:
@@ -1014,18 +1014,21 @@
             pl.when(i == at)(lambda at=at: self.tick(CHUNKS + 1 + at))
 
     def have_qkv(self, j):
+        if isinstance(j, int):
+            self.scatter_start(QKV, 0, j)
+            return
         for at in range(1, CHUNKS):
             pl.when(j == at)(lambda at=at: self.scatter_start(QKV, 0, at))
 
     def have_vectors(self):
+        self.tick(3 * CHUNKS + 1)
         self.spread_vectors()
-        self.scatter_start(QKV, 0, 0)
+        self.scatter_start(QKV, 0, VECTORS)
 
     def have_grad(self):
-        end = 3 * CHUNKS + 1
-        self.tick(end)
+        self.scatter_on(QKV, 0, VECTORS)
         self.start(self.swaps[3] + self.kept[3:4])
-        for t in range(end + 1, max(SCHEDULE) + 1):
+        for t in range(3 * CHUNKS + 2, max(SCHEDULE) + 1):
             self.tick(t)
         for i in (2, 3):
             self.kept[i].wait()
@@ -1081,7 +1084,7 @@
         + [pltpu.VMEM(one.shape, BF) for one in vectors]
         + [pltpu.VMEM((packed_rows, LANES), F32), pltpu.VMEM((8, LANES), F32), pltpu.VMEM((N_VECTORS, LANES), F32)]
         + landing
-        + [dma((17,)), dma((8, 3)), dma((2, len(UNITS), 7)), dma((2, 4 * CHUNKS * CHUNK_COPIES))],
+        + [dma((17,)), dma((8, 3)), dma((2, len(UNITS), 7)), dma((2, (CHUNKS_BEFORE[-1] + CHUNKS) * CHUNK_COPIES))],
         compiler_params=pltpu.CompilerParams(
             vmem_limit_bytes=62 * 2**20, collective_id=0, has_side_effects=True
         ),

time: 138 us -> 135 us (0.978)
  Pallas kernels: 136 us -> 133 us
    pallas_call x1, Pallas kernels: 133 us -> 130 us  [run_group(): pl.pallas_call(group_kernel, out_shape=[jax.ShapeDtypeStruct(tokens.shape...]
where the time goes in v5:
time: 135 us; the launch traced here: 134 us
  Pallas kernels  133 us (99%)
    pallas_call x1, Pallas kernels, run_group(): pl.pallas_call(group_kernel, out_shape=[jax.ShapeDtypeStruct(tokens.shape...  130 us
    pallas_call x1, Pallas kernels, finish(): pl.pallas_call(finish_kernel, out_shape=[jax.ShapeDtypeStruct(*one) for o...  3.43 us

profile of v5, /device:TPU:0, one launch (start us, length us, event | category | flops | bytes accessed | tf_op | source)
XLA Modules:
  0.0 134.2 jit_solution(1304596237424247218)
XLA Ops:
  0.7 130.0 %shard_map.254 = (bf16[4,256,512]{2,1,0:T(8,128)(2,1)}, bf16[4,256,512]{2,1,0:T(8,128)(2,1)}, f32[16,1536]{1,0:T(8,128)}, f32[16,512]{1,0:T(8,128)}, f32[16,2048...) custom-call(s32[1,2,4]{2,1,0:T(2,128)} %bitcast.1, bf16[16]{0:T(256)(128)(2,1)} %refs_1_.1, bf16[16]{0:T(256)(128)(2,1)} %refs_2_.1, ...), custom_call_target="tpu_custom_call" | custom-call | tf_op jit(solution)/shard_map/pallas_call | solution.py:1075
  130.6 3.4 %shard_map.255 = (bf16[4,256,512]{2,1,0:T(8,128)(2,1)}, bf16[4,256,512]{2,1,0:T(8,128)(2,1)}, f32[16,1536]{1,0:T(8,128)}, f32[16,512]{1,0:T(8,128)}, f32[16,2048...) custom-call(bf16[4,256,512]{2,1,0:T(8,128)(2,1)} %get-tuple-element., ...), custom_call_target="tpu_custom_call" | custom-call | tf_op jit(solution)/shard_map/pallas_call | solution.py:1129

commit v6 on v5

--- a/solution.py
+++ b/solution.py
@@ -651,10 +651,15 @@
     def __init__(self, b, ins, outs, scratch):
         self.b = b
         self.tokens, self.cotangent, self.vectors, self.shards = ins
-        self.result, self.grad_x, self.outs, self.g_total = outs
+        self.result, self.grad_x, held, targets = outs
+        self.outs, self.g_total = held[:4], held[4]
         (self.lengths, self.own_lengths, self.own_qkv, self.own_vec, self.packed, self.turn, self.tile, self.arrived,
          self.local_sem, self.token_sem, self.ag_sem, self.rs_sem) = scratch
         self.weights = tuple(b[-4:])
+        self.handed = [
+            pltpu.make_async_copy(one, target, self.local_sem.at[17 + i])
+            for i, (one, target) in enumerate(zip(held, targets))
+        ]
         dp, blk = lax.axis_index("dp"), lax.axis_index("blk")
         z, y, x, c = dp // SPREAD[Y], dp % SPREAD[Y], blk // SPREAD[C], blk % SPREAD[C]
         self.mine = (z, y, x, c)
@@ -1030,6 +1035,9 @@
         self.start(self.swaps[3] + self.kept[3:4])
         for t in range(3 * CHUNKS + 2, max(SCHEDULE) + 1):
             self.tick(t)
+        self.start(self.handed)
+        for copy in self.handed:
+            copy.wait()
         for i in (2, 3):
             self.kept[i].wait()
             self.arrive(self.swaps[i])
@@ -1052,13 +1060,14 @@
     b = Buffers(*take(len(Buffers._fields)))
     (own_lengths, own_qkv), own_vec, (packed, turn, tile) = take(2), take(N_VECTORS), take(3)
     arrived = [take(4) for _ in range(4)]
+    held = take(5)
     scratch = [lengths, own_lengths, own_qkv, own_vec, packed, turn, tile, arrived] + refs
-    group = Group(b, (tokens, cotangent, vectors, shards), (result, grad_x, outs, g_total), scratch)
+    group = Group(b, (tokens, cotangent, vectors, shards), (result, grad_x, held, outs + [g_total]), scratch)
     compute(b, group)
 
 
 def run_group(lengths, vectors, tokens, cotangent, weights):
-    vmem, anywhere = pl.BlockSpec(memory_space=pltpu.VMEM), pl.BlockSpec(memory_space=pl.ANY)
+    anywhere = pl.BlockSpec(memory_space=pl.ANY)
     blk, height, width = tokens.shape
     extra = [0] * 4
     for which, _ in VECTOR_TILES:
@@ -1078,13 +1087,15 @@
         + [jax.ShapeDtypeStruct(one.shape, F32) for one in weights]
         + [jax.ShapeDtypeStruct((N_VECTORS, LANES), F32)],
         in_specs=[anywhere] * (N_VECTORS + 7),
-        out_specs=[anywhere] * 2 + [vmem] * 5,
+        out_specs=[anywhere] * 7,
         scratch_shapes=buffers(blk * height, width, shapes)
         + [pltpu.VMEM(lengths.shape, lengths.dtype), pltpu.VMEM(weights[QKV].shape, BF)]
         + [pltpu.VMEM(one.shape, BF) for one in vectors]
         + [pltpu.VMEM((packed_rows, LANES), F32), pltpu.VMEM((8, LANES), F32), pltpu.VMEM((N_VECTORS, LANES), F32)]
         + landing
-        + [dma((17,)), dma((8, 3)), dma((2, len(UNITS), 7)), dma((2, (CHUNKS_BEFORE[-1] + CHUNKS) * CHUNK_COPIES))],
+        + [pltpu.VMEM(one.shape, F32) for one in weights]
+        + [pltpu.VMEM((N_VECTORS, LANES), F32)]
+        + [dma((22,)), dma((8, 3)), dma((2, len(UNITS), 7)), dma((2, (CHUNKS_BEFORE[-1] + CHUNKS) * CHUNK_COPIES))],
         compiler_params=pltpu.CompilerParams(
             vmem_limit_bytes=62 * 2**20, collective_id=0, has_side_effects=True
         ),

time: 135 us -> 134 us (level)
  no operation moved by 1% of the time
where the time goes in v6:
time: 134 us
  Pallas kernels  133 us (99%)
    pallas_call x1, Pallas kernels, run_group(): pl.pallas_call(group_kernel, out_shape=[jax.ShapeDtypeStruct(tokens.shape...  130 us
    pallas_call x1, Pallas kernels, finish(): pl.pallas_call(finish_kernel, out_shape=[jax.ShapeDtypeStruct(*one) for o...  3.43 us

profile of v6, /device:TPU:0, one launch (start us, length us, event | category | flops | bytes accessed | tf_op | source)
XLA Modules:
  0.0 134.3 jit_solution(5937300165053704828)
XLA Ops:
  0.7 130.0 %shard_map.254 = (bf16[4,256,512]{2,1,0:T(8,128)(2,1)}, bf16[4,256,512]{2,1,0:T(8,128)(2,1)}, f32[16,1536]{1,0:T(8,128)}, f32[16,512]{1,0:T(8,128)}, f32[16,2048...) custom-call(s32[1,2,4]{2,1,0:T(2,128)} %bitcast.1, bf16[16]{0:T(256)(128)(2,1)} %refs_1_.1, bf16[16]{0:T(256)(128)(2,1)} %refs_2_.1, ...), custom_call_target="tpu_custom_call" | custom-call | tf_op jit(solution)/shard_map/pallas_call | solution.py:1084
  130.7 3.4 %shard_map.255 = (bf16[4,256,512]{2,1,0:T(8,128)(2,1)}, bf16[4,256,512]{2,1,0:T(8,128)(2,1)}, f32[16,1536]{1,0:T(8,128)}, f32[16,512]{1,0:T(8,128)}, f32[16,2048...) custom-call(bf16[4,256,512]{2,1,0:T(8,128)(2,1)} %get-tuple-element., ...), custom_call_target="tpu_custom_call" | custom-call | tf_op jit(solution)/shard_map/pallas_call | solution.py:1140
